TPU v7x, 128 devices: a whole 4x4x4 slice. The times are simulated.
128 devices in a mesh: sec: 16 (over z, x), freq: 8 (over y, core).
Axes of the slice: x: 4, y: 4, z: 4, core: 2. Of those that a mesh axis runs over, the one named last changes fastest.
Arguments:
- coupling: float32 [128, 28800], P('sec'), may hold values from -1 to 1
- propagation: float32 [128, 120], P('sec'), may hold values from 0.5 to 3
- frequency_offset: float32 [64], P('freq'), may hold values from -3.140625 to 3.140625
- measured: float32 [64, 28800], P('freq'), may hold values from -0.54 to 0.54
Outputs:
- gradients: float32 [128, 28800], P('sec')
All inputs are finite; a program needn't handle non-finite values.
Results may differ from a plain program's by a relative error of at most 0.0003.
Values sent between devices are 32-bit elements; how exact they have to be, the bound alone decides.
No kernel may reach another device: no remote copies, remote signals or barrier semaphores. Data moves between devices by JAX's collectives and lax.ppermute only.
A program may use at most 128 MiB of HBM per device.

v0:
```python
import jax
import jax.numpy as jnp
from jax import lax
from jax.sharding import PartitionSpec as P

highest = lax.Precision.HIGHEST


def complex_product(outer_matrix, inner_matrix):
    mode_count = outer_matrix.shape[-2]
    from_real = jnp.einsum(
        "...ij,...jk->...ik", outer_matrix[..., :mode_count], inner_matrix, precision=highest
    )
    from_imag = jnp.einsum(
        "...ij,...jk->...ik", outer_matrix[..., mode_count:], inner_matrix, precision=highest
    )
    return jnp.concatenate(
        [
            from_real[..., :mode_count] - from_imag[..., mode_count:],
            from_real[..., mode_count:] + from_imag[..., :mode_count],
        ],
        axis=-1,
    )


def adjoint(matrix):
    mode_count = matrix.shape[-2]
    real_part = jnp.swapaxes(matrix[..., :mode_count], -1, -2)
    imag_part = jnp.swapaxes(matrix[..., mode_count:], -1, -2)
    return jnp.concatenate([real_part, -imag_part], axis=-1)


def rotate_rows(matrix, phases):
    mode_count = matrix.shape[-2]
    cosine_rows = jnp.cos(phases)[..., None]
    sine_rows = jnp.sin(phases)[..., None]
    real_part = matrix[..., :mode_count]
    imag_part = matrix[..., mode_count:]
    return jnp.concatenate(
        [
            cosine_rows * real_part - sine_rows * imag_part,
            cosine_rows * imag_part + sine_rows * real_part,
        ],
        axis=-1,
    )


def identity_stack(freq_count, mode_count):
    unit = jnp.broadcast_to(
        jnp.eye(mode_count, dtype=jnp.float32), (freq_count, mode_count, mode_count)
    )
    return jnp.concatenate([unit, jnp.zeros_like(unit)], axis=-1)


def frequency_term(pulled, before):
    mode_count = pulled.shape[-2]
    swapped = jnp.concatenate([pulled[..., mode_count:], -pulled[..., :mode_count]], axis=-1)
    real_part = jnp.einsum("fij,flj->il", pulled, before, precision=highest)
    imag_part = jnp.einsum("fij,flj->il", swapped, before, precision=highest)
    return 2.0 * jnp.concatenate([real_part, imag_part], axis=-1)


def shards(coupling, propagation, frequency_offset, measured):
    mode_count = propagation.shape[1]
    freq_count = frequency_offset.shape[0]
    coupling = coupling.reshape(-1, mode_count, 2 * mode_count)
    measured = measured.reshape(-1, mode_count, 2 * mode_count)
    identity = identity_stack(freq_count, mode_count)
    phase_table = propagation[:, None, :] * frequency_offset[None, :, None]
    sections = rotate_rows(coupling[:, None], phase_table)

    def advance(prefix, section):
        product = complex_product(section, prefix)
        return (product, product)

    aggregate, later_rows = lax.scan(advance, sections[0], sections[1:])
    partial_rows = jnp.concatenate([sections[0][None], later_rows], axis=0)
    flat_aggregate = aggregate.reshape(freq_count, -1)
    flat_matrix = lax.all_gather(flat_aggregate[None], "sec", axis=0, tiled=True)
    aggregates = flat_matrix.reshape(flat_matrix.shape[:-1] + (mode_count, 2 * mode_count))
    position = lax.axis_index("sec")

    def combine_all(carry, items):
        slot_index, piece = items
        lower_state, upper_state = carry
        below = slot_index < position
        chosen = jnp.where(below, lower_state, upper_state)
        moved = complex_product(piece, chosen)
        lower_state = jnp.where(below, moved, lower_state)
        upper_state = jnp.where(slot_index > position, moved, upper_state)
        return ((lower_state, upper_state), None)

    slots = jnp.arange(aggregates.shape[0], dtype=jnp.int32)
    (earlier, later), _ = lax.scan(combine_all, (identity, identity), (slots, aggregates))
    prefixes = complex_product(partial_rows, earlier[None])
    befores = jnp.concatenate([earlier[None], prefixes[:-1]], axis=0)
    total_map = complex_product(later, prefixes[-1])
    misfit = total_map - measured
    start_state = complex_product(adjoint(later), misfit)

    def retreat(back_state, items):
        section_coupling, phases, before = items
        pulled = rotate_rows(back_state, -phases)
        gradient = frequency_term(pulled, before)
        return (complex_product(adjoint(section_coupling)[None], pulled), gradient)

    _, gradients = lax.scan(retreat, start_state, (coupling, phase_table, befores), reverse=True)
    flat_gradients = gradients.reshape(gradients.shape[0], -1)
    return lax.psum(flat_gradients, "freq")


def solution(mesh):
    in_specs = (P("sec", None), P("sec", None), P("freq"), P("freq", None))
    out_specs = P("sec", None)
    return jax.shard_map(shards, mesh=mesh, in_specs=in_specs, out_specs=out_specs, check_vma=False)
```

profile of v0, /device:TPU:1, one launch (start us, length us, event | category | flops | bytes accessed | tf_op | source)
XLA Modules:
  0.0 464.4 jit_solution(541581909381429958)
XLA Ops:
  7.5 2.0 broadcast_in_dim_reshape.6
  9.7 2.2 multiply_subtract_fusion.1
  12.2 4.7 %pad_maximum_fusion.8 = f32[7,8,120,240]{3,2,0,1:T(8,128)} fusion(f32[8,8,120,120]{3,2,0,1:T(8,128)S(1)} %get-tuple-element.276, f32[8,8,120,120]{3,2,0,1:T(8,128)S(1)} %get-tuple-element.275), kind=kLoop, calls=%fused_computation.59 | loop fusion | flops 1612800 | bytes 13824000 | tf_op jit(solution)/shard_map/concatenate | solution.py:39
  16.9 34.5 %while.40 = (s32[]{:T(128)}, f32[8,120,240]{2,1,0:T(8,128)S(1)}, f32[7,8,120,240]{3,2,0,1:T(8,128)}, f32[7,8,120,240]{3,2,0,1:T(8,128)}, s32[]{:T(128)}) while((s32[]{:T(128)}, f32[8,120,240]{2,1,0:T(8,128)S(1)}, f32[7,8,120,240]{3,2,0,1:T(8,128)}, f32[7,8,120,240]{3,2,0,1:T(8,128)}, s32[]{:T(128)}) %tuple.101), condition=%wide.region_1.2_spmd, body=%wide.region_0.1_spmd.sunk | while | flops 664012800 | bytes 12227137 | solution.py:76
  17.0 1.4 dynamic-slice_bitcast_fusion.4
  20.7 1.3 bitcast_dynamic-update-slice_fusion.2
  22.0 1.3 dynamic-slice_bitcast_fusion.4
  25.6 1.3 bitcast_dynamic-update-slice_fusion.2
  30.5 1.3 bitcast_dynamic-update-slice_fusion.2
  31.8 1.3 dynamic-slice_bitcast_fusion.4
  35.4 1.3 bitcast_dynamic-update-slice_fusion.2
  40.3 1.3 bitcast_dynamic-update-slice_fusion.2
  45.3 1.3 bitcast_dynamic-update-slice_fusion.2
  50.2 1.3 bitcast_dynamic-update-slice_fusion.2
  51.5 1.3 broadcast_in_dim_reshape.7
  53.1 1.8 reshape.82
  55.1 1.8 reshape.81
  56.9 100.4 %all-gather.2.cloned.1.call-done = f32[16,8,28800]{2,1,0:T(8,128)} async-done(((f32[1,8,28800]{2,1,0:T(8,128)}), f32[16,8,28800]{2,1,0:T(8,128)}) %all-gather.2.cloned.1.call-update) | async-done | bytes 14745616 | tf_op jit(solution)/shard_map/all_gather | solution.py:79
  157.3 17.9 %reshape.80 = f32[16,8,120,240]{3,2,1,0:T(8,128)} reshape(f32[16,8,28800]{2,1,0:T(8,128)} %all-gather.2.cloned.1.call-done) | data formatting | bytes 29491200 | tf_op jit(solution)/shard_map/reshape | solution.py:80
  175.2 99.3 %while.41 = (s32[]{:T(128)}, f32[8,120,240]{2,1,0:T(8,128)S(1)}, f32[8,120,240]{2,1,0:T(8,128)S(1)}, s32[16]{0:T(128)S(1)}, s32[]{:T(128)}, /*index=5*/f32[16,8,120,240]{3,2,1,0:T(8,128)}, s32[]{:T(128)}) while((s32[]{:T(128)}, f32[8,120,240]{2,1,0:T(8,128)S(1)}, f32[8,120,240]{2,1,0:T(8,128)S(1)}, s32[16]{0:T(128)S(1)}, s32[]{:T(128)}, ...), condition=%wide.region_3.4_spmd, body=%wide.region_2.3_spmd.sunk | while | flops 664934400 | bytes 15974515 | solution.py:94
  176.4 1.3 dynamic-slice_bitcast_fusion.5
  182.6 1.3 dynamic-slice_bitcast_fusion.5
  188.8 1.3 dynamic-slice_bitcast_fusion.5
  195.0 1.3 dynamic-slice_bitcast_fusion.5
  201.2 1.3 dynamic-slice_bitcast_fusion.5
  207.4 1.3 dynamic-slice_bitcast_fusion.5
  213.6 1.3 dynamic-slice_bitcast_fusion.5
  219.8 1.3 dynamic-slice_bitcast_fusion.5
  226.1 1.3 dynamic-slice_bitcast_fusion.5
  232.3 1.3 dynamic-slice_bitcast_fusion.5
  238.5 1.3 dynamic-slice_bitcast_fusion.5
  244.7 1.3 dynamic-slice_bitcast_fusion.5
  250.9 1.3 dynamic-slice_bitcast_fusion.5
  257.1 1.3 dynamic-slice_bitcast_fusion.5
  263.3 1.3 dynamic-slice_bitcast_fusion.5
  269.5 1.3 dynamic-slice_bitcast_fusion.5
  274.5 10.5 %fusion.31 = f32[8,8,120,240]{2,3,0,1:T(8,128)} fusion(f32[1,8,120,240]{3,2,0,1:T(8,128)} %copy-done.1, f32[7,8,120,240]{3,2,0,1:T(8,128)} %get-tuple-element.186, f32[8,120,240]{2,1,0:T(8,128)S(1)} %get-tuple-element.185), kind=kOutput, calls=%fused_computation.70 | convolution fusion | flops 2655129600 | bytes 15667200 | tf_op jit(solution)/shard_map/...ij,...jk->...ik/dot_general | solution.py:11
  285.0 12.0 %fusion.30 = f32[8,8,120,240]{2,3,0,1:T(8,128)} fusion(f32[7,8,120,240]{3,2,0,1:T(8,128)} %get-tuple-element.186, f32[1,8,120,240]{3,2,0,1:T(8,128)S(1)} %copy-done.2, f32[8,120,240]{2,1,0:T(8,128)S(1)} %get-tuple-element.185), kind=kOutput, calls=%fused_computation.69 | convolution fusion | flops 2655129600 | bytes 15667200 | tf_op jit(solution)/shard_map/...ij,...jk->...ik/dot_general | solution.py:14
  297.3 8.4 %slice_subtract_fusion.3 = (f32[8,8,120,120]{2,3,0,1:T(8,128)S(1)}, f32[8,8,120,120]{2,3,0,1:T(8,128)}) fusion(f32[8,8,120,240]{2,3,0,1:T(8,128)} %fusion.30, f32[8,8,120,240]{2,3,0,1:T(8,128)} %fusion.31), kind=kLoop, calls=%fused_computation.63 | loop fusion | flops 1843200 | bytes 22118400 | tf_op jit(solution)/shard_map/sub | solution.py:19
  307.0 2.0 fusion.43
  309.0 2.0 fusion.39
  311.4 1.3 fusion.41
  312.8 1.5 fusion.36
  314.2 3.4 fusion.24
  318.8 75.9 %while.42 = (s32[]{:T(128)}, f32[8,120,240]{1,2,0:T(8,128)S(1)}, f32[8,120,240]{2,1,0:T(8,128)S(1)}, f32[8,8,120]{2,1,0:T(8,128)S(1)}, f32[8,120,240]{2,1,0:T(8,...) while((s32[]{:T(128)}, f32[8,120,240]{1,2,0:T(8,128)S(1)}, f32[8,120,240]{2,1,0:T(8,128)S(1)}, ...), condition=%wide.region_5.6_spmd, body=%wide.region_4.5_spmd.sunk | while | flops 1329394560 | bytes 16423793 | solution.py:107
  318.9 2.9 convolution_bitcast_fusion.9
  321.9 2.9 convolution_bitcast_fusion.8
  328.4 2.9 convolution_bitcast_fusion.9
  331.4 2.9 convolution_bitcast_fusion.8
  337.9 2.9 convolution_bitcast_fusion.9
  340.8 2.9 convolution_bitcast_fusion.8
  347.4 2.9 convolution_bitcast_fusion.9
  350.3 2.9 convolution_bitcast_fusion.8
  356.9 2.9 convolution_bitcast_fusion.9
  359.8 2.9 convolution_bitcast_fusion.8
  366.4 2.9 convolution_bitcast_fusion.9
  369.3 2.9 convolution_bitcast_fusion.8
  375.8 2.9 convolution_bitcast_fusion.9
  378.8 2.9 convolution_bitcast_fusion.8
  385.3 2.9 convolution_bitcast_fusion.9
  388.3 2.9 convolution_bitcast_fusion.8
  394.6 1.3 reshape.83
  396.0 59.4 %all-reduce.3.cloned.1.call-done = f32[8,28800]{1,0:T(8,128)} async-done(((f32[8,28800]{1,0:T(8,128)}), f32[8,28800]{1,0:T(8,128)}) %all-reduce.3.cloned.1.call-update) | async-done | bytes 921616 | tf_op jit(solution)/shard_map/psum | solution.py:109
  455.4 2.2 copy.111
  (236 shorter events, 111.6 us)
Async XLA Ops:
  6.5 150.7 %all-gather.2.cloned.1.call-start = ((), (), s32[]{:S(2)}) async-start(), calls=%async_computation | async-start | bytes 15667200 | tf_op jit(solution)/shard_map/all_gather | solution.py:79
  12.2 4.7 %copy-start.1 = (f32[1,8,120,240]{3,2,0,1:T(8,128)}, f32[1,8,120,240]{3,2,0,1:T(8,128)S(1)}, u32[]{:S(2)}) copy-start(f32[1,8,120,240]{3,2,0,1:T(8,128)S(1)} %pad_maximum_fusion.13) | copy-start | bytes 2764804
  16.9 36.2 %copy-start.4 = (f32[8,28800]{1,0:T(8,128)S(1)}, f32[8,28800]{1,0:T(8,128)}, u32[]{:S(2)}) copy-start(f32[8,28800]{1,0:T(8,128)} %param.10) | copy-start | bytes 2764804
  51.5 3.6 copy-start.5
  52.9 402.5 %all-reduce.3.cloned.1.call-start = ((), (), s32[]{:S(2)}) async-start(), calls=%async_computation.1 | async-start | bytes 1843200 | tf_op jit(solution)/shard_map/psum | solution.py:109
  274.4 10.5 %copy-start.2 = (f32[1,8,120,240]{3,2,0,1:T(8,128)S(1)}, f32[1,8,120,240]{3,2,0,1:T(8,128)}, u32[]{:S(2)}) copy-start(f32[1,8,120,240]{3,2,0,1:T(8,128)} %copy-done.1) | copy-start | bytes 2764804
  305.8 5.7 %copy-start.3 = (f32[8,120,240]{2,1,0:T(8,128)S(1)}, f32[8,120,240]{2,1,0:T(8,128)}, u32[]{:S(2)}) copy-start(f32[8,120,240]{2,1,0:T(8,128)} %reshape.81) | copy-start | bytes 2764804
  306.9 7.3 %copy-start = (f32[8,8,120,120]{2,3,0,1:T(8,128)S(1)}, f32[8,8,120,120]{2,3,0,1:T(8,128)}, u32[]{:S(2)}) copy-start(f32[8,8,120,120]{2,3,0,1:T(8,128)} %get-tuple-element.270) | copy-start | bytes 11059204
Sparse Core Ops, SparseCore 0:
  53.0 104.2 all-gather.1
  396.1 59.2 all-reduce.2
where the time goes:
time: 469 us; the launch traced here: 464 us
  waiting for transfers between devices  160 us (34%)
  matrix products  139 us (30%)
  local copies, waits for them, and re-layouts  77 us (16%)
  other arithmetic  51.7 us (11%)
  loops' own time  22.6 us (5%)
  between operations  13.6 us (3%)
    all_gather x1, waiting for transfers between devices, shards(): lax.all_gather(flat_aggregate[None], 'sec', axis=0, tiled=True)  100 us
    psum x1, waiting for transfers between devices, shards(): return lax.psum(flat_gradients, 'freq')  59.4 us
    dot_general x34, matrix products, complex_product(): jnp.einsum('...ij,...jk->...ik', outer_matrix[..., mode_count:], inner_ma...  47.8 us
    dot_general x34, matrix products, complex_product(): jnp.einsum('...ij,...jk->...ik', outer_matrix[..., :mode_count], inner_ma...  44.6 us
    dot_general x8, matrix products, frequency_term(): imag_part = jnp.einsum('fij,flj->il', swapped, before, precision=highest)  23.5 us
    dot_general x8, matrix products, frequency_term(): real_part = jnp.einsum('fij,flj->il', pulled, before, precision=highest)  23.5 us
    another operation x1, loops' own time, shards(): lax.scan(combine_all, (identity, identity), (slots, aggregates))  21.6 us
    squeeze x16, local copies, waits for them, and re-layouts, shards(): lax.scan(combine_all, (identity, identity), (slots, aggregates))  20.4 us
  transfers between devices with their start and end apart: 2, of which 2 were waited for; matrix products, arithmetic and copies ran while one was open for 1% of the time, Pallas kernels for 0%

commit v1 on v0

v1 whole, which is shorter than its diff:
```python
import functools

import jax
import jax.numpy as jnp
from jax import lax
from jax.experimental import pallas as pl
from jax.experimental.pallas import tpu as pltpu
from jax.sharding import Mesh, PartitionSpec as P

M = 120
W = 2 * M
L = 128
ND = 8
F32, BF16 = jnp.float32, jnp.bfloat16
PARAMS = pltpu.CompilerParams(vmem_limit_bytes=56 * 1024 * 1024)
VMEM = pl.BlockSpec(memory_space=pltpu.VMEM)
SMEM = pl.BlockSpec(memory_space=pltpu.SMEM)


def shape(*dims):
    return jax.ShapeDtypeStruct(dims, F32)


def split(x):
    high = x.astype(BF16)
    return high, (x - high.astype(F32)).astype(BF16)


def right_form(x):
    real, imag = x[:, :L], x[:, L:]
    return jnp.concatenate([x, jnp.concatenate([-imag, real], axis=1)], axis=0)


def dot(a, b):
    return jnp.dot(a, b, preferred_element_type=F32)


def product(left, right):
    left_high, left_low = split(left)
    right_high, right_low = split(right_form(right))
    return dot(left_high, right_high) + (dot(left_low, right_high) + dot(left_high, right_low))


def scaled(x, cosine, sine):
    real, imag = x[:, :L], x[:, L:]
    return jnp.concatenate([cosine * real - sine * imag, cosine * imag + sine * real], axis=1)


def adjoint(x):
    return jnp.concatenate([x[:, :L].T, -x[:, L:].T], axis=1)


def padded(x):
    return jnp.concatenate([x, jnp.zeros((L - M, 2 * L), F32)], axis=0)


def unpack_rows(flat_ref, out_ref):
    out_ref[...] = jnp.zeros(out_ref.shape, F32)
    zeros = jnp.zeros((ND, L - M), F32)
    for m in range(M):
        rows = pl.ds(m, ND, stride=L)
        real = flat_ref[:, m * W : m * W + M]
        imag = flat_ref[:, m * W + M : (m + 1) * W]
        out_ref[0, rows, :] = jnp.concatenate([real, zeros], axis=1)
        out_ref[1, rows, :] = jnp.concatenate([imag, zeros], axis=1)


def unpacked(rows_ref, start):
    return jnp.concatenate([rows_ref[0, pl.ds(start, L), :], rows_ref[1, pl.ds(start, L), :]], axis=1)


def up_kernel(freq_ref, prop_ref, flat_ref, a_ref, c_ref, tab_ref, tabt_ref, p_ref, q_ref, lhs_ref):
    tab_ref[...] = jnp.zeros(tab_ref.shape, F32)
    for f in range(ND):
        phase = prop_ref[...] * freq_ref[f]
        tab_ref[0, f * ND : (f + 1) * ND, 0:M] = jnp.cos(phase)
        tab_ref[1, f * ND : (f + 1) * ND, 0:M] = jnp.sin(phase)
    tabt_ref[0] = tab_ref[0].T
    tabt_ref[1] = tab_ref[1].T
    unpack_rows(flat_ref, c_ref)

    def columns(x, k, f):
        i = f * ND + k
        return scaled(x, tab_ref[0, i : i + 1, :], tab_ref[1, i : i + 1, :])

    def rows(x, k, f):
        i = f * ND + k
        return scaled(x, tabt_ref[0, :, i : i + 1], tabt_ref[1, :, i : i + 1])

    for j in range(4):
        low, up = 2 * j, 2 * j + 1
        c_up = unpacked(c_ref, up * L)
        for f in range(ND):
            lhs_ref[f * L : (f + 1) * L, :] = columns(c_up, low, f)
        res = product(lhs_ref[...], unpacked(c_ref, low * L))
        for f in range(ND):
            one = res[f * L : (f + 1) * L]
            p_ref[j, f] = rows(one, up, f) if j % 2 == 0 else one
    for f in range(ND):
        q0 = rows(product(p_ref[1, f], p_ref[0, f]), 3, f)
        q1 = product(p_ref[3, f], p_ref[2, f])
        q_ref[0, f] = q0
        q_ref[1, f] = q1
        a_ref[f] = rows(product(q1, q0), 7, f)[:M]


def up(freq, prop, flat):
    return pl.pallas_call(
        up_kernel,
        out_shape=(
            shape(ND, M, 2 * L),
            shape(2, ND * L, L),
            shape(2, ND * ND, L),
            shape(2, L, ND * ND),
            shape(4, ND, L, 2 * L),
            shape(2, ND, L, 2 * L),
        ),
        in_specs=[SMEM, VMEM, VMEM],
        out_specs=(VMEM,) * 6,
        scratch_shapes=[pltpu.VMEM((ND * L, 2 * L), F32)],
        compiler_params=PARAMS,
        name="up",
    )(freq, prop, flat)


def half_kernel(r_ref, flat_ref, h_ref, m_ref, p_ref, q_ref, rows_ref):
    for j in range(4):
        p_ref[j] = product(padded(r_ref[2 * j + 1]), padded(r_ref[2 * j]))
    for j in range(2):
        q_ref[j] = product(p_ref[2 * j + 1], p_ref[2 * j])
    h_ref[...] = product(q_ref[1], q_ref[0])[:M]
    unpack_rows(flat_ref, rows_ref)
    own = (lax.axis_index("zl") * 4 + lax.axis_index("x") + 4 * lax.axis_index("zh")) % ND
    m_ref[...] = unpacked(rows_ref, pl.multiple_of(own * L, L))


def half(r, flat):
    return pl.pallas_call(
        half_kernel,
        out_shape=(shape(M, 2 * L), shape(L, 2 * L), shape(4, L, 2 * L), shape(2, L, 2 * L)),
        in_specs=[VMEM, VMEM],
        out_specs=(VMEM,) * 4,
        scratch_shapes=[pltpu.VMEM((2, ND * L, L), F32)],
        compiler_params=PARAMS,
        name="half",
    )(r, flat)


def top_kernel(r_ref, m_ref, p_ref, q_ref, h_ref, other_ref, v_ref):
    upper = lax.axis_index("zh") == 1
    own, other = padded(h_ref[...]), padded(other_ref[...])
    h0 = jnp.where(upper, other, own)
    h1 = jnp.where(upper, own, other)
    misfit = adjoint(product(h1, h0) - m_ref[...])
    v = product(jnp.where(upper, h0, misfit), jnp.where(upper, misfit, h1))
    v0, v1 = product(v, q_ref[1]), product(q_ref[0], v)
    pairs = (product(v0, p_ref[1]), product(p_ref[0], v0), product(v1, p_ref[3]), product(p_ref[2], v1))
    for j in range(4):
        v_ref[2 * j] = product(pairs[j], padded(r_ref[2 * j + 1]))[:M]
        v_ref[2 * j + 1] = product(padded(r_ref[2 * j]), pairs[j])[:M]


def top(r, m, p, q, h, other):
    return pl.pallas_call(
        top_kernel,
        out_shape=shape(ND, M, 2 * L),
        in_specs=[VMEM] * 6,
        out_specs=VMEM,
        compiler_params=PARAMS,
        name="top",
    )(r, m, p, q, h, other)


def down_kernel(v_ref, c_ref, tab_ref, tabt_ref, p_ref, q_ref, g_ref, vp_ref):
    def columns(x, k, f):
        i = f * ND + k
        return scaled(x, tab_ref[0, i : i + 1, :], tab_ref[1, i : i + 1, :])

    def rows(x, k, f):
        i = f * ND + k
        return scaled(x, tabt_ref[0, :, i : i + 1], tabt_ref[1, :, i : i + 1])

    for f in range(ND):
        v = columns(padded(v_ref[f]), 7, f)
        v0 = columns(product(v, q_ref[1, f]), 3, f)
        v1 = product(q_ref[0, f], v)
        at = pl.ds(f * L, L)
        vp_ref[0, at] = columns(product(v0, p_ref[1, f]), 1, f)
        vp_ref[1, at] = product(p_ref[0, f], v0)
        vp_ref[2, at] = columns(product(v1, p_ref[3, f]), 5, f)
        vp_ref[3, at] = product(p_ref[2, f], v1)

    core, y = lax.axis_index("c"), lax.axis_index("y")

    def place(k):
        return jnp.where(core == k // 4, 0, 4) + (k % 4 - y + 4) % 4

    for j in range(4):
        low, up = 2 * j, 2 * j + 1
        c_low = unpacked(c_ref, low * L)
        res = product(vp_ref[j], unpacked(c_ref, up * L))
        g_low = columns(res[0:L], low, 0)
        g_up = rows(product(c_low, vp_ref[j, 0:L]), low, 0)
        for f in range(1, ND):
            g_low += columns(res[f * L : (f + 1) * L], low, f)
            g_up += rows(product(c_low, vp_ref[j, f * L : (f + 1) * L]), low, f)
        g_ref[place(low)] = g_low[:M]
        g_ref[place(up)] = g_up[:M]


def down(v, c, tab, tabt, p, q):
    return pl.pallas_call(
        down_kernel,
        out_shape=shape(ND, M, 2 * L),
        in_specs=[VMEM] * 6,
        out_specs=VMEM,
        scratch_shapes=[pltpu.VMEM((4, ND * L, 2 * L), F32)],
        compiler_params=PARAMS,
        name="down",
    )(v, c, tab, tabt, p, q)


def sum_kernel(own_ref, a_ref, b_ref, c_ref, out_ref):
    total = (own_ref[...] + a_ref[...]) + (b_ref[...] + c_ref[...])
    out_ref[...] = 2.0 * adjoint(padded(total))[:M]


def sum_up(own, a, b, c):
    return pl.pallas_call(
        sum_kernel,
        out_shape=shape(M, 2 * L),
        in_specs=[VMEM] * 4,
        out_specs=VMEM,
        compiler_params=PARAMS,
        name="sum_up",
    )(own, a, b, c)


def store_kernel(*refs):
    parts, out_ref, rows_ref = refs[:ND], refs[ND], refs[ND + 1]
    core, y = lax.axis_index("c"), lax.axis_index("y")
    for i in range(ND):
        place = (4 * core if i < 4 else 4 * (1 - core)) + (y - i % 4 + 4) % 4
        at = pl.ds(pl.multiple_of(place * L, L), M)
        rows_ref[0, at, :] = parts[i][:, :L]
        rows_ref[1, at, :] = parts[i][:, L:]
    for m in range(M):
        rows = pl.ds(m, ND, stride=L)
        out_ref[:, m * W : m * W + M] = rows_ref[0, rows, :][:, :M]
        out_ref[:, m * W + M : (m + 1) * W] = rows_ref[1, rows, :][:, :M]


def store(parts):
    return pl.pallas_call(
        store_kernel,
        out_shape=shape(ND, M * W),
        in_specs=[VMEM] * ND,
        out_specs=VMEM,
        scratch_shapes=[pltpu.VMEM((2, ND * L, L), F32)],
        compiler_params=PARAMS,
        name="store",
    )(*parts)


def shards(coupling, propagation, frequency_offset, measured):
    upper = lax.axis_index("zh") == 1
    freq = jnp.where(upper, jnp.roll(frequency_offset, 4), frequency_offset)
    a, c, tab, tabt, p, q = up(freq, propagation, coupling)
    r = lax.all_to_all(a, ("zl", "x"), 0, 0, tiled=True)
    h, m, hp, hq = half(r, measured)
    other = lax.ppermute(h, ("zh", "zl"), [(0, 3), (1, 2), (2, 1), (3, 0)])
    v = top(r, m, hp, hq, h, other)
    v = lax.all_to_all(v, ("zl", "x"), 0, 0, tiled=True)
    g = down(v, c, tab, tabt, p, q)
    swap = [(0, 1), (1, 0)]
    g = g[:4] + lax.ppermute(g[4:], "c", swap)
    turned = lambda i, x: lax.ppermute(x, "y", [(s, (s + i) % 4) for s in range(4)])
    total = sum_up(g[0], *[turned(i, g[i]) for i in range(1, 4)])
    parts = [total] + [turned(i, total) for i in range(1, 4)]
    parts += [lax.ppermute(x, "c", swap) for x in parts]
    return store(parts)


def solution(mesh):
    fine = Mesh(mesh.devices.reshape(2, 2, 4, 4, 2), ("zh", "zl", "x", "y", "c"))
    sec, freq = ("zh", "zl", "x"), ("y", "c")
    return jax.shard_map(
        shards,
        mesh=fine,
        in_specs=(P(sec, None), P(sec, None), P(freq), P(freq, None)),
        out_specs=P(sec, None),
        check_vma=False,
    )
```

time: 469 us -> 110 us (0.23)
  waiting for transfers between devices: 160 us -> 17.2 us
  matrix products: 139 us -> 0 us
  local copies, waits for them, and re-layouts: 77 us -> 4.53 us
  other arithmetic: 51.7 us -> 2.34 us
  blocking collectives: 0 us -> 37 us
  Pallas kernels: 0 us -> 31.5 us
  loops' own time: 22.6 us -> 0 us
  starting transfers between devices: 0.22 us -> 16.4 us
  between operations: 13.6 us -> 0.09 us
    dot_general x84 -> x0, matrix products: 139 us -> none  [the longest x34 47.8 us: complex_product(): jnp.einsum('...ij,...jk->...ik', outer_matrix[..., mode_count:], inner_ma...]
    all_gather x1 -> x0, waiting for transfers between devices: 100 us -> none  [shards(): lax.all_gather(flat_aggregate[None], 'sec', axis=0, tiled=True)]
    psum x1 -> x0, waiting for transfers between devices: 59.4 us -> none  [shards(): return lax.psum(flat_gradients, 'freq')]
    all_to_all x0 -> x2, blocking collectives: none -> 37 us  [the longest x1 20.6 us: shards(): r = lax.all_to_all(a, ('zl', 'x'), 0, 0, tiled=True)]
    pallas_call x0 -> x6, Pallas kernels: none -> 31.5 us  [the longest x1 11.4 us: down(): pl.pallas_call(down_kernel, out_shape=shape(ND, M, 2 * L), in_specs=[VMEM...]
    squeeze x23 -> x1, local copies, waits for them, and re-layouts: 29.3 us -> 0.68 us  [shards(): total = sum_up(g[0], *[turned(i, g[i]) for i in range(1, 4)])]
    reshape x4 -> x0, local copies, waits for them, and re-layouts: 22.8 us -> none  [the longest x1 17.9 us: shards(): flat_matrix.reshape(flat_matrix.shape[:-1] + (mode_count, 2 * mode_count))]
    another operation x3 -> x0, loops' own time: 22.6 us -> none  [the longest x1 21.6 us: shards(): lax.scan(combine_all, (identity, identity), (slots, aggregates))]
  transfers between devices with their start and end apart: 2 -> 12, of which waited for: 2 -> 8; matrix products, arithmetic and copies ran while one was open for 1% -> 0% of each run, Pallas kernels for 0% -> 0%
where the time goes in v1:
time: 110 us; the launch traced here: 109 us
  blocking collectives  37 us (34%)
  Pallas kernels  31.5 us (29%)
  waiting for transfers between devices  17.2 us (16%)
  starting transfers between devices  16.4 us (15%)
  local copies, waits for them, and re-layouts  4.53 us (4%)
  other arithmetic  2.34 us (2%)
    all_to_all x1, blocking collectives, shards(): r = lax.all_to_all(a, ('zl', 'x'), 0, 0, tiled=True)  20.6 us
    all_to_all x1, blocking collectives, shards(): v = lax.all_to_all(v, ('zl', 'x'), 0, 0, tiled=True)  16.4 us
    pallas_call x1, Pallas kernels, down(): pl.pallas_call(down_kernel, out_shape=shape(ND, M, 2 * L), in_specs=[VMEM...  11.4 us
    ppermute x6, waiting for transfers between devices, shards(): lax.ppermute(x, 'y', [(s, (s + i) % 4) for s in range(4)])  11.3 us
    pallas_call x1, Pallas kernels, up(): pl.pallas_call(up_kernel, out_shape=(shape(ND, M, 2 * L), shape(2, ND * L...  7.86 us
    ppermute x4, starting transfers between devices, shards(): parts += [lax.ppermute(x, 'c', swap) for x in parts]  5.62 us
    ppermute x6, starting transfers between devices, shards(): lax.ppermute(x, 'y', [(s, (s + i) % 4) for s in range(4)])  5.25 us
    pallas_call x1, Pallas kernels, top(): pl.pallas_call(top_kernel, out_shape=shape(ND, M, 2 * L), in_specs=[VMEM]...  4.02 us
  transfers between devices with their start and end apart: 12, of which 8 were waited for; matrix products, arithmetic and copies ran while one was open for 0% of the time, Pallas kernels for 0%

profile of v1, /device:TPU:1, one launch (start us, length us, event | category | flops | bytes accessed | tf_op | source)
XLA Modules:
  0.0 109.1 jit_solution(9031046918847237563)
XLA Ops:
  0.0 0.8 fusion
  0.8 1.2 %broadcast_select_fusion.freq_ref = f32[8]{0:T(128)} fusion(f32[8]{0:T(128)} %param.6, pred[]{:T(512)S(6)} %eq.3, f32[4]{0:T(128)S(1)} %get-tuple-element.30, f32[4]{0:T(128)S(1)} %get-tuple-element.29), kind=kLoop, calls=%fused_computation.5 | loop fusion | flops 16 | bytes 97 | tf_op jit(solution)/shard_map/jit(_where)/select_n | solution.py:267
  2.0 7.9 %up.1 = (f32[8,120,256]{2,1,0:T(8,128)}, f32[2,1024,128]{2,1,0:T(8,128)}, f32[2,64,128]{2,1,0:T(8,128)}, f32[2,128,64]{2,1,0:T(8,128)}, f32[4,8,128,256]{3,2,1,0:T(8,128)}, /*index=5*/f32[2,8,128,256]{3,2,1,0:T(8,128)}) custom-call(f32[8]{0:T(128)} %broadcast_select_fusion.freq_ref, f32[8,120]{1,0:T(8,128)} %prop_ref.1, f32[8,28800]{1,0:T(8,128)} %flat_ref.2), custom_call_target="tpu_custom_call" | custom-call | tf_op jit(solution)/shard_map/up/pallas_call | solution.py:108
  9.9 20.6 %all_to_all.10.r_ref = f32[8,120,256]{2,1,0:T(8,128)} all-to-all(f32[8,120,256]{2,1,0:T(8,128)} %get-tuple-element.15), channel_id=1, replica_groups=mesh['zh'=2,'zl'=2,'x'=4,'y'=4,'c'=2] {'zl','x'}, dimensions={0} | all-to-all | bytes 1966080 | tf_op jit(solution)/shard_map/all_to_all | solution.py:269
  30.5 3.5 %half.1 = (f32[120,256]{1,0:T(8,128)}, f32[128,256]{1,0:T(8,128)}, f32[4,128,256]{2,1,0:T(8,128)}, f32[2,128,256]{2,1,0:T(8,128)}) custom-call(f32[8,120,256]{2,1,0:T(8,128)} %all_to_all.10.r_ref, f32[8,28800]{1,0:T(8,128)} %flat_ref.3), custom_call_target="tpu_custom_call" | custom-call | tf_op jit(solution)/shard_map/half/pallas_call | solution.py:138
  34.0 1.8 %collective-permute-start = (f32[120,256]{1,0:T(8,128)}, f32[120,256]{1,0:T(8,128)S(1)}, u32[]{:S(2)}, u32[]{:S(2)}) collective-permute-start(f32[120,256]{1,0:T(8,128)} %get-tuple-element.19.h_ref), channel_id=1, source_target_pairs={{0,96},{32,64},{64,32},{96,0},{1,97},{33,65},{65,33},{97,1},{2,98}... | collective-permute-start | bytes 368648 | tf_op jit(solution)/shard_map/ppermute | solution.py:271
  35.7 3.4 %collective-permute-done.other_ref = f32[120,256]{1,0:T(8,128)S(1)} collective-permute-done((f32[120,256]{1,0:T(8,128)}, f32[120,256]{1,0:T(8,128)S(1)}, u32[]{:S(2)}, u32[]{:S(2)}) %collective-permute-start) | collective-permute-done | bytes 122912 | tf_op jit(solution)/shard_map/ppermute | solution.py:271
  39.1 0.0 copy-start.3
  39.1 0.7 copy-done.3
  39.8 4.0 %top.1 = f32[8,120,256]{2,1,0:T(8,128)} custom-call(f32[8,120,256]{2,1,0:T(8,128)} %all_to_all.10.r_ref, f32[128,256]{1,0:T(8,128)} %get-tuple-element.16.m_ref, f32[4,128,256]{2,1,0:T(8,128)} %get-tuple-element.17.p_ref, f32[2,128,256]{2,1,0:T(8,128)} %get-tuple-element.18.q_ref, f32[120,256]{1,0:T(8,128)} %get-tuple-element.19.h_ref, f32[120,256]{1,0:T(8,128)} %copy-done.3), custom_call_target="tpu_custom_call" | custom-call | tf_op jit(solution)/shard_map/top/pallas_call | solution.py:164
  43.8 16.4 %all_to_all.11.v_ref = f32[8,120,256]{2,1,0:T(8,128)} all-to-all(f32[8,120,256]{2,1,0:T(8,128)} %top.1), channel_id=1, replica_groups=mesh['zh'=2,'zl'=2,'x'=4,'y'=4,'c'=2] {'zl','x'}, dimensions={0} | all-to-all | bytes 1966080 | tf_op jit(solution)/shard_map/all_to_all | solution.py:273
  60.3 11.4 %down.1 = f32[8,120,256]{2,1,0:T(8,128)} custom-call(f32[8,120,256]{2,1,0:T(8,128)} %all_to_all.11.v_ref, f32[2,1024,128]{2,1,0:T(8,128)} %get-tuple-element.20.c_ref, f32[2,64,128]{2,1,0:T(8,128)} %get-tuple-element.21.tab_ref, f32[2,128,64]{2,1,0:T(8,128)} %get-tuple-element.22.tabt_ref, f32[4,8,128,256]{3,2,1,0:T(8,128)} %get-tuple-element.23.p_ref, ...), custom_call_target="tpu_custom_call" | custom-call | tf_op jit(solution)/shard_map/down/pallas_call | solution.py:212
  71.6 1.1 slice.35
  72.7 3.8 %collective-permute-start.1 = (f32[4,120,256]{2,1,0:T(8,128)S(1)}, f32[4,120,256]{2,1,0:T(8,128)S(1)}, u32[]{:S(2)}, u32[]{:S(2)}) collective-permute-start(f32[4,120,256]{2,1,0:T(8,128)S(1)} %slice.35), channel_id=1, source_target_pairs={{0,1},{1,0},{2,3},{3,2},{4,5},{5,4},{6,7},{7,6},{8,9},{9,8},{10,11... | collective-permute-start | bytes 1474568 | tf_op jit(solution)/shard_map/ppermute | solution.py:276
  76.5 1.5 %collective-permute-done.1 = f32[4,120,256]{2,1,0:T(8,128)S(1)} collective-permute-done((f32[4,120,256]{2,1,0:T(8,128)S(1)}, f32[4,120,256]{2,1,0:T(8,128)S(1)}, u32[]{:S(2)}, u32[]{:S(2)}) %collective-permute-start.1) | collective-permute-done | bytes 491552 | tf_op jit(solution)/shard_map/ppermute | solution.py:276
  78.0 1.1 %slice_add_fusion = f32[4,120,256]{2,1,0:T(8,128)S(1)} fusion(f32[4,120,256]{2,1,0:T(8,128)S(1)} %collective-permute-done.1, f32[8,120,256]{2,1,0:T(8,128)} %down.1), kind=kLoop, calls=%fused_computation | loop fusion | flops 122880 | bytes 1474560 | tf_op jit(solution)/shard_map/add | solution.py:276
  79.1 0.7 slice_bitcast_fusion
  79.8 2.7 %collective-permute-start.4 = (f32[120,256]{1,0:T(8,128)S(1)}, f32[120,256]{1,0:T(8,128)S(1)}, u32[]{:S(2)}, u32[]{:S(2)}) collective-permute-start(f32[120,256]{1,0:T(8,128)S(1)} %get-tuple-element.25), channel_id=1, source_target_pairs={{0,6},{2,0},{4,2},{6,4},{1,7},{3,1},{5,3},{7,5},{8,14},{10,8},{12,... | collective-permute-start | bytes 368648 | tf_op jit(solution)/shard_map/ppermute | solution.py:277
  82.5 0.4 collective-permute-start.3
  82.9 0.7 collective-permute-start.2
  83.6 3.8 %collective-permute-done.4.c_ref = f32[120,256]{1,0:T(8,128)S(1)} collective-permute-done((f32[120,256]{1,0:T(8,128)S(1)}, f32[120,256]{1,0:T(8,128)S(1)}, u32[]{:S(2)}, u32[]{:S(2)}) %collective-permute-start.4) | collective-permute-done | bytes 122912 | tf_op jit(solution)/shard_map/ppermute | solution.py:277
  87.3 0.0 copy-start
  87.3 0.9 collective-permute-done.3.b_ref
  88.2 0.0 copy-start.1
  88.2 3.7 %collective-permute-done.2.a_ref = f32[120,256]{1,0:T(8,128)S(1)} collective-permute-done((f32[120,256]{1,0:T(8,128)S(1)}, f32[120,256]{1,0:T(8,128)S(1)}, u32[]{:S(2)}, u32[]{:S(2)}) %collective-permute-start.2) | collective-permute-done | bytes 122912 | tf_op jit(solution)/shard_map/ppermute | solution.py:277
  91.9 0.0 copy-start.2
  91.9 0.0 copy-done
  91.9 0.0 copy-done.1
  91.9 0.6 copy-done.2
  92.5 1.8 %sum_up.1.refs_0_ = f32[120,256]{1,0:T(8,128)} custom-call(f32[120,256]{1,0:T(8,128)} %get-tuple-element.28.own_ref, f32[120,256]{1,0:T(8,128)} %copy-done.2, f32[120,256]{1,0:T(8,128)} %copy-done.1, f32[120,256]{1,0:T(8,128)} %copy-done), custom_call_target="tpu_custom_call" | custom-call | tf_op jit(solution)/shard_map/sum_up/pallas_call | solution.py:229
  94.4 0.0 collective-permute-start.7
  94.4 0.0 collective-permute-start.6
  94.4 1.5 %collective-permute-start.5 = (f32[120,256]{1,0:T(8,128)}, f32[120,256]{1,0:T(8,128)S(1)}, u32[]{:S(2)}, u32[]{:S(2)}) collective-permute-start(f32[120,256]{1,0:T(8,128)} %sum_up.1.refs_0_), channel_id=1, source_target_pairs={{0,2},{2,4},{4,6},{6,0},{1,3},{3,5},{5,7},{7,1},{8,10},{10,12},{12... | collective-permute-start | bytes 368648 | tf_op jit(solution)/shard_map/ppermute | solution.py:277
  95.8 1.1 collective-permute-start.8
  96.9 2.1 %collective-permute-done.7.refs_3_ = f32[120,256]{1,0:T(8,128)S(1)} collective-permute-done((f32[120,256]{1,0:T(8,128)}, f32[120,256]{1,0:T(8,128)S(1)}, u32[]{:S(2)}, u32[]{:S(2)}) %collective-permute-start.7) | collective-permute-done | bytes 122912 | tf_op jit(solution)/shard_map/ppermute | solution.py:277
  99.0 0.0 copy-start.4
  99.0 2.3 %collective-permute-start.11 = (f32[120,256]{1,0:T(8,128)S(1)}, f32[120,256]{1,0:T(8,128)S(1)}, u32[]{:S(2)}, u32[]{:S(2)}) collective-permute-start(f32[120,256]{1,0:T(8,128)S(1)} %collective-permute-done.7.refs_3_), channel_id=1, source_target_pairs={{0,1},{1,0},{2,3},{3,2},{4,5},{5,4},{6,7},{7,6},{8,9},{9,8},{10,11... | collective-permute-start | bytes 368648 | tf_op jit(solution)/shard_map/ppermute | solution.py:280
  101.3 0.0 collective-permute-done.6.refs_2_
  101.3 0.0 copy-start.5
  101.3 1.6 %collective-permute-start.10 = (f32[120,256]{1,0:T(8,128)S(1)}, f32[120,256]{1,0:T(8,128)S(1)}, u32[]{:S(2)}, u32[]{:S(2)}) collective-permute-start(f32[120,256]{1,0:T(8,128)S(1)} %collective-permute-done.6.refs_2_), channel_id=1, source_target_pairs={{0,1},{1,0},{2,3},{3,2},{4,5},{5,4},{6,7},{7,6},{8,9},{9,8},{10,11... | collective-permute-start | bytes 368648 | tf_op jit(solution)/shard_map/ppermute | solution.py:280
  102.9 0.9 collective-permute-done.5.refs_1_
  103.8 0.0 copy-start.6
  103.8 0.7 collective-permute-start.9
  104.5 0.0 collective-permute-done.8.refs_4_
  104.5 0.0 copy-start.7
  104.5 0.0 collective-permute-done.11.refs_7_
  104.5 0.0 copy-start.8
  104.5 0.0 collective-permute-done.10.refs_6_
  104.5 0.0 copy-start.9
  104.5 0.9 collective-permute-done.9.refs_5_
  105.4 0.0 copy-done.4
  105.4 0.0 copy-done.5
  105.4 0.0 copy-done.6
  105.4 0.0 copy-done.7
  105.5 0.0 copy-done.8
  105.5 0.0 copy-done.9
  105.5 0.0 copy-start.10
  105.5 0.6 copy-done.10
  106.1 2.9 %store.1 = f32[8,28800]{1,0:T(8,128)} custom-call(f32[120,256]{1,0:T(8,128)} %sum_up.1.refs_0_, f32[120,256]{1,0:T(8,128)} %copy-done.6, f32[120,256]{1,0:T(8,128)} %copy-done.5, f32[120,256]{1,0:T(8,128)} %copy-done.4, f32[120,256]{1,0:T(8,128)} %copy-done.7, f32[120,256]{1,0:T(8,128)} %copy-done.10, f32[120,256]{1,0:T(8,128)} %copy-done.9, ...), custom_call_target="tpu_custom_call" | custom-call | tf_op jit(solution)/shard_map/store/pallas_call | solution.py:254
Async XLA Ops:
  34.0 5.2 %collective-permute-start = (f32[120,256]{1,0:T(8,128)}, f32[120,256]{1,0:T(8,128)S(1)}, u32[]{:S(2)}, u32[]{:S(2)}) collective-permute-start(f32[120,256]{1,0:T(8,128)} %get-tuple-element.19.h_ref), channel_id=1, source_target_pairs={{0,96},{32,64},{64,32},{96,0},{1,97},{33,65},{65,33},{97,1},{2,98}... | collective-permute-start | bytes 368648 | tf_op jit(solution)/shard_map/ppermute | solution.py:271
  39.1 0.7 copy-start.3
  72.7 5.3 %collective-permute-start.1 = (f32[4,120,256]{2,1,0:T(8,128)S(1)}, f32[4,120,256]{2,1,0:T(8,128)S(1)}, u32[]{:S(2)}, u32[]{:S(2)}) collective-permute-start(f32[4,120,256]{2,1,0:T(8,128)S(1)} %slice.35), channel_id=1, source_target_pairs={{0,1},{1,0},{2,3},{3,2},{4,5},{5,4},{6,7},{7,6},{8,9},{9,8},{10,11... | collective-permute-start | bytes 1474568 | tf_op jit(solution)/shard_map/ppermute | solution.py:276
  79.8 7.6 %collective-permute-start.4 = (f32[120,256]{1,0:T(8,128)S(1)}, f32[120,256]{1,0:T(8,128)S(1)}, u32[]{:S(2)}, u32[]{:S(2)}) collective-permute-start(f32[120,256]{1,0:T(8,128)S(1)} %get-tuple-element.25), channel_id=1, source_target_pairs={{0,6},{2,0},{4,2},{6,4},{1,7},{3,1},{5,3},{7,5},{8,14},{10,8},{12,... | collective-permute-start | bytes 368648 | tf_op jit(solution)/shard_map/ppermute | solution.py:277
  82.5 5.7 %collective-permute-start.3 = (f32[120,256]{1,0:T(8,128)S(1)}, f32[120,256]{1,0:T(8,128)S(1)}, u32[]{:S(2)}, u32[]{:S(2)}) collective-permute-start(f32[120,256]{1,0:T(8,128)S(1)} %get-tuple-element.26), channel_id=1, source_target_pairs={{0,4},{2,6},{4,0},{6,2},{1,5},{3,7},{5,1},{7,3},{8,12},{10,14},{12... | collective-permute-start | bytes 368648 | tf_op jit(solution)/shard_map/ppermute | solution.py:277
  82.9 9.0 %collective-permute-start.2 = (f32[120,256]{1,0:T(8,128)S(1)}, f32[120,256]{1,0:T(8,128)S(1)}, u32[]{:S(2)}, u32[]{:S(2)}) collective-permute-start(f32[120,256]{1,0:T(8,128)S(1)} %get-tuple-element.27), channel_id=1, source_target_pairs={{0,2},{2,4},{4,6},{6,0},{1,3},{3,5},{5,7},{7,1},{8,10},{10,12},{12... | collective-permute-start | bytes 368648 | tf_op jit(solution)/shard_map/ppermute | solution.py:277
  87.3 4.6 %copy-start = (f32[120,256]{1,0:T(8,128)}, f32[120,256]{1,0:T(8,128)S(1)}, u32[]{:S(2)}) copy-start(f32[120,256]{1,0:T(8,128)S(1)} %collective-permute-done.4.c_ref) | copy-start | bytes 368644
  88.2 3.7 %copy-start.1 = (f32[120,256]{1,0:T(8,128)}, f32[120,256]{1,0:T(8,128)S(1)}, u32[]{:S(2)}) copy-start(f32[120,256]{1,0:T(8,128)S(1)} %collective-permute-done.3.b_ref) | copy-start | bytes 368644
  91.9 0.6 copy-start.2
  94.4 4.6 %collective-permute-start.7 = (f32[120,256]{1,0:T(8,128)}, f32[120,256]{1,0:T(8,128)S(1)}, u32[]{:S(2)}, u32[]{:S(2)}) collective-permute-start(f32[120,256]{1,0:T(8,128)} %sum_up.1.refs_0_), channel_id=1, source_target_pairs={{0,6},{2,0},{4,2},{6,4},{1,7},{3,1},{5,3},{7,5},{8,14},{10,8},{12,... | collective-permute-start | bytes 368648 | tf_op jit(solution)/shard_map/ppermute | solution.py:277
  94.4 6.9 %collective-permute-start.6 = (f32[120,256]{1,0:T(8,128)}, f32[120,256]{1,0:T(8,128)S(1)}, u32[]{:S(2)}, u32[]{:S(2)}) collective-permute-start(f32[120,256]{1,0:T(8,128)} %sum_up.1.refs_0_), channel_id=1, source_target_pairs={{0,4},{2,6},{4,0},{6,2},{1,5},{3,7},{5,1},{7,3},{8,12},{10,14},{12... | collective-permute-start | bytes 368648 | tf_op jit(solution)/shard_map/ppermute | solution.py:277
  94.4 9.4 %collective-permute-start.5 = (f32[120,256]{1,0:T(8,128)}, f32[120,256]{1,0:T(8,128)S(1)}, u32[]{:S(2)}, u32[]{:S(2)}) collective-permute-start(f32[120,256]{1,0:T(8,128)} %sum_up.1.refs_0_), channel_id=1, source_target_pairs={{0,2},{2,4},{4,6},{6,0},{1,3},{3,5},{5,7},{7,1},{8,10},{10,12},{12... | collective-permute-start | bytes 368648 | tf_op jit(solution)/shard_map/ppermute | solution.py:277
  95.8 8.6 %collective-permute-start.8 = (f32[120,256]{1,0:T(8,128)}, f32[120,256]{1,0:T(8,128)S(1)}, u32[]{:S(2)}, u32[]{:S(2)}) collective-permute-start(f32[120,256]{1,0:T(8,128)} %sum_up.1.refs_0_), channel_id=1, source_target_pairs={{0,1},{1,0},{2,3},{3,2},{4,5},{5,4},{6,7},{7,6},{8,9},{9,8},{10,11... | collective-permute-start | bytes 368648 | tf_op jit(solution)/shard_map/ppermute | solution.py:280
  99.0 6.5 %copy-start.4 = (f32[120,256]{1,0:T(8,128)}, f32[120,256]{1,0:T(8,128)S(1)}, u32[]{:S(2)}) copy-start(f32[120,256]{1,0:T(8,128)S(1)} %collective-permute-done.7.refs_3_) | copy-start | bytes 368644
  99.0 5.5 %collective-permute-start.11 = (f32[120,256]{1,0:T(8,128)S(1)}, f32[120,256]{1,0:T(8,128)S(1)}, u32[]{:S(2)}, u32[]{:S(2)}) collective-permute-start(f32[120,256]{1,0:T(8,128)S(1)} %collective-permute-done.7.refs_3_), channel_id=1, source_target_pairs={{0,1},{1,0},{2,3},{3,2},{4,5},{5,4},{6,7},{7,6},{8,9},{9,8},{10,11... | collective-permute-start | bytes 368648 | tf_op jit(solution)/shard_map/ppermute | solution.py:280
  101.3 4.2 %copy-start.5 = (f32[120,256]{1,0:T(8,128)}, f32[120,256]{1,0:T(8,128)S(1)}, u32[]{:S(2)}) copy-start(f32[120,256]{1,0:T(8,128)S(1)} %collective-permute-done.6.refs_2_) | copy-start | bytes 368644
  101.3 3.2 %collective-permute-start.10 = (f32[120,256]{1,0:T(8,128)S(1)}, f32[120,256]{1,0:T(8,128)S(1)}, u32[]{:S(2)}, u32[]{:S(2)}) collective-permute-start(f32[120,256]{1,0:T(8,128)S(1)} %collective-permute-done.6.refs_2_), channel_id=1, source_target_pairs={{0,1},{1,0},{2,3},{3,2},{4,5},{5,4},{6,7},{7,6},{8,9},{9,8},{10,11... | collective-permute-start | bytes 368648 | tf_op jit(solution)/shard_map/ppermute | solution.py:280
  103.8 1.7 %copy-start.6 = (f32[120,256]{1,0:T(8,128)}, f32[120,256]{1,0:T(8,128)S(1)}, u32[]{:S(2)}) copy-start(f32[120,256]{1,0:T(8,128)S(1)} %collective-permute-done.5.refs_1_) | copy-start | bytes 368644
  103.8 1.6 %collective-permute-start.9 = (f32[120,256]{1,0:T(8,128)S(1)}, f32[120,256]{1,0:T(8,128)S(1)}, u32[]{:S(2)}, u32[]{:S(2)}) collective-permute-start(f32[120,256]{1,0:T(8,128)S(1)} %collective-permute-done.5.refs_1_), channel_id=1, source_target_pairs={{0,1},{1,0},{2,3},{3,2},{4,5},{5,4},{6,7},{7,6},{8,9},{9,8},{10,11... | collective-permute-start | bytes 368648 | tf_op jit(solution)/shard_map/ppermute | solution.py:280
  104.5 1.0 copy-start.7
  104.5 1.0 copy-start.8
  104.5 1.0 copy-start.9
  105.5 0.7 copy-start.10

commit v2 on v1

v2 whole, which is shorter than its diff:
```python
import functools

import jax
import jax.numpy as jnp
from jax import lax
from jax.experimental import pallas as pl
from jax.experimental.pallas import tpu as pltpu
from jax.sharding import Mesh, PartitionSpec as P

M = 120
W = 2 * M
L = 128
ND = 8
F32, BF16 = jnp.float32, jnp.bfloat16
PARAMS = pltpu.CompilerParams(vmem_limit_bytes=20 * 1024 * 1024)
VMEM = pl.BlockSpec(memory_space=pltpu.VMEM)
SMEM = pl.BlockSpec(memory_space=pltpu.SMEM)


def shape(*dims):
    return jax.ShapeDtypeStruct(dims, F32)


def split(x):
    high = x.astype(BF16)
    return high, (x - high.astype(F32)).astype(BF16)


def right_form(x):
    real, imag = x[:, :L], x[:, L:]
    return jnp.concatenate([x, jnp.concatenate([-imag, real], axis=1)], axis=0)


def dot(a, b):
    return jnp.dot(a, b, preferred_element_type=F32)


def product(left, right):
    left_high, left_low = split(left)
    right_high, right_low = split(right_form(right))
    return dot(left_high, right_high) + (dot(left_low, right_high) + dot(left_high, right_low))


def scaled(x, cosine, sine):
    real, imag = x[:, :L], x[:, L:]
    return jnp.concatenate([cosine * real - sine * imag, cosine * imag + sine * real], axis=1)


def adjoint(x):
    return jnp.concatenate([x[:, :L].T, -x[:, L:].T], axis=1)


def padded(x):
    return jnp.concatenate([x, jnp.zeros((L - M, 2 * L), F32)], axis=0)


def unpack_rows(flat_ref, out_ref):
    out_ref[...] = jnp.zeros(out_ref.shape, F32)
    zeros = jnp.zeros((ND, L - M), F32)
    for m in range(M):
        rows = pl.ds(m, ND, stride=L)
        real = flat_ref[:, m * W : m * W + M]
        imag = flat_ref[:, m * W + M : (m + 1) * W]
        out_ref[0, rows, :] = jnp.concatenate([real, zeros], axis=1)
        out_ref[1, rows, :] = jnp.concatenate([imag, zeros], axis=1)


def unpacked(rows_ref, start):
    return jnp.concatenate([rows_ref[0, pl.ds(start, L), :], rows_ref[1, pl.ds(start, L), :]], axis=1)


OFFSETS = (6, 2, 7, 5, 4, 3, 1, 0)
HALF = ND // 2


def number():
    return lax.axis_index("zl") * 4 + lax.axis_index("x")


def owned():
    return number() ^ (lax.axis_index("zh") * 4)


def scalings(tab_ref, tabt_ref):
    def columns(x, k, f):
        i = f * ND + k
        return scaled(x, tab_ref[0, i : i + 1, :], tab_ref[1, i : i + 1, :])

    def rows(x, k, f):
        i = f * ND + k
        return scaled(x, tabt_ref[0, :, i : i + 1], tabt_ref[1, :, i : i + 1])

    return columns, rows


def up_half(first, a_refs, c_ref, tab_ref, tabt_ref, p_ref, q_ref, lhs_ref):
    columns, rows = scalings(tab_ref, tabt_ref)
    for j in range(4):
        low, up = 2 * j, 2 * j + 1
        c_up = unpacked(c_ref, up * L)
        for f in range(HALF):
            lhs_ref[f * L : (f + 1) * L, :] = columns(c_up, low, first + f)
        res = product(lhs_ref[...], unpacked(c_ref, low * L))
        for f in range(HALF):
            one = res[f * L : (f + 1) * L]
            p_ref[j, f] = rows(one, up, first + f) if j % 2 == 0 else one
    for f in range(HALF):
        q0 = rows(product(p_ref[1, f], p_ref[0, f]), 3, first + f)
        q1 = product(p_ref[3, f], p_ref[2, f])
        q_ref[0, f] = q0
        q_ref[1, f] = q1
        a_refs[f][...] = rows(product(q1, q0), 7, first + f)[:M]


def up_first_kernel(freq_ref, prop_ref, flat_ref, c_ref, tab_ref, tabt_ref, p_ref, q_ref, *refs):
    tab_ref[...] = jnp.zeros(tab_ref.shape, F32)
    for f in range(ND):
        phase = prop_ref[...] * freq_ref[owned() ^ OFFSETS[f]]
        tab_ref[0, f * ND : (f + 1) * ND, 0:M] = jnp.cos(phase)
        tab_ref[1, f * ND : (f + 1) * ND, 0:M] = jnp.sin(phase)
    tabt_ref[0] = tab_ref[0].T
    tabt_ref[1] = tab_ref[1].T
    unpack_rows(flat_ref, c_ref)
    up_half(0, refs[:HALF], c_ref, tab_ref, tabt_ref, p_ref, q_ref, refs[HALF])


def up_second_kernel(c_ref, tab_ref, tabt_ref, p_ref, q_ref, *refs):
    up_half(HALF, refs[:HALF], c_ref, tab_ref, tabt_ref, p_ref, q_ref, refs[HALF])


NODES = (shape(4, HALF, L, 2 * L), shape(2, HALF, L, 2 * L))
LHS = [pltpu.VMEM((HALF * L, 2 * L), F32)]


def up_first(freq, prop, flat):
    tables = (shape(2, ND * L, L), shape(2, ND * ND, L), shape(2, L, ND * ND))
    outs = tables + NODES + (shape(M, 2 * L),) * HALF
    res = pl.pallas_call(
        up_first_kernel,
        out_shape=outs,
        in_specs=[SMEM, VMEM, VMEM],
        out_specs=(VMEM,) * len(outs),
        scratch_shapes=LHS,
        compiler_params=PARAMS,
        name="up_first",
    )(freq, prop, flat)
    return res[:3], res[3:5], res[5:]


def up_second(tables):
    outs = NODES + (shape(M, 2 * L),) * HALF
    res = pl.pallas_call(
        up_second_kernel,
        out_shape=outs,
        in_specs=[VMEM] * 3,
        out_specs=(VMEM,) * len(outs),
        scratch_shapes=LHS,
        compiler_params=PARAMS,
        name="up_second",
    )(*tables)
    return res[:2], res[2:]


def half_kernel(*refs):
    received, (h_ref, r_ref, p_ref, q_ref) = refs[:ND], refs[ND:]
    me = number()
    for i, offset in enumerate(OFFSETS):
        r_ref[me ^ offset] = padded(received[i][...])
    for j in range(4):
        p_ref[j] = product(r_ref[2 * j + 1], r_ref[2 * j])
    for j in range(2):
        q_ref[j] = product(p_ref[2 * j + 1], p_ref[2 * j])
    h_ref[...] = product(q_ref[1], q_ref[0])[:M]


def half(received):
    return pl.pallas_call(
        half_kernel,
        out_shape=(shape(M, 2 * L), shape(ND, L, 2 * L), shape(4, L, 2 * L), shape(2, L, 2 * L)),
        in_specs=[VMEM] * ND,
        out_specs=(VMEM,) * 4,
        compiler_params=PARAMS,
        name="half",
    )(*received)


def pick_kernel(flat_ref, m_ref, rows_ref):
    unpack_rows(flat_ref, rows_ref)
    m_ref[...] = unpacked(rows_ref, pl.multiple_of(owned() * L, L))


def pick(flat):
    return pl.pallas_call(
        pick_kernel,
        out_shape=shape(L, 2 * L),
        in_specs=[VMEM],
        out_specs=VMEM,
        scratch_shapes=[pltpu.VMEM((2, ND * L, L), F32)],
        compiler_params=PARAMS,
        name="pick",
    )(flat)


def top_kernel(r_ref, m_ref, p_ref, q_ref, h_ref, other_ref, *refs):
    v_refs, leaf_ref = refs[:ND], refs[ND]
    upper = lax.axis_index("zh") == 1
    own, other = padded(h_ref[...]), padded(other_ref[...])
    h0 = jnp.where(upper, other, own)
    h1 = jnp.where(upper, own, other)
    misfit = adjoint(product(h1, h0) - m_ref[...])
    v = product(jnp.where(upper, h0, misfit), jnp.where(upper, misfit, h1))
    v0, v1 = product(v, q_ref[1]), product(q_ref[0], v)
    pairs = (product(v0, p_ref[1]), product(p_ref[0], v0), product(v1, p_ref[3]), product(p_ref[2], v1))
    for j in range(4):
        leaf_ref[2 * j] = product(pairs[j], r_ref[2 * j + 1])[:M]
        leaf_ref[2 * j + 1] = product(r_ref[2 * j], pairs[j])[:M]
    me = number()
    for i, offset in enumerate(OFFSETS):
        v_refs[i][...] = leaf_ref[me ^ offset]


def top(r, m, p, q, h, other):
    return pl.pallas_call(
        top_kernel,
        out_shape=(shape(M, 2 * L),) * ND,
        in_specs=[VMEM] * 6,
        out_specs=(VMEM,) * ND,
        scratch_shapes=[pltpu.VMEM((ND, M, 2 * L), F32)],
        compiler_params=PARAMS,
        name="top",
    )(r, m, p, q, h, other)


def quad_down(quad, first, v, c_ref, tab_ref, tabt_ref, p_ref, q_ref, vp_ref):
    columns, rows = scalings(tab_ref, tabt_ref)
    for f in range(HALF):
        if quad == 0:
            mine = columns(product(v[f], q_ref[1, f]), 3, first + f)
        else:
            mine = product(q_ref[0, f], v[f])
        at = pl.ds(f * L, L)
        vp_ref[0, at] = columns(product(mine, p_ref[2 * quad + 1, f]), 4 * quad + 1, first + f)
        vp_ref[1, at] = product(p_ref[2 * quad, f], mine)
    out = []
    for j in range(2):
        low, up = 4 * quad + 2 * j, 4 * quad + 2 * j + 1
        c_low = unpacked(c_ref, low * L)
        res = product(vp_ref[j], unpacked(c_ref, up * L))
        g_low = columns(res[0:L], low, first)
        g_up = rows(product(c_low, vp_ref[j, 0:L]), low, first)
        for f in range(1, HALF):
            g_low += columns(res[f * L : (f + 1) * L], low, first + f)
            g_up += rows(product(c_low, vp_ref[j, f * L : (f + 1) * L]), low, first + f)
        out += [g_low[:M], g_up[:M]]
    return out


def whole_v(first, v_refs, tab_ref, tabt_ref):
    columns, _ = scalings(tab_ref, tabt_ref)
    return [columns(padded(v_refs[f][...]), 7, first + f) for f in range(HALF)]


def down_first_kernel(*refs):
    v_refs, (c_ref, tab_ref, tabt_ref, p_ref, q_ref, g_ref, vp_ref) = refs[:HALF], refs[HALF:]
    v = whole_v(0, v_refs, tab_ref, tabt_ref)
    for quad in range(2):
        res = quad_down(quad, 0, v, c_ref, tab_ref, tabt_ref, p_ref, q_ref, vp_ref)
        for i in range(4):
            g_ref[4 * quad + i] = res[i]


VP = [pltpu.VMEM((2, HALF * L, 2 * L), F32)]


def down_first(v, tables, nodes):
    return pl.pallas_call(
        down_first_kernel,
        out_shape=shape(ND, M, 2 * L),
        in_specs=[VMEM] * (HALF + 5),
        out_specs=VMEM,
        scratch_shapes=VP,
        compiler_params=PARAMS,
        name="down_first",
    )(*v, *tables, *nodes)


def down_second_kernel(mine, *refs):
    v_refs, (c_ref, tab_ref, tabt_ref, p_ref, q_ref, part_ref, g_ref, vp_ref) = refs[:HALF], refs[HALF:]
    core, y = lax.axis_index("c"), lax.axis_index("y")
    for quad in range(2):

        @pl.when(core == (quad if mine else 1 - quad))
        def _():
            v = whole_v(HALF, v_refs, tab_ref, tabt_ref)
            res = quad_down(quad, HALF, v, c_ref, tab_ref, tabt_ref, p_ref, q_ref, vp_ref)
            for i in range(4):
                g_ref[(i - y + 4) % 4] = res[i] + part_ref[4 * quad + i]


def down_second(mine, v, tables, nodes, part):
    return pl.pallas_call(
        functools.partial(down_second_kernel, mine),
        out_shape=shape(4, M, 2 * L),
        in_specs=[VMEM] * (HALF + 6),
        out_specs=VMEM,
        scratch_shapes=VP,
        compiler_params=PARAMS,
        name="down_mine" if mine else "down_theirs",
    )(*v, *tables, *nodes, part)


def sum_kernel(own_ref, a_ref, b_ref, c_ref, out_ref):
    total = (own_ref[...] + a_ref[...]) + (b_ref[...] + c_ref[...])
    out_ref[...] = 2.0 * adjoint(padded(total))[:M]


def sum_up(own, a, b, c):
    return pl.pallas_call(
        sum_kernel,
        out_shape=shape(M, 2 * L),
        in_specs=[VMEM] * 4,
        out_specs=VMEM,
        compiler_params=PARAMS,
        name="sum_up",
    )(own, a, b, c)


def store_kernel(*refs):
    parts, out_ref, rows_ref = refs[:ND], refs[ND], refs[ND + 1]
    core, y = lax.axis_index("c"), lax.axis_index("y")
    for i in range(ND):
        place = (4 * core if i < 4 else 4 * (1 - core)) + (y - i % 4 + 4) % 4
        at = pl.ds(pl.multiple_of(place * L, L), M)
        rows_ref[0, at, :] = parts[i][:, :L]
        rows_ref[1, at, :] = parts[i][:, L:]
    for m in range(M):
        rows = pl.ds(m, ND, stride=L)
        out_ref[:, m * W : m * W + M] = rows_ref[0, rows, :][:, :M]
        out_ref[:, m * W + M : (m + 1) * W] = rows_ref[1, rows, :][:, :M]


def store(parts):
    return pl.pallas_call(
        store_kernel,
        out_shape=shape(ND, M * W),
        in_specs=[VMEM] * ND,
        out_specs=VMEM,
        scratch_shapes=[pltpu.VMEM((2, ND * L, L), F32)],
        compiler_params=PARAMS,
        name="store",
    )(*parts)


def shards(coupling, propagation, frequency_offset, measured):
    swap = [(0, 1), (1, 0)]

    def exchange(offset, x):
        return lax.ppermute(x, ("zl", "x"), [(s, s ^ offset) for s in range(ND)]) if offset else x

    def turned(i, x):
        return lax.ppermute(x, "y", [(s, (s + i) % 4) for s in range(4)])

    tables, nodes_first, a_first = up_first(frequency_offset, propagation, coupling)
    nodes_second, a_second = up_second(tables)
    received = [exchange(offset, a) for offset, a in zip(OFFSETS, (*a_first, *a_second))]
    h, r, p, q = half(received)
    other = lax.ppermute(h, ("zh", "zl"), [(0, 3), (1, 2), (2, 1), (3, 0)])
    v = top(r, pick(measured), p, q, h, other)
    v = [exchange(offset, x) for offset, x in zip(OFFSETS, v)]
    part = down_first(v[:HALF], tables, nodes_first)
    theirs = down_second(False, v[HALF:], tables, nodes_second, part)
    received = lax.ppermute(theirs, "c", swap)
    mine = down_second(True, v[HALF:], tables, nodes_second, part)
    g = mine + received
    total = sum_up(g[0], *[turned(i, g[i]) for i in range(1, 4)])
    parts = [total] + [turned(i, total) for i in range(1, 4)]
    parts += [lax.ppermute(x, "c", swap) for x in parts]
    return store(parts)


def solution(mesh):
    fine = Mesh(mesh.devices.reshape(2, 2, 4, 4, 2), ("zh", "zl", "x", "y", "c"))
    sec, freq = ("zh", "zl", "x"), ("y", "c")
    return jax.shard_map(
        shards,
        mesh=fine,
        in_specs=(P(sec, None), P(sec, None), P(freq), P(freq, None)),
        out_specs=P(sec, None),
        check_vma=False,
    )
```

time: 110 us -> 83.4 us (0.76)
  blocking collectives: 37 us -> 0 us
  starting transfers between devices: 16.4 us -> 35.3 us
  Pallas kernels: 31.5 us -> 19.9 us
  waiting for transfers between devices: 17.2 us -> 25.2 us
  other arithmetic: 2.34 us -> 0.06 us
  local copies, waits for them, and re-layouts: 4.53 us -> 2.56 us
    all_to_all x2 -> x0, blocking collectives: 37 us -> none  [the longest x1 20.6 us: shards(): r = lax.all_to_all(a, ('zl', 'x'), 0, 0, tiled=True)]
    ppermute x7 -> x21, starting transfers between devices: 9.08 us -> 26.3 us  [the longest x14 19 us: exchange(): lax.ppermute(x, ('zl', 'x'), [(s, s ^ offset) for s in range(ND)])]
    ppermute x7 -> x21, waiting for transfers between devices: 12.8 us -> 21.9 us  [the longest x6 11.3 us: turned(): return lax.ppermute(x, 'y', [(s, (s + i) % 4) for s in range(4)])]
    pallas_call x4 -> x8, Pallas kernels: 26.8 us -> 18.1 us  [the longest x2 4.52 us: down_second(): pl.pallas_call(functools.partial(down_second_kernel, mine), out_shape=sha...]
    slice x2 -> x0, local copies, waits for them, and re-layouts: 1.86 us -> none  [the longest x1 1.06 us: shards(): g = g[:4] + lax.ppermute(g[4:], 'c', swap)]
    pallas_call x1, Pallas kernels: 1.83 us -> 0.1 us  [sum_up(): pl.pallas_call(sum_kernel, out_shape=shape(M, 2 * L), in_specs=[VMEM] * 4...]
    ppermute x1, starting transfers between devices: 1.75 us -> 3.45 us  [shards(): other = lax.ppermute(h, ('zh', 'zl'), [(0, 3), (1, 2), (2, 1), (3, 0)])]
    pallas_call x1, Pallas kernels: 2.94 us -> 1.67 us  [store(): pl.pallas_call(store_kernel, out_shape=shape(ND, M * W), in_specs=[VMEM]...]
  transfers between devices with their start and end apart: 12 -> 26, of which waited for: 8 -> 11; matrix products, arithmetic and copies ran while one was open for 0% -> 0% of each run, Pallas kernels for 0% -> 12%
where the time goes in v2:
time: 83.4 us; the launch traced here: 83.2 us
  starting transfers between devices  35.3 us (42%)
  waiting for transfers between devices  25.2 us (30%)
  Pallas kernels  19.9 us (24%)
  local copies, waits for them, and re-layouts  2.56 us (3%)
    ppermute x14, starting transfers between devices, exchange(): lax.ppermute(x, ('zl', 'x'), [(s, s ^ offset) for s in range(ND)])  19 us
    ppermute x6, waiting for transfers between devices, turned(): return lax.ppermute(x, 'y', [(s, (s + i) % 4) for s in range(4)])  11.3 us
    ppermute x14, waiting for transfers between devices, exchange(): lax.ppermute(x, ('zl', 'x'), [(s, s ^ offset) for s in range(ND)])  10.6 us
    ppermute x4, starting transfers between devices, shards(): parts += [lax.ppermute(x, 'c', swap) for x in parts]  5.54 us
    ppermute x6, starting transfers between devices, turned(): return lax.ppermute(x, 'y', [(s, (s + i) % 4) for s in range(4)])  5.37 us
    pallas_call x2, Pallas kernels, down_second(): pl.pallas_call(functools.partial(down_second_kernel, mine), out_shape=sha...  4.52 us
    pallas_call x1, Pallas kernels, down_first(): pl.pallas_call(down_first_kernel, out_shape=shape(ND, M, 2 * L), in_specs...  4.23 us
    pallas_call x1, Pallas kernels, up_first(): pl.pallas_call(up_first_kernel, out_shape=outs, in_specs=[SMEM, VMEM, VME...  3.78 us
  transfers between devices with their start and end apart: 26, of which 11 were waited for; matrix products, arithmetic and copies ran while one was open for 0% of the time, Pallas kernels for 12%

profile of v2, /device:TPU:1, one launch (start us, length us, event | category | flops | bytes accessed | tf_op | source)
XLA Modules:
  0.0 83.2 jit_solution(252454837293542816)
XLA Ops:
  0.0 1.2 %copy-done = f32[8,28800]{1,0:T(8,128)S(1)} copy-done((f32[8,28800]{1,0:T(8,128)S(1)}, f32[8,28800]{1,0:T(8,128)}, u32[]{:S(2)}) %copy-start) | copy-done | bytes 921624
  1.2 0.7 copy-done.2
  1.9 0.7 copy-done.3
  2.5 3.8 %up_first.1 = (f32[2,1024,128]{2,1,0:T(8,128)S(1)}, f32[2,64,128]{2,1,0:T(8,128)S(1)}, f32[2,128,64]{2,1,0:T(8,128)S(1)}, f32[4,4,128,256]{3,2,1,0:T(8,128)S(1)}...) custom-call(f32[8]{0:T(128)S(1)} %copy-done.3, ...), custom_call_target="tpu_custom_call" | custom-call | tf_op jit(solution)/shard_map/up_first/pallas_call | solution.py:138
  6.3 5.0 %collective-permute-start = (f32[120,256]{1,0:T(8,128)S(1)}, f32[120,256]{1,0:T(8,128)S(1)}, u32[]{:S(2)}, u32[]{:S(2)}) collective-permute-start(f32[120,256]{1,0:T(8,128)S(1)} %get-tuple-element.32), channel_id=1, source_target_pairs={{0,48},{8,56},{16,32},{24,40},{32,16},{40,24},{48,0},{56,8},{1,49}... | collective-permute-start | bytes 368648 | tf_op jit(solution)/shard_map/ppermute | solution.py:358
  11.3 0.2 collective-permute-start.1
  11.6 2.0 %collective-permute-start.2 = (f32[120,256]{1,0:T(8,128)S(1)}, f32[120,256]{1,0:T(8,128)S(1)}, u32[]{:S(2)}, u32[]{:S(2)}) collective-permute-start(f32[120,256]{1,0:T(8,128)S(1)} %get-tuple-element.34), channel_id=1, source_target_pairs={{0,56},{8,48},{16,40},{24,32},{32,24},{40,16},{48,8},{56,0},{1,57}... | collective-permute-start | bytes 368648 | tf_op jit(solution)/shard_map/ppermute | solution.py:358
  13.6 1.3 %collective-permute-start.3 = (f32[120,256]{1,0:T(8,128)S(1)}, f32[120,256]{1,0:T(8,128)S(1)}, u32[]{:S(2)}, u32[]{:S(2)}) collective-permute-start(f32[120,256]{1,0:T(8,128)S(1)} %get-tuple-element.35), channel_id=1, source_target_pairs={{0,40},{8,32},{16,56},{24,48},{32,8},{40,0},{48,24},{56,16},{1,41}... | collective-permute-start | bytes 368648 | tf_op jit(solution)/shard_map/ppermute | solution.py:358
  14.9 2.3 %up_second.1 = (f32[4,4,128,256]{3,2,1,0:T(8,128)S(1)}, f32[2,4,128,256]{3,2,1,0:T(8,128)S(1)}, f32[120,256]{1,0:T(8,128)S(1)}, f32[120,256]{1,0:T(8,128)S(1)}, ...) custom-call(f32[2,1024,128]{2,1,0:T(8,128)S(1)} %get-tuple-element.36.c_ref.refs_4_, ...), custom_call_target="tpu_custom_call" | custom-call | tf_op jit(solution)/shard_map/up_second/pallas_call | solution.py:152
  17.1 0.4 collective-permute-start.4
  17.6 0.0 collective-permute-done.refs_0_
  17.6 0.6 collective-permute-start.5
  18.2 0.0 collective-permute-done.1.refs_1_
  18.2 0.8 collective-permute-start.6
  19.0 2.5 %collective-permute-done.2.refs_2_ = f32[120,256]{1,0:T(8,128)S(1)} collective-permute-done((f32[120,256]{1,0:T(8,128)S(1)}, f32[120,256]{1,0:T(8,128)S(1)}, u32[]{:S(2)}, u32[]{:S(2)}) %collective-permute-start.2) | collective-permute-done | bytes 122912 | tf_op jit(solution)/shard_map/ppermute | solution.py:358
  21.4 0.0 collective-permute-done.3.refs_3_
  21.4 3.7 %collective-permute-done.4.refs_4_ = f32[120,256]{1,0:T(8,128)S(1)} collective-permute-done((f32[120,256]{1,0:T(8,128)S(1)}, f32[120,256]{1,0:T(8,128)S(1)}, u32[]{:S(2)}, u32[]{:S(2)}) %collective-permute-start.4) | collective-permute-done | bytes 122912 | tf_op jit(solution)/shard_map/ppermute | solution.py:358
  25.1 0.0 collective-permute-done.5.refs_5_
  25.1 0.0 collective-permute-done.6.refs_6_
  25.1 0.9 %half.1 = (f32[120,256]{1,0:T(8,128)S(1)}, f32[8,128,256]{2,1,0:T(8,128)S(1)}, f32[4,128,256]{2,1,0:T(8,128)S(1)}, f32[2,128,256]{2,1,0:T(8,128)S(1)}) custom-call(f32[120,256]{1,0:T(8,128)S(1)} %collective-permute-done.refs_0_, f32[120,256]{1,0:T(8,128)S(1)} %collective-permute-done.1.refs_1_, f32[120,256]{1,0:T(8,128)S(1)} %collective-permute-done.2.refs_2_, ...), custom_call_target="tpu_custom_call" | custom-call | tf_op jit(solution)/shard_map/half/pallas_call | solution.py:177
  26.0 3.4 %collective-permute-start.7 = (f32[120,256]{1,0:T(8,128)S(1)}, f32[120,256]{1,0:T(8,128)S(1)}, u32[]{:S(2)}, u32[]{:S(2)}) collective-permute-start(f32[120,256]{1,0:T(8,128)S(1)} %get-tuple-element.46.h_ref), channel_id=1, source_target_pairs={{0,96},{32,64},{64,32},{96,0},{1,97},{33,65},{65,33},{97,1},{2,98}... | collective-permute-start | bytes 368648 | tf_op jit(solution)/shard_map/ppermute | solution.py:367
  29.5 0.9 %pick.1.m_ref = f32[128,256]{1,0:T(8,128)S(1)} custom-call(f32[8,28800]{1,0:T(8,128)S(1)} %copy-done.1), custom_call_target="tpu_custom_call" | custom-call | tf_op jit(solution)/shard_map/pick/pallas_call | solution.py:193
  30.3 2.4 %collective-permute-done.7.other_ref = f32[120,256]{1,0:T(8,128)S(1)} collective-permute-done((f32[120,256]{1,0:T(8,128)S(1)}, f32[120,256]{1,0:T(8,128)S(1)}, u32[]{:S(2)}, u32[]{:S(2)}) %collective-permute-start.7) | collective-permute-done | bytes 122912 | tf_op jit(solution)/shard_map/ppermute | solution.py:367
  32.7 1.6 %top.1 = (f32[120,256]{1,0:T(8,128)S(1)}, f32[120,256]{1,0:T(8,128)S(1)}, f32[120,256]{1,0:T(8,128)S(1)}, f32[120,256]{1,0:T(8,128)S(1)}, f32[120,256]{1,0:T(8,1...) custom-call(f32[8,128,256]{2,1,0:T(8,128)S(1)} %get-tuple-element.43.r_ref, ...), custom_call_target="tpu_custom_call" | custom-call | tf_op jit(solution)/shard_map/top/pallas_call | solution.py:223
  34.3 0.7 collective-permute-start.11
  35.0 1.7 %collective-permute-start.12 = (f32[120,256]{1,0:T(8,128)S(1)}, f32[120,256]{1,0:T(8,128)S(1)}, u32[]{:S(2)}, u32[]{:S(2)}) collective-permute-start(f32[120,256]{1,0:T(8,128)S(1)} %get-tuple-element.54), channel_id=1, source_target_pairs={{0,16},{8,24},{16,0},{24,8},{32,48},{40,56},{48,32},{56,40},{1,17}... | collective-permute-start | bytes 368648 | tf_op jit(solution)/shard_map/ppermute | solution.py:358
  36.7 1.8 %collective-permute-start.8 = (f32[120,256]{1,0:T(8,128)S(1)}, f32[120,256]{1,0:T(8,128)S(1)}, u32[]{:S(2)}, u32[]{:S(2)}) collective-permute-start(f32[120,256]{1,0:T(8,128)S(1)} %get-tuple-element.47), channel_id=1, source_target_pairs={{0,32},{8,40},{16,48},{24,56},{32,0},{40,8},{48,16},{56,24},{1,33}... | collective-permute-start | bytes 368648 | tf_op jit(solution)/shard_map/ppermute | solution.py:358
  38.5 0.4 collective-permute-start.13
  39.0 1.6 %collective-permute-start.14 = (f32[120,256]{1,0:T(8,128)S(1)}, f32[120,256]{1,0:T(8,128)S(1)}, u32[]{:S(2)}, u32[]{:S(2)}) collective-permute-start(f32[120,256]{1,0:T(8,128)S(1)} %get-tuple-element.56), channel_id=1, source_target_pairs={{0,40},{8,32},{16,56},{24,48},{32,8},{40,0},{48,24},{56,16},{1,41}... | collective-permute-start | bytes 368648 | tf_op jit(solution)/shard_map/ppermute | solution.py:358
  40.6 0.1 collective-permute-done.11.refs_0_
  40.6 1.8 %collective-permute-start.9 = (f32[120,256]{1,0:T(8,128)S(1)}, f32[120,256]{1,0:T(8,128)S(1)}, u32[]{:S(2)}, u32[]{:S(2)}) collective-permute-start(f32[120,256]{1,0:T(8,128)S(1)} %get-tuple-element.48), channel_id=1, source_target_pairs={{0,24},{8,16},{16,8},{24,0},{32,56},{40,48},{48,40},{56,32},{1,25}... | collective-permute-start | bytes 368648 | tf_op jit(solution)/shard_map/ppermute | solution.py:358
  42.4 0.0 collective-permute-done.12.refs_1_
  42.4 0.6 collective-permute-start.10
  43.0 4.3 %collective-permute-done.13.refs_2_ = f32[120,256]{1,0:T(8,128)S(1)} collective-permute-done((f32[120,256]{1,0:T(8,128)S(1)}, f32[120,256]{1,0:T(8,128)S(1)}, u32[]{:S(2)}, u32[]{:S(2)}) %collective-permute-start.13) | collective-permute-done | bytes 122912 | tf_op jit(solution)/shard_map/ppermute | solution.py:358
  47.3 0.0 collective-permute-done.14.refs_3_
  47.3 4.2 %down_first.1.refs_9_ = f32[8,120,256]{2,1,0:T(8,128)S(1)} custom-call(f32[120,256]{1,0:T(8,128)S(1)} %collective-permute-done.11.refs_0_, f32[120,256]{1,0:T(8,128)S(1)} %collective-permute-done.12.refs_1_, f32[120,256]{1,0:T(8,128)S(1)} %collective-permute-done.13.refs_2_, f32[120,256]{1,0:T(8,128)S(1)} %collective-permute-done.14.refs_3_, ...), custom_call_target="tpu_custom_call" | custom-call | tf_op jit(solution)/shard_map/down_first/pallas_call | solution.py:276
  51.6 0.0 collective-permute-done.8.refs_0_
  51.6 0.0 collective-permute-done.9.refs_1_
  51.6 0.0 collective-permute-done.10.refs_2_
  51.6 2.3 %down_theirs.1 = f32[4,120,256]{2,1,0:T(8,128)S(1)} custom-call(f32[120,256]{1,0:T(8,128)S(1)} %collective-permute-done.8.refs_0_, f32[120,256]{1,0:T(8,128)S(1)} %collective-permute-done.9.refs_1_, f32[120,256]{1,0:T(8,128)S(1)} %collective-permute-done.10.refs_2_, f32[120,256]{1,0:T(8,128)S(1)} %get-tuple-element.50.refs_3_, ...), custom_call_target="tpu_custom_call" | custom-call | tf_op jit(solution)/shard_map/down_theirs/pallas_call | solution.py:301
  53.9 1.9 %collective-permute-start.15 = (f32[4,120,256]{2,1,0:T(8,128)S(1)}, f32[4,120,256]{2,1,0:T(8,128)S(1)}, u32[]{:S(2)}, u32[]{:S(2)}) collective-permute-start(f32[4,120,256]{2,1,0:T(8,128)S(1)} %down_theirs.1), channel_id=1, source_target_pairs={{0,1},{1,0},{2,3},{3,2},{4,5},{5,4},{6,7},{7,6},{8,9},{9,8},{10,11... | collective-permute-start | bytes 1474568 | tf_op jit(solution)/shard_map/ppermute | solution.py:372
  55.8 2.3 %down_mine.1 = f32[4,120,256]{2,1,0:T(8,128)S(1)} custom-call(f32[120,256]{1,0:T(8,128)S(1)} %collective-permute-done.8.refs_0_, f32[120,256]{1,0:T(8,128)S(1)} %collective-permute-done.9.refs_1_, f32[120,256]{1,0:T(8,128)S(1)} %collective-permute-done.10.refs_2_, f32[120,256]{1,0:T(8,128)S(1)} %get-tuple-element.50.refs_3_, ...), custom_call_target="tpu_custom_call" | custom-call | tf_op jit(solution)/shard_map/down_mine/pallas_call | solution.py:301
  58.1 0.1 add.3
  58.2 2.8 %collective-permute-start.18 = (f32[120,256]{1,0:T(8,128)S(1)}, f32[120,256]{1,0:T(8,128)S(1)}, u32[]{:S(2)}, u32[]{:S(2)}) collective-permute-start(f32[120,256]{1,0:T(8,128)S(1)} %get-tuple-element.59), channel_id=1, source_target_pairs={{0,6},{2,0},{4,2},{6,4},{1,7},{3,1},{5,3},{7,5},{8,14},{10,8},{12,... | collective-permute-start | bytes 368648 | tf_op jit(solution)/shard_map/ppermute | solution.py:361
  61.0 0.3 collective-permute-start.17
  61.3 0.7 collective-permute-start.16
  62.0 3.9 %collective-permute-done.18.c_ref = f32[120,256]{1,0:T(8,128)S(1)} collective-permute-done((f32[120,256]{1,0:T(8,128)S(1)}, f32[120,256]{1,0:T(8,128)S(1)}, u32[]{:S(2)}, u32[]{:S(2)}) %collective-permute-start.18) | collective-permute-done | bytes 122912 | tf_op jit(solution)/shard_map/ppermute | solution.py:361
  66.0 0.9 %collective-permute-done.17.b_ref = f32[120,256]{1,0:T(8,128)S(1)} collective-permute-done((f32[120,256]{1,0:T(8,128)S(1)}, f32[120,256]{1,0:T(8,128)S(1)}, u32[]{:S(2)}, u32[]{:S(2)}) %collective-permute-start.17) | collective-permute-done | bytes 122912 | tf_op jit(solution)/shard_map/ppermute | solution.py:361
  66.9 3.5 %collective-permute-done.16.a_ref = f32[120,256]{1,0:T(8,128)S(1)} collective-permute-done((f32[120,256]{1,0:T(8,128)S(1)}, f32[120,256]{1,0:T(8,128)S(1)}, u32[]{:S(2)}, u32[]{:S(2)}) %collective-permute-start.16) | collective-permute-done | bytes 122912 | tf_op jit(solution)/shard_map/ppermute | solution.py:361
  70.4 0.1 sum_up.1.refs_0_
  70.5 0.1 collective-permute-start.21
  70.6 0.1 collective-permute-start.20
  70.7 1.3 %collective-permute-start.19 = (f32[120,256]{1,0:T(8,128)S(1)}, f32[120,256]{1,0:T(8,128)S(1)}, u32[]{:S(2)}, u32[]{:S(2)}) collective-permute-start(f32[120,256]{1,0:T(8,128)S(1)} %sum_up.1.refs_0_), channel_id=1, source_target_pairs={{0,2},{2,4},{4,6},{6,0},{1,3},{3,5},{5,7},{7,1},{8,10},{10,12},{12... | collective-permute-start | bytes 368648 | tf_op jit(solution)/shard_map/ppermute | solution.py:361
  72.0 1.1 %collective-permute-start.22 = (f32[120,256]{1,0:T(8,128)S(1)}, f32[120,256]{1,0:T(8,128)S(1)}, u32[]{:S(2)}, u32[]{:S(2)}) collective-permute-start(f32[120,256]{1,0:T(8,128)S(1)} %sum_up.1.refs_0_), channel_id=1, source_target_pairs={{0,1},{1,0},{2,3},{3,2},{4,5},{5,4},{6,7},{7,6},{8,9},{9,8},{10,11... | collective-permute-start | bytes 368648 | tf_op jit(solution)/shard_map/ppermute | solution.py:377
  73.1 1.9 %collective-permute-done.21.refs_3_ = f32[120,256]{1,0:T(8,128)S(1)} collective-permute-done((f32[120,256]{1,0:T(8,128)S(1)}, f32[120,256]{1,0:T(8,128)S(1)}, u32[]{:S(2)}, u32[]{:S(2)}) %collective-permute-start.21) | collective-permute-done | bytes 122912 | tf_op jit(solution)/shard_map/ppermute | solution.py:361
  75.0 2.3 %collective-permute-start.25 = (f32[120,256]{1,0:T(8,128)S(1)}, f32[120,256]{1,0:T(8,128)S(1)}, u32[]{:S(2)}, u32[]{:S(2)}) collective-permute-start(f32[120,256]{1,0:T(8,128)S(1)} %collective-permute-done.21.refs_3_), channel_id=1, source_target_pairs={{0,1},{1,0},{2,3},{3,2},{4,5},{5,4},{6,7},{7,6},{8,9},{9,8},{10,11... | collective-permute-start | bytes 368648 | tf_op jit(solution)/shard_map/ppermute | solution.py:377
  77.2 0.0 collective-permute-done.20.refs_2_
  77.2 1.6 %collective-permute-start.24 = (f32[120,256]{1,0:T(8,128)S(1)}, f32[120,256]{1,0:T(8,128)S(1)}, u32[]{:S(2)}, u32[]{:S(2)}) collective-permute-start(f32[120,256]{1,0:T(8,128)S(1)} %collective-permute-done.20.refs_2_), channel_id=1, source_target_pairs={{0,1},{1,0},{2,3},{3,2},{4,5},{5,4},{6,7},{7,6},{8,9},{9,8},{10,11... | collective-permute-start | bytes 368648 | tf_op jit(solution)/shard_map/ppermute | solution.py:377
  78.9 1.1 %collective-permute-done.19.refs_1_ = f32[120,256]{1,0:T(8,128)S(1)} collective-permute-done((f32[120,256]{1,0:T(8,128)S(1)}, f32[120,256]{1,0:T(8,128)S(1)}, u32[]{:S(2)}, u32[]{:S(2)}) %collective-permute-start.19) | collective-permute-done | bytes 122912 | tf_op jit(solution)/shard_map/ppermute | solution.py:361
  80.0 0.6 collective-permute-start.23
  80.5 0.0 collective-permute-done.22.refs_4_
  80.5 0.0 collective-permute-done.25.refs_7_
  80.5 1.0 %collective-permute-done.23.refs_5_ = f32[120,256]{1,0:T(8,128)S(1)} collective-permute-done((f32[120,256]{1,0:T(8,128)S(1)}, f32[120,256]{1,0:T(8,128)S(1)}, u32[]{:S(2)}, u32[]{:S(2)}) %collective-permute-start.23) | collective-permute-done | bytes 122912 | tf_op jit(solution)/shard_map/ppermute | solution.py:377
  81.5 1.7 %store.1 = f32[8,28800]{1,0:T(8,128)} custom-call(f32[120,256]{1,0:T(8,128)S(1)} %sum_up.1.refs_0_, f32[120,256]{1,0:T(8,128)S(1)} %collective-permute-done.19.refs_1_, f32[120,256]{1,0:T(8,128)S(1)} %collective-permute-done.20.refs_2_, f32[120,256]{1,0:T(8,128)S(1)} %collective-permute-done.21.refs_3_, f32[120,256]{1,0:T(8,128)S(1)} %collective-permute-done.22.refs_4_, ...), custom_call_target="tpu_custom_call" | custom-call | tf_op jit(solution)/shard_map/store/pallas_call | solution.py:343
  (8 shorter events, 0.0 us)
Async XLA Ops:
  0.0 1.2 %copy-start = (f32[8,28800]{1,0:T(8,128)S(1)}, f32[8,28800]{1,0:T(8,128)}, u32[]{:S(2)}) copy-start(f32[8,28800]{1,0:T(8,128)} %flat_ref.2) | copy-start | bytes 2764804
  1.2 0.7 copy-start.2
  1.9 0.7 copy-start.3
  2.5 26.9 %copy-start.1 = (f32[8,28800]{1,0:T(8,128)S(1)}, f32[8,28800]{1,0:T(8,128)}, u32[]{:S(2)}) copy-start(f32[8,28800]{1,0:T(8,128)} %flat_ref.3) | copy-start | bytes 2764804
  6.3 11.3 %collective-permute-start = (f32[120,256]{1,0:T(8,128)S(1)}, f32[120,256]{1,0:T(8,128)S(1)}, u32[]{:S(2)}, u32[]{:S(2)}) collective-permute-start(f32[120,256]{1,0:T(8,128)S(1)} %get-tuple-element.32), channel_id=1, source_target_pairs={{0,48},{8,56},{16,32},{24,40},{32,16},{40,24},{48,0},{56,8},{1,49}... | collective-permute-start | bytes 368648 | tf_op jit(solution)/shard_map/ppermute | solution.py:358
  11.3 6.9 %collective-permute-start.1 = (f32[120,256]{1,0:T(8,128)S(1)}, f32[120,256]{1,0:T(8,128)S(1)}, u32[]{:S(2)}, u32[]{:S(2)}) collective-permute-start(f32[120,256]{1,0:T(8,128)S(1)} %get-tuple-element.33), channel_id=1, source_target_pairs={{0,16},{8,24},{16,0},{24,8},{32,48},{40,56},{48,32},{56,40},{1,17}... | collective-permute-start | bytes 368648 | tf_op jit(solution)/shard_map/ppermute | solution.py:358
  11.6 9.9 %collective-permute-start.2 = (f32[120,256]{1,0:T(8,128)S(1)}, f32[120,256]{1,0:T(8,128)S(1)}, u32[]{:S(2)}, u32[]{:S(2)}) collective-permute-start(f32[120,256]{1,0:T(8,128)S(1)} %get-tuple-element.34), channel_id=1, source_target_pairs={{0,56},{8,48},{16,40},{24,32},{32,24},{40,16},{48,8},{56,0},{1,57}... | collective-permute-start | bytes 368648 | tf_op jit(solution)/shard_map/ppermute | solution.py:358
  13.6 7.9 %collective-permute-start.3 = (f32[120,256]{1,0:T(8,128)S(1)}, f32[120,256]{1,0:T(8,128)S(1)}, u32[]{:S(2)}, u32[]{:S(2)}) collective-permute-start(f32[120,256]{1,0:T(8,128)S(1)} %get-tuple-element.35), channel_id=1, source_target_pairs={{0,40},{8,32},{16,56},{24,48},{32,8},{40,0},{48,24},{56,16},{1,41}... | collective-permute-start | bytes 368648 | tf_op jit(solution)/shard_map/ppermute | solution.py:358
  17.1 8.0 %collective-permute-start.4 = (f32[120,256]{1,0:T(8,128)S(1)}, f32[120,256]{1,0:T(8,128)S(1)}, u32[]{:S(2)}, u32[]{:S(2)}) collective-permute-start(f32[120,256]{1,0:T(8,128)S(1)} %get-tuple-element.39), channel_id=1, source_target_pairs={{0,32},{8,40},{16,48},{24,56},{32,0},{40,8},{48,16},{56,24},{1,33}... | collective-permute-start | bytes 368648 | tf_op jit(solution)/shard_map/ppermute | solution.py:358
  17.6 7.5 %collective-permute-start.5 = (f32[120,256]{1,0:T(8,128)S(1)}, f32[120,256]{1,0:T(8,128)S(1)}, u32[]{:S(2)}, u32[]{:S(2)}) collective-permute-start(f32[120,256]{1,0:T(8,128)S(1)} %get-tuple-element.40), channel_id=1, source_target_pairs={{0,24},{8,16},{16,8},{24,0},{32,56},{40,48},{48,40},{56,32},{1,25}... | collective-permute-start | bytes 368648 | tf_op jit(solution)/shard_map/ppermute | solution.py:358
  18.2 6.9 %collective-permute-start.6 = (f32[120,256]{1,0:T(8,128)S(1)}, f32[120,256]{1,0:T(8,128)S(1)}, u32[]{:S(2)}, u32[]{:S(2)}) collective-permute-start(f32[120,256]{1,0:T(8,128)S(1)} %get-tuple-element.41), channel_id=1, source_target_pairs={{0,8},{8,0},{16,24},{24,16},{32,40},{40,32},{48,56},{56,48},{1,9},... | collective-permute-start | bytes 368648 | tf_op jit(solution)/shard_map/ppermute | solution.py:358
  26.0 6.7 %collective-permute-start.7 = (f32[120,256]{1,0:T(8,128)S(1)}, f32[120,256]{1,0:T(8,128)S(1)}, u32[]{:S(2)}, u32[]{:S(2)}) collective-permute-start(f32[120,256]{1,0:T(8,128)S(1)} %get-tuple-element.46.h_ref), channel_id=1, source_target_pairs={{0,96},{32,64},{64,32},{96,0},{1,97},{33,65},{65,33},{97,1},{2,98}... | collective-permute-start | bytes 368648 | tf_op jit(solution)/shard_map/ppermute | solution.py:367
  34.3 6.3 %collective-permute-start.11 = (f32[120,256]{1,0:T(8,128)S(1)}, f32[120,256]{1,0:T(8,128)S(1)}, u32[]{:S(2)}, u32[]{:S(2)}) collective-permute-start(f32[120,256]{1,0:T(8,128)S(1)} %get-tuple-element.53), channel_id=1, source_target_pairs={{0,48},{8,56},{16,32},{24,40},{32,16},{40,24},{48,0},{56,8},{1,49}... | collective-permute-start | bytes 368648 | tf_op jit(solution)/shard_map/ppermute | solution.py:358
  35.0 7.4 %collective-permute-start.12 = (f32[120,256]{1,0:T(8,128)S(1)}, f32[120,256]{1,0:T(8,128)S(1)}, u32[]{:S(2)}, u32[]{:S(2)}) collective-permute-start(f32[120,256]{1,0:T(8,128)S(1)} %get-tuple-element.54), channel_id=1, source_target_pairs={{0,16},{8,24},{16,0},{24,8},{32,48},{40,56},{48,32},{56,40},{1,17}... | collective-permute-start | bytes 368648 | tf_op jit(solution)/shard_map/ppermute | solution.py:358
  36.7 14.9 %collective-permute-start.8 = (f32[120,256]{1,0:T(8,128)S(1)}, f32[120,256]{1,0:T(8,128)S(1)}, u32[]{:S(2)}, u32[]{:S(2)}) collective-permute-start(f32[120,256]{1,0:T(8,128)S(1)} %get-tuple-element.47), channel_id=1, source_target_pairs={{0,32},{8,40},{16,48},{24,56},{32,0},{40,8},{48,16},{56,24},{1,33}... | collective-permute-start | bytes 368648 | tf_op jit(solution)/shard_map/ppermute | solution.py:358
  38.5 8.8 %collective-permute-start.13 = (f32[120,256]{1,0:T(8,128)S(1)}, f32[120,256]{1,0:T(8,128)S(1)}, u32[]{:S(2)}, u32[]{:S(2)}) collective-permute-start(f32[120,256]{1,0:T(8,128)S(1)} %get-tuple-element.55), channel_id=1, source_target_pairs={{0,56},{8,48},{16,40},{24,32},{32,24},{40,16},{48,8},{56,0},{1,57}... | collective-permute-start | bytes 368648 | tf_op jit(solution)/shard_map/ppermute | solution.py:358
  39.0 8.4 %collective-permute-start.14 = (f32[120,256]{1,0:T(8,128)S(1)}, f32[120,256]{1,0:T(8,128)S(1)}, u32[]{:S(2)}, u32[]{:S(2)}) collective-permute-start(f32[120,256]{1,0:T(8,128)S(1)} %get-tuple-element.56), channel_id=1, source_target_pairs={{0,40},{8,32},{16,56},{24,48},{32,8},{40,0},{48,24},{56,16},{1,41}... | collective-permute-start | bytes 368648 | tf_op jit(solution)/shard_map/ppermute | solution.py:358
  40.6 11.0 %collective-permute-start.9 = (f32[120,256]{1,0:T(8,128)S(1)}, f32[120,256]{1,0:T(8,128)S(1)}, u32[]{:S(2)}, u32[]{:S(2)}) collective-permute-start(f32[120,256]{1,0:T(8,128)S(1)} %get-tuple-element.48), channel_id=1, source_target_pairs={{0,24},{8,16},{16,8},{24,0},{32,56},{40,48},{48,40},{56,32},{1,25}... | collective-permute-start | bytes 368648 | tf_op jit(solution)/shard_map/ppermute | solution.py:358
  42.4 9.2 %collective-permute-start.10 = (f32[120,256]{1,0:T(8,128)S(1)}, f32[120,256]{1,0:T(8,128)S(1)}, u32[]{:S(2)}, u32[]{:S(2)}) collective-permute-start(f32[120,256]{1,0:T(8,128)S(1)} %get-tuple-element.49), channel_id=1, source_target_pairs={{0,8},{8,0},{16,24},{24,16},{32,40},{40,32},{48,56},{56,48},{1,9},... | collective-permute-start | bytes 368648 | tf_op jit(solution)/shard_map/ppermute | solution.py:358
  53.9 4.2 %collective-permute-start.15 = (f32[4,120,256]{2,1,0:T(8,128)S(1)}, f32[4,120,256]{2,1,0:T(8,128)S(1)}, u32[]{:S(2)}, u32[]{:S(2)}) collective-permute-start(f32[4,120,256]{2,1,0:T(8,128)S(1)} %down_theirs.1), channel_id=1, source_target_pairs={{0,1},{1,0},{2,3},{3,2},{4,5},{5,4},{6,7},{7,6},{8,9},{9,8},{10,11... | collective-permute-start | bytes 1474568 | tf_op jit(solution)/shard_map/ppermute | solution.py:372
  58.2 7.8 %collective-permute-start.18 = (f32[120,256]{1,0:T(8,128)S(1)}, f32[120,256]{1,0:T(8,128)S(1)}, u32[]{:S(2)}, u32[]{:S(2)}) collective-permute-start(f32[120,256]{1,0:T(8,128)S(1)} %get-tuple-element.59), channel_id=1, source_target_pairs={{0,6},{2,0},{4,2},{6,4},{1,7},{3,1},{5,3},{7,5},{8,14},{10,8},{12,... | collective-permute-start | bytes 368648 | tf_op jit(solution)/shard_map/ppermute | solution.py:361
  61.0 5.9 %collective-permute-start.17 = (f32[120,256]{1,0:T(8,128)S(1)}, f32[120,256]{1,0:T(8,128)S(1)}, u32[]{:S(2)}, u32[]{:S(2)}) collective-permute-start(f32[120,256]{1,0:T(8,128)S(1)} %get-tuple-element.60), channel_id=1, source_target_pairs={{0,4},{2,6},{4,0},{6,2},{1,5},{3,7},{5,1},{7,3},{8,12},{10,14},{12... | collective-permute-start | bytes 368648 | tf_op jit(solution)/shard_map/ppermute | solution.py:361
  61.3 9.0 %collective-permute-start.16 = (f32[120,256]{1,0:T(8,128)S(1)}, f32[120,256]{1,0:T(8,128)S(1)}, u32[]{:S(2)}, u32[]{:S(2)}) collective-permute-start(f32[120,256]{1,0:T(8,128)S(1)} %get-tuple-element.61), channel_id=1, source_target_pairs={{0,2},{2,4},{4,6},{6,0},{1,3},{3,5},{5,7},{7,1},{8,10},{10,12},{12... | collective-permute-start | bytes 368648 | tf_op jit(solution)/shard_map/ppermute | solution.py:361
  70.5 4.5 %collective-permute-start.21 = (f32[120,256]{1,0:T(8,128)S(1)}, f32[120,256]{1,0:T(8,128)S(1)}, u32[]{:S(2)}, u32[]{:S(2)}) collective-permute-start(f32[120,256]{1,0:T(8,128)S(1)} %sum_up.1.refs_0_), channel_id=1, source_target_pairs={{0,6},{2,0},{4,2},{6,4},{1,7},{3,1},{5,3},{7,5},{8,14},{10,8},{12,... | collective-permute-start | bytes 368648 | tf_op jit(solution)/shard_map/ppermute | solution.py:361
  70.6 6.7 %collective-permute-start.20 = (f32[120,256]{1,0:T(8,128)S(1)}, f32[120,256]{1,0:T(8,128)S(1)}, u32[]{:S(2)}, u32[]{:S(2)}) collective-permute-start(f32[120,256]{1,0:T(8,128)S(1)} %sum_up.1.refs_0_), channel_id=1, source_target_pairs={{0,4},{2,6},{4,0},{6,2},{1,5},{3,7},{5,1},{7,3},{8,12},{10,14},{12... | collective-permute-start | bytes 368648 | tf_op jit(solution)/shard_map/ppermute | solution.py:361
  70.7 9.3 %collective-permute-start.19 = (f32[120,256]{1,0:T(8,128)S(1)}, f32[120,256]{1,0:T(8,128)S(1)}, u32[]{:S(2)}, u32[]{:S(2)}) collective-permute-start(f32[120,256]{1,0:T(8,128)S(1)} %sum_up.1.refs_0_), channel_id=1, source_target_pairs={{0,2},{2,4},{4,6},{6,0},{1,3},{3,5},{5,7},{7,1},{8,10},{10,12},{12... | collective-permute-start | bytes 368648 | tf_op jit(solution)/shard_map/ppermute | solution.py:361
  72.0 8.5 %collective-permute-start.22 = (f32[120,256]{1,0:T(8,128)S(1)}, f32[120,256]{1,0:T(8,128)S(1)}, u32[]{:S(2)}, u32[]{:S(2)}) collective-permute-start(f32[120,256]{1,0:T(8,128)S(1)} %sum_up.1.refs_0_), channel_id=1, source_target_pairs={{0,1},{1,0},{2,3},{3,2},{4,5},{5,4},{6,7},{7,6},{8,9},{9,8},{10,11... | collective-permute-start | bytes 368648 | tf_op jit(solution)/shard_map/ppermute | solution.py:377
  75.0 5.6 %collective-permute-start.25 = (f32[120,256]{1,0:T(8,128)S(1)}, f32[120,256]{1,0:T(8,128)S(1)}, u32[]{:S(2)}, u32[]{:S(2)}) collective-permute-start(f32[120,256]{1,0:T(8,128)S(1)} %collective-permute-done.21.refs_3_), channel_id=1, source_target_pairs={{0,1},{1,0},{2,3},{3,2},{4,5},{5,4},{6,7},{7,6},{8,9},{9,8},{10,11... | collective-permute-start | bytes 368648 | tf_op jit(solution)/shard_map/ppermute | solution.py:377
  77.2 3.3 %collective-permute-start.24 = (f32[120,256]{1,0:T(8,128)S(1)}, f32[120,256]{1,0:T(8,128)S(1)}, u32[]{:S(2)}, u32[]{:S(2)}) collective-permute-start(f32[120,256]{1,0:T(8,128)S(1)} %collective-permute-done.20.refs_2_), channel_id=1, source_target_pairs={{0,1},{1,0},{2,3},{3,2},{4,5},{5,4},{6,7},{7,6},{8,9},{9,8},{10,11... | collective-permute-start | bytes 368648 | tf_op jit(solution)/shard_map/ppermute | solution.py:377
  80.0 1.6 %collective-permute-start.23 = (f32[120,256]{1,0:T(8,128)S(1)}, f32[120,256]{1,0:T(8,128)S(1)}, u32[]{:S(2)}, u32[]{:S(2)}) collective-permute-start(f32[120,256]{1,0:T(8,128)S(1)} %collective-permute-done.19.refs_1_), channel_id=1, source_target_pairs={{0,1},{1,0},{2,3},{3,2},{4,5},{5,4},{6,7},{7,6},{8,9},{9,8},{10,11... | collective-permute-start | bytes 368648 | tf_op jit(solution)/shard_map/ppermute | solution.py:377

commit v3 on v2

v3 whole, which is shorter than its diff:
```python
import functools

import jax
import jax.numpy as jnp
from jax import lax
from jax.experimental import pallas as pl
from jax.experimental.pallas import tpu as pltpu
from jax.sharding import Mesh, PartitionSpec as P

M = 120
W = 2 * M
L = 128
ND = 8
F32, BF16 = jnp.float32, jnp.bfloat16
PARAMS = pltpu.CompilerParams(vmem_limit_bytes=20 * 1024 * 1024)
VMEM = pl.BlockSpec(memory_space=pltpu.VMEM)
SMEM = pl.BlockSpec(memory_space=pltpu.SMEM)
HBM = pl.BlockSpec(memory_space=pltpu.HBM)

OFFSETS = (6, 2, 7, 5, 4, 3, 1, 0)
UP_GROUPS = ((0, 1, 2), (3, 4, 5, 6, 7))
DOWN_GROUPS = ((7, 0, 1), (2, 3, 4, 5, 6))
NODES = 2 * len(UP_GROUPS)
ROWS = ((0, 32), (32, 64), (64, 96), (96, 120))


def single(*dims):
    return jax.ShapeDtypeStruct(dims, F32)


def halves(*dims):
    return jax.ShapeDtypeStruct((*dims, 2, L, 2 * L), BF16)


def split(x):
    high = x.astype(BF16)
    return high, (x - high.astype(F32)).astype(BF16)


def right_form(x):
    real, imag = x[:, :L], x[:, L:]
    return jnp.concatenate([x, jnp.concatenate([-imag, real], axis=1)], axis=0)


def product(left, right):
    (left_high, left_low), (right_high, right_low) = left, right
    right_high, right_low = right_form(right_high), right_form(right_low)
    return jnp.dot(
        jnp.concatenate([left_high, left_low, left_high], axis=1),
        jnp.concatenate([right_high, right_high, right_low], axis=0),
        preferred_element_type=F32,
    )


def load(ref, *at):
    return ref[(*at, 0)], ref[(*at, 1)]


def keep(ref, x, *at):
    ref[(*at, 0)], ref[(*at, 1)] = split(x)


def scaled(x, cosine, sine):
    real, imag = x[:, :L], x[:, L:]
    return jnp.concatenate([cosine * real - sine * imag, cosine * imag + sine * real], axis=1)


def adjoint(x):
    return jnp.concatenate([x[:, :L].T, -x[:, L:].T], axis=1)


def padded(x):
    return jnp.concatenate([x, jnp.zeros((L - M, 2 * L), F32)], axis=0)


def start_rows(flat_ref, buffer_ref, sems):
    copies = []
    for i, (a, b) in enumerate(ROWS):
        at = (slice(None), pl.ds(a * W, (b - a) * W))
        copies.append(pltpu.make_async_copy(flat_ref.at[at], buffer_ref.at[at], sems.at[i]))
        copies[-1].start()
    return copies


def unpack_rows(copies, buffer_ref, out_ref):
    zeros = jnp.zeros((ND, L - M), F32)
    for (a, b), copy in zip(ROWS, copies):
        copy.wait()
        for m in range(a, b):
            rows = pl.ds(m, ND, stride=L)
            real = buffer_ref[:, m * W : m * W + M]
            imag = buffer_ref[:, m * W + M : (m + 1) * W]
            out_ref[0, rows, :] = jnp.concatenate([real, zeros], axis=1)
            out_ref[1, rows, :] = jnp.concatenate([imag, zeros], axis=1)
    for k in range(ND):
        out_ref[:, k * L + M : (k + 1) * L, :] = jnp.zeros((2, L - M, L), F32)


def unpacked(rows_ref, start):
    return jnp.concatenate([rows_ref[0, pl.ds(start, L), :], rows_ref[1, pl.ds(start, L), :]], axis=1)


ROW_SCRATCH = [pltpu.VMEM((ND, M * W), F32), pltpu.SemaphoreType.DMA((len(ROWS),))]


def number():
    return lax.axis_index("zl") * 4 + lax.axis_index("x")


def owned():
    return number() ^ (lax.axis_index("zh") * 4)


def scalings(tab_ref, tabt_ref):
    def columns(x, k, f):
        i = f * ND + k
        return scaled(x, tab_ref[0, i : i + 1, :], tab_ref[1, i : i + 1, :])

    def rows(x, k, f):
        i = f * ND + k
        return scaled(x, tabt_ref[0, :, i : i + 1], tabt_ref[1, :, i : i + 1])

    return columns, rows


def up_group(group, a_refs, c_ref, ch_ref, tab_ref, tabt_ref, p_ref, q_ref, lhs_ref):
    columns, rows = scalings(tab_ref, tabt_ref)
    count = len(group)
    for j in range(4):
        low, up = 2 * j, 2 * j + 1
        c_up = unpacked(c_ref, up * L)
        for i, f in enumerate(group):
            at = slice(i * L, (i + 1) * L)
            lhs_ref[j, 0, at], lhs_ref[j, 1, at] = split(columns(c_up, low, f))
        res = product(load(lhs_ref, j), load(ch_ref, low))
        for i, f in enumerate(group):
            one = res[i * L : (i + 1) * L]
            keep(p_ref, rows(one, up, f) if j % 2 == 0 else one, j, i)
    for i, f in enumerate(group):
        keep(q_ref, rows(product(load(p_ref, 1, i), load(p_ref, 0, i)), 3, f), 0, i)
    for i, f in enumerate(group):
        keep(q_ref, product(load(p_ref, 3, i), load(p_ref, 2, i)), 1, i)
    for i, f in enumerate(group):
        a_refs[i][...] = rows(product(load(q_ref, 1, i), load(q_ref, 0, i)), 7, f)[:M]


def up_kernel(group, freq_hbm, prop_hbm, flat_hbm, c_ref, ch_ref, tab_ref, tabt_ref, p_ref, q_ref, *refs):
    count = len(group)
    a_refs, (lhs_ref, freq_ref, prop_ref, small, buffer_ref, sems) = refs[:count], refs[count:]
    first = pltpu.make_async_copy(freq_hbm, freq_ref, small.at[0])
    second = pltpu.make_async_copy(prop_hbm, prop_ref, small.at[1])
    first.start()
    second.start()
    copies = start_rows(flat_hbm, buffer_ref, sems)
    tab_ref[...] = jnp.zeros(tab_ref.shape, F32)
    first.wait()
    second.wait()
    for f in range(ND):
        phase = prop_ref[...] * freq_ref[owned() ^ OFFSETS[f]]
        tab_ref[0, f * ND : (f + 1) * ND, 0:M] = jnp.cos(phase)
        tab_ref[1, f * ND : (f + 1) * ND, 0:M] = jnp.sin(phase)
    tabt_ref[0] = tab_ref[0].T
    tabt_ref[1] = tab_ref[1].T
    unpack_rows(copies, buffer_ref, c_ref)
    for k in range(ND):
        keep(ch_ref, unpacked(c_ref, k * L), k)
    up_group(group, a_refs, c_ref, ch_ref, tab_ref, tabt_ref, p_ref, q_ref, lhs_ref)


def up_second_kernel(group, c_ref, ch_ref, tab_ref, tabt_ref, p_ref, q_ref, *refs):
    a_refs, (lhs_ref,) = refs[: len(group)], refs[len(group) :]
    up_group(group, a_refs, c_ref, ch_ref, tab_ref, tabt_ref, p_ref, q_ref, lhs_ref)


def up_outs(group):
    count = len(group)
    return (halves(4, count), halves(2, count)) + (single(M, 2 * L),) * count


def lhs_scratch(group):
    return pltpu.VMEM((4, 2, len(group) * L, 2 * L), BF16)


def in_hbm(x):
    return pltpu.with_memory_space_constraint(x, pltpu.HBM)


def up(group, freq, prop, flat):
    tables = (single(2, ND * L, L), halves(ND), single(2, ND * ND, L), single(2, L, ND * ND))
    outs = tables + up_outs(group)
    res = pl.pallas_call(
        functools.partial(up_kernel, group),
        out_shape=outs,
        in_specs=[HBM, HBM, HBM],
        out_specs=(VMEM,) * len(outs),
        scratch_shapes=[
            lhs_scratch(group),
            pltpu.SMEM((ND,), F32),
            pltpu.VMEM((ND, M), F32),
            pltpu.SemaphoreType.DMA((2,)),
            *ROW_SCRATCH,
        ],
        compiler_params=PARAMS,
        name="up",
    )(in_hbm(freq), in_hbm(prop), in_hbm(flat))
    return res[:4], res[4:6], res[6:]


def up_second(group, tables):
    outs = up_outs(group)
    res = pl.pallas_call(
        functools.partial(up_second_kernel, group),
        out_shape=outs,
        in_specs=[VMEM] * 4,
        out_specs=(VMEM,) * len(outs),
        scratch_shapes=[lhs_scratch(group)],
        compiler_params=PARAMS,
        name="up_second",
    )(*tables)
    return res[:2], res[2:]


def half_kernel(*refs):
    received, (h_ref, r_ref, p_ref, q_ref) = refs[:ND], refs[ND:]
    me = number()
    for i, offset in enumerate(OFFSETS):
        keep(r_ref, padded(received[i][...]), me ^ offset)
    for j in range(4):
        keep(p_ref, product(load(r_ref, 2 * j + 1), load(r_ref, 2 * j)), j)
    for j in range(2):
        keep(q_ref, product(load(p_ref, 2 * j + 1), load(p_ref, 2 * j)), j)
    h_ref[...] = product(load(q_ref, 1), load(q_ref, 0))[:M]


def half(received):
    return pl.pallas_call(
        half_kernel,
        out_shape=(single(M, 2 * L), halves(ND), halves(4), halves(2)),
        in_specs=[VMEM] * ND,
        out_specs=(VMEM,) * 4,
        compiler_params=PARAMS,
        name="half",
    )(*received)


def pick_kernel(flat_ref, m_ref, rows_ref, buffer_ref, sems):
    unpack_rows(start_rows(flat_ref, buffer_ref, sems), buffer_ref, rows_ref)
    m_ref[...] = unpacked(rows_ref, pl.multiple_of(owned() * L, L))


def pick(flat):
    return pl.pallas_call(
        pick_kernel,
        out_shape=single(L, 2 * L),
        in_specs=[HBM],
        out_specs=VMEM,
        scratch_shapes=[pltpu.VMEM((2, ND * L, L), F32), *ROW_SCRATCH],
        compiler_params=PARAMS,
        name="pick",
    )(in_hbm(flat))


def top_kernel(r_ref, m_ref, p_ref, q_ref, h_ref, other_ref, *refs):
    v_refs, leaf_ref = refs[:ND], refs[ND]
    upper = lax.axis_index("zh") == 1
    own, other = padded(h_ref[...]), padded(other_ref[...])
    h0 = split(jnp.where(upper, other, own))
    h1 = split(jnp.where(upper, own, other))
    misfit = split(adjoint(product(h1, h0) - m_ref[...]))
    left = [jnp.where(upper, a, b) for a, b in zip(h0, misfit)]
    right = [jnp.where(upper, a, b) for a, b in zip(misfit, h1)]
    v = split(product(left, right))
    v0, v1 = split(product(v, load(q_ref, 1))), split(product(load(q_ref, 0), v))
    pairs = (
        product(v0, load(p_ref, 1)),
        product(load(p_ref, 0), v0),
        product(v1, load(p_ref, 3)),
        product(load(p_ref, 2), v1),
    )
    for j in range(4):
        pair = split(pairs[j])
        leaf_ref[2 * j] = product(pair, load(r_ref, 2 * j + 1))[:M]
        leaf_ref[2 * j + 1] = product(load(r_ref, 2 * j), pair)[:M]
    me = number()
    for i, offset in enumerate(OFFSETS):
        v_refs[i][...] = leaf_ref[me ^ offset]


def top(r, m, p, q, h, other):
    return pl.pallas_call(
        top_kernel,
        out_shape=(single(M, 2 * L),) * ND,
        in_specs=[VMEM] * 6,
        out_specs=(VMEM,) * ND,
        scratch_shapes=[pltpu.VMEM((ND, M, 2 * L), F32)],
        compiler_params=PARAMS,
        name="top",
    )(r, m, p, q, h, other)


def quads_down(quads, group, v_refs, ch_ref, tab_ref, tabt_ref, nodes, v_ref, vq_ref, vp_ref):
    columns, rows = scalings(tab_ref, tabt_ref)
    count = len(group)
    place = {f: (n, i) for n, fs in enumerate(UP_GROUPS) for i, f in enumerate(fs)}

    def node(level, j, f):
        n, i = place[f]
        return load(nodes[2 * n + level], j, i)

    for i, f in enumerate(group):
        keep(v_ref, columns(padded(v_refs[i][...]), 7, f), i)
    for quad in quads:
        for i, f in enumerate(group):
            v = load(v_ref, i)
            if quad == 0:
                keep(vq_ref, columns(product(v, node(1, 1, f)), 3, f), 0, i)
            else:
                keep(vq_ref, product(node(1, 0, f), v), 1, i)
    for quad in quads:
        for i, f in enumerate(group):
            v = load(vq_ref, quad, i)
            at = slice(i * L, (i + 1) * L)
            res = columns(product(v, node(0, 2 * quad + 1, f)), 4 * quad + 1, f)
            vp_ref[2 * quad, 0, at], vp_ref[2 * quad, 1, at] = split(res)
            res = product(node(0, 2 * quad, f), v)
            vp_ref[2 * quad + 1, 0, at], vp_ref[2 * quad + 1, 1, at] = split(res)
    out = {}
    for quad in quads:
        for j in (2 * quad, 2 * quad + 1):
            low, up = 2 * j, 2 * j + 1
            res = product(load(vp_ref, j), load(ch_ref, up))
            g_low = g_up = None
            for i, f in enumerate(group):
                at = slice(i * L, (i + 1) * L)
                one = columns(res[at], low, f)
                g_low = one if i == 0 else g_low + one
                one = rows(product(load(ch_ref, low), (vp_ref[j, 0, at], vp_ref[j, 1, at])), low, f)
                g_up = one if i == 0 else g_up + one
            out[low], out[up] = g_low[:M], g_up[:M]
    return out


def down_whole_kernel(group, has_part, *refs):
    count = len(group)
    v_refs, (ch_ref, tab_ref, tabt_ref, *rest) = refs[:count], refs[count:]
    nodes, rest = rest[:NODES], rest[NODES:]
    part_ref = rest.pop(0) if has_part else None
    g_ref, *scratch = rest
    out = quads_down((0, 1), group, v_refs, ch_ref, tab_ref, tabt_ref, nodes, *scratch)
    for k in range(ND):
        g_ref[k] = out[k] + part_ref[k] if has_part else out[k]


def down_last_kernel(mine, group, *refs):
    count = len(group)
    v_refs, (ch_ref, tab_ref, tabt_ref, *rest) = refs[:count], refs[count:]
    nodes, (part_ref, g_ref, *scratch) = rest[:NODES], rest[NODES:]
    core, y = lax.axis_index("c"), lax.axis_index("y")
    for quad in range(2):

        @pl.when(core == (quad if mine else 1 - quad))
        def _():
            out = quads_down((quad,), group, v_refs, ch_ref, tab_ref, tabt_ref, nodes, *scratch)
            for i in range(4):
                g_ref[i ^ y] = out[4 * quad + i] + part_ref[4 * quad + i]


def down(kernel, name, sections, group, v, tables, nodes, *part):
    count = len(group)
    args = (*v, *tables[1:], *nodes, *part)
    return pl.pallas_call(
        kernel,
        out_shape=single(sections, M, 2 * L),
        in_specs=[VMEM] * len(args),
        out_specs=VMEM,
        scratch_shapes=[
            pltpu.VMEM((count, 2, L, 2 * L), BF16),
            pltpu.VMEM((2, count, 2, L, 2 * L), BF16),
            pltpu.VMEM((4, 2, count * L, 2 * L), BF16),
        ],
        compiler_params=PARAMS,
        name=name,
    )(*args)


def sum_kernel(own_ref, a_ref, b_ref, c_ref, out_ref):
    total = (own_ref[...] + a_ref[...]) + (b_ref[...] + c_ref[...])
    out_ref[...] = 2.0 * adjoint(padded(total))[:M]


def sum_up(own, a, b, c):
    return pl.pallas_call(
        sum_kernel,
        out_shape=single(M, 2 * L),
        in_specs=[VMEM] * 4,
        out_specs=VMEM,
        compiler_params=PARAMS,
        name="sum_up",
    )(own, a, b, c)


def store_kernel(*refs):
    parts, (out_ref, rows_ref, buffer_ref, sems) = refs[:ND], refs[ND:]
    core, y = lax.axis_index("c"), lax.axis_index("y")
    for i in range(ND):
        place = (4 * core if i < 4 else 4 * (1 - core)) + (y ^ (i % 4))
        at = pl.ds(pl.multiple_of(place * L, L), M)
        rows_ref[0, at, :] = parts[i][:, :L]
        rows_ref[1, at, :] = parts[i][:, L:]
    copies = []
    for i, (a, b) in enumerate(ROWS):
        for m in range(a, b):
            rows = pl.ds(m, ND, stride=L)
            buffer_ref[:, m * W : m * W + M] = rows_ref[0, rows, :][:, :M]
            buffer_ref[:, m * W + M : (m + 1) * W] = rows_ref[1, rows, :][:, :M]
        at = (slice(None), pl.ds(a * W, (b - a) * W))
        copies.append(pltpu.make_async_copy(buffer_ref.at[at], out_ref.at[at], sems.at[i]))
        copies[-1].start()
    for copy in copies:
        copy.wait()


def store(parts):
    return pl.pallas_call(
        store_kernel,
        out_shape=single(ND, M * W),
        in_specs=[VMEM] * ND,
        out_specs=HBM,
        scratch_shapes=[pltpu.VMEM((2, ND * L, L), F32), *ROW_SCRATCH],
        compiler_params=PARAMS,
        name="store",
    )(*parts)


def shards(coupling, propagation, frequency_offset, measured):
    swap = [(0, 1), (1, 0)]

    def exchange(i, x):
        return lax.ppermute(x, ("zl", "x"), [(s, s ^ OFFSETS[i]) for s in range(ND)]) if OFFSETS[i] else x

    def turned(i, x):
        return lax.ppermute(x, "y", [(s, s ^ i) for s in range(4)])

    tables, nodes_first, a_first = up(UP_GROUPS[0], frequency_offset, propagation, coupling)
    nodes_second, a_second = up_second(UP_GROUPS[1], tables)
    nodes, a = (*nodes_first, *nodes_second), (*a_first, *a_second)
    h, r, p, q = half([exchange(i, x) for i, x in enumerate(a)])
    other = lax.ppermute(h, ("zh", "zl"), [(0, 3), (1, 2), (2, 1), (3, 0)])
    v = top(r, pick(measured), p, q, h, other)
    v = [exchange(i, x) for i, x in enumerate(v)]

    one, two = DOWN_GROUPS
    part = down(functools.partial(down_whole_kernel, one, False), "down_1", ND, one, [v[i] for i in one], tables, nodes)
    last = [v[i] for i in two]
    theirs = down(functools.partial(down_last_kernel, False, two), "down_theirs", 4, two, last, tables, nodes, part)
    received = lax.ppermute(theirs, "c", swap)
    mine = down(functools.partial(down_last_kernel, True, two), "down_mine", 4, two, last, tables, nodes, part)

    g = mine + received
    total = sum_up(g[0], *[turned(i, g[i]) for i in range(1, 4)])
    parts = [total] + [turned(i, total) for i in range(1, 4)]
    parts += [lax.ppermute(x, "c", swap) for x in parts]
    return store(parts)


def solution(mesh):
    fine = Mesh(mesh.devices.reshape(2, 2, 4, 4, 2), ("zh", "zl", "x", "y", "c"))
    sec, freq = ("zh", "zl", "x"), ("y", "c")
    return jax.shard_map(
        shards,
        mesh=fine,
        in_specs=(P(sec, None), P(sec, None), P(freq), P(freq, None)),
        out_specs=P(sec, None),
        check_vma=False,
    )
```

time: 83.4 us -> 77.8 us (0.933)
  waiting for transfers between devices: 25.2 us -> 20 us
  starting transfers between devices: 35.3 us -> 38.1 us
  local copies, waits for them, and re-layouts: 2.56 us -> 0.03 us
    ppermute x20, waiting for transfers between devices: 21.9 us -> 17.4 us  [the longest x14 10.9 us: exchange(): lax.ppermute(x, ('zl', 'x'), [(s, s ^ OFFSETS[i]) for s in range(ND)])]
    unnamed x8 -> x0, local copies, waits for them, and re-layouts: 2.52 us -> none
    ppermute x20, starting transfers between devices: 24.4 us -> 26.1 us  [the longest x14 19.1 us: exchange(): lax.ppermute(x, ('zl', 'x'), [(s, s ^ OFFSETS[i]) for s in range(ND)])]
    ppermute x4, starting transfers between devices: 5.54 us -> 7.12 us  [shards(): parts += [lax.ppermute(x, 'c', swap) for x in parts]]
    ppermute x1, waiting for transfers between devices: 2.39 us -> 1.27 us  [shards(): other = lax.ppermute(h, ('zh', 'zl'), [(0, 3), (1, 2), (2, 1), (3, 0)])]
  transfers between devices with their start and end apart: 26 -> 26, of which waited for: 11 -> 12; matrix products, arithmetic and copies ran while one was open for 0% -> 0% of each run, Pallas kernels for 12% -> 12%
where the time goes in v3:
time: 77.8 us; the launch traced here: 77.7 us
  starting transfers between devices  38.1 us (49%)
  waiting for transfers between devices  20 us (26%)
  Pallas kernels  19.1 us (25%)
    ppermute x14, starting transfers between devices, exchange(): lax.ppermute(x, ('zl', 'x'), [(s, s ^ OFFSETS[i]) for s in range(ND)])  19.1 us
    ppermute x14, waiting for transfers between devices, exchange(): lax.ppermute(x, ('zl', 'x'), [(s, s ^ OFFSETS[i]) for s in range(ND)])  10.9 us
    ppermute x4, starting transfers between devices, shards(): parts += [lax.ppermute(x, 'c', swap) for x in parts]  7.12 us
    ppermute x6, starting transfers between devices, turned(): return lax.ppermute(x, 'y', [(s, s ^ i) for s in range(4)])  7.03 us
    pallas_call x3, Pallas kernels, down(): pl.pallas_call(kernel, out_shape=single(sections, M, 2 * L), in_specs=[VM...  6.86 us
    ppermute x6, waiting for transfers between devices, turned(): return lax.ppermute(x, 'y', [(s, s ^ i) for s in range(4)])  6.58 us
    pallas_call x1, Pallas kernels, up(): pl.pallas_call(functools.partial(up_kernel, group), out_shape=outs, in_sp...  3.9 us
    ppermute x1, starting transfers between devices, shards(): other = lax.ppermute(h, ('zh', 'zl'), [(0, 3), (1, 2), (2, 1), (3, 0)])  3.6 us
  transfers between devices with their start and end apart: 26, of which 12 were waited for; matrix products, arithmetic and copies ran while one was open for 0% of the time, Pallas kernels for 12%

profile of v3, /device:TPU:1, one launch (start us, length us, event | category | flops | bytes accessed | tf_op | source)
XLA Modules:
  0.0 77.7 jit_solution(10104609742470036517)
XLA Ops:
  0.0 3.9 %up.1 = (f32[2,1024,128]{2,1,0:T(8,128)S(1)}, bf16[8,2,128,256]{3,2,1,0:T(8,128)(2,1)S(1)}, f32[2,64,128]{2,1,0:T(8,128)S(1)}, f32[2,128,64]{2,1,0:T(8,128)S(1)}...) custom-call(f32[8]{0:T(128)} %freq_hbm.1, ...), custom_call_target="tpu_custom_call" | custom-call | tf_op jit(solution)/shard_map/up/pallas_call | solution.py:191
  3.9 5.0 %collective-permute-start = (f32[120,256]{1,0:T(8,128)S(1)}, f32[120,256]{1,0:T(8,128)S(1)}, u32[]{:S(2)}, u32[]{:S(2)}) collective-permute-start(f32[120,256]{1,0:T(8,128)S(1)} %get-tuple-element.33), channel_id=1, source_target_pairs={{0,48},{8,56},{16,32},{24,40},{32,16},{40,24},{48,0},{56,8},{1,49}... | collective-permute-start | bytes 368648 | tf_op jit(solution)/shard_map/ppermute | solution.py:439
  8.9 0.2 collective-permute-start.1
  9.1 2.0 %collective-permute-start.2 = (f32[120,256]{1,0:T(8,128)S(1)}, f32[120,256]{1,0:T(8,128)S(1)}, u32[]{:S(2)}, u32[]{:S(2)}) collective-permute-start(f32[120,256]{1,0:T(8,128)S(1)} %get-tuple-element.35), channel_id=1, source_target_pairs={{0,56},{8,48},{16,40},{24,32},{32,24},{40,16},{48,8},{56,0},{1,57}... | collective-permute-start | bytes 368648 | tf_op jit(solution)/shard_map/ppermute | solution.py:439
  11.2 2.3 %up_second.1 = (bf16[4,5,2,128,256]{4,3,2,1,0:T(8,128)(2,1)S(1)}, bf16[2,5,2,128,256]{4,3,2,1,0:T(8,128)(2,1)S(1)}, f32[120,256]{1,0:T(8,128)S(1)}, f32[120,256]...) custom-call(f32[2,1024,128]{2,1,0:T(8,128)S(1)} %get-tuple-element.36.c_ref, ...), custom_call_target="tpu_custom_call" | custom-call | tf_op jit(solution)/shard_map/up_second/pallas_call | solution.py:211
  13.5 1.4 %collective-permute-start.3 = (f32[120,256]{1,0:T(8,128)S(1)}, f32[120,256]{1,0:T(8,128)S(1)}, u32[]{:S(2)}, u32[]{:S(2)}) collective-permute-start(f32[120,256]{1,0:T(8,128)S(1)} %get-tuple-element.40), channel_id=1, source_target_pairs={{0,40},{8,32},{16,56},{24,48},{32,8},{40,0},{48,24},{56,16},{1,41}... | collective-permute-start | bytes 368648 | tf_op jit(solution)/shard_map/ppermute | solution.py:439
  14.9 0.4 collective-permute-start.4
  15.3 0.0 collective-permute-done.refs_0_
  15.3 0.5 collective-permute-start.5
  15.8 0.0 collective-permute-done.1.refs_1_
  15.8 0.7 collective-permute-start.6
  16.5 1.8 %collective-permute-done.2.refs_2_ = f32[120,256]{1,0:T(8,128)S(1)} collective-permute-done((f32[120,256]{1,0:T(8,128)S(1)}, f32[120,256]{1,0:T(8,128)S(1)}, u32[]{:S(2)}, u32[]{:S(2)}) %collective-permute-start.2) | collective-permute-done | bytes 122912 | tf_op jit(solution)/shard_map/ppermute | solution.py:439
  18.3 0.9 %collective-permute-done.3.refs_3_ = f32[120,256]{1,0:T(8,128)S(1)} collective-permute-done((f32[120,256]{1,0:T(8,128)S(1)}, f32[120,256]{1,0:T(8,128)S(1)}, u32[]{:S(2)}, u32[]{:S(2)}) %collective-permute-start.3) | collective-permute-done | bytes 122912 | tf_op jit(solution)/shard_map/ppermute | solution.py:439
  19.2 4.0 %collective-permute-done.4.refs_4_ = f32[120,256]{1,0:T(8,128)S(1)} collective-permute-done((f32[120,256]{1,0:T(8,128)S(1)}, f32[120,256]{1,0:T(8,128)S(1)}, u32[]{:S(2)}, u32[]{:S(2)}) %collective-permute-start.4) | collective-permute-done | bytes 122912 | tf_op jit(solution)/shard_map/ppermute | solution.py:439
  23.2 0.0 collective-permute-done.5.refs_5_
  23.2 0.0 collective-permute-done.6.refs_6_
  23.2 0.9 %half.1 = (f32[120,256]{1,0:T(8,128)S(1)}, bf16[8,2,128,256]{3,2,1,0:T(8,128)(2,1)S(1)}, bf16[4,2,128,256]{3,2,1,0:T(8,128)(2,1)S(1)}, bf16[2,2,128,256]{3,2,1,0:T(8,128)(2,1)S(1)}) custom-call(f32[120,256]{1,0:T(8,128)S(1)} %collective-permute-done.refs_0_, f32[120,256]{1,0:T(8,128)S(1)} %collective-permute-done.1.refs_1_, ...), custom_call_target="tpu_custom_call" | custom-call | tf_op jit(solution)/shard_map/half/pallas_call | solution.py:236
  24.2 3.6 %collective-permute-start.7 = (f32[120,256]{1,0:T(8,128)S(1)}, f32[120,256]{1,0:T(8,128)S(1)}, u32[]{:S(2)}, u32[]{:S(2)}) collective-permute-start(f32[120,256]{1,0:T(8,128)S(1)} %get-tuple-element.48.h_ref), channel_id=1, source_target_pairs={{0,96},{32,64},{64,32},{96,0},{1,97},{33,65},{65,33},{97,1},{2,98}... | collective-permute-start | bytes 368648 | tf_op jit(solution)/shard_map/ppermute | solution.py:448
  27.8 2.0 %pick.1.m_ref = f32[128,256]{1,0:T(8,128)S(1)} custom-call(f32[8,28800]{1,0:T(8,128)} %flat_ref.1), custom_call_target="tpu_custom_call" | custom-call | tf_op jit(solution)/shard_map/pick/pallas_call | solution.py:252
  29.7 1.3 %collective-permute-done.7.other_ref = f32[120,256]{1,0:T(8,128)S(1)} collective-permute-done((f32[120,256]{1,0:T(8,128)S(1)}, f32[120,256]{1,0:T(8,128)S(1)}, u32[]{:S(2)}, u32[]{:S(2)}) %collective-permute-start.7) | collective-permute-done | bytes 122912 | tf_op jit(solution)/shard_map/ppermute | solution.py:448
  31.0 1.6 %top.1 = (f32[120,256]{1,0:T(8,128)S(1)}, f32[120,256]{1,0:T(8,128)S(1)}, f32[120,256]{1,0:T(8,128)S(1)}, f32[120,256]{1,0:T(8,128)S(1)}, f32[120,256]{1,0:T(8,1...) custom-call(bf16[8,2,128,256]{3,2,1,0:T(8,128)(2,1)S(1)} %get-tuple-element.45.r_ref, ...), custom_call_target="tpu_custom_call" | custom-call | tf_op jit(solution)/shard_map/top/pallas_call | solution.py:290
  32.6 1.7 %collective-permute-start.13 = (f32[120,256]{1,0:T(8,128)S(1)}, f32[120,256]{1,0:T(8,128)S(1)}, u32[]{:S(2)}, u32[]{:S(2)}) collective-permute-start(f32[120,256]{1,0:T(8,128)S(1)} %get-tuple-element.59), channel_id=1, source_target_pairs={{0,48},{8,56},{16,32},{24,40},{32,16},{40,24},{48,0},{56,8},{1,49}... | collective-permute-start | bytes 368648 | tf_op jit(solution)/shard_map/ppermute | solution.py:439
  34.3 0.7 collective-permute-start.14
  35.0 2.5 %collective-permute-start.8 = (f32[120,256]{1,0:T(8,128)S(1)}, f32[120,256]{1,0:T(8,128)S(1)}, u32[]{:S(2)}, u32[]{:S(2)}) collective-permute-start(f32[120,256]{1,0:T(8,128)S(1)} %get-tuple-element.49), channel_id=1, source_target_pairs={{0,56},{8,48},{16,40},{24,32},{32,24},{40,16},{48,8},{56,0},{1,57}... | collective-permute-start | bytes 368648 | tf_op jit(solution)/shard_map/ppermute | solution.py:439
  37.5 0.4 collective-permute-start.9
  37.9 1.4 %collective-permute-start.10 = (f32[120,256]{1,0:T(8,128)S(1)}, f32[120,256]{1,0:T(8,128)S(1)}, u32[]{:S(2)}, u32[]{:S(2)}) collective-permute-start(f32[120,256]{1,0:T(8,128)S(1)} %get-tuple-element.51), channel_id=1, source_target_pairs={{0,32},{8,40},{16,48},{24,56},{32,0},{40,8},{48,16},{56,24},{1,33}... | collective-permute-start | bytes 368648 | tf_op jit(solution)/shard_map/ppermute | solution.py:439
  39.3 0.0 collective-permute-done.13.refs_1_
  39.3 1.8 %collective-permute-start.11 = (f32[120,256]{1,0:T(8,128)S(1)}, f32[120,256]{1,0:T(8,128)S(1)}, u32[]{:S(2)}, u32[]{:S(2)}) collective-permute-start(f32[120,256]{1,0:T(8,128)S(1)} %get-tuple-element.52), channel_id=1, source_target_pairs={{0,24},{8,16},{16,8},{24,0},{32,56},{40,48},{48,40},{56,32},{1,25}... | collective-permute-start | bytes 368648 | tf_op jit(solution)/shard_map/ppermute | solution.py:439
  41.0 0.0 collective-permute-done.14.refs_2_
  41.0 0.4 collective-permute-start.12
  41.4 2.6 %down_1.1.refs_12_ = f32[8,120,256]{2,1,0:T(8,128)S(1)} custom-call(f32[120,256]{1,0:T(8,128)S(1)} %get-tuple-element.58.refs_0_, f32[120,256]{1,0:T(8,128)S(1)} %collective-permute-done.13.refs_1_, f32[120,256]{1,0:T(8,128)S(1)} %collective-permute-done.14.refs_2_, bf16[8,2,128,256]{3,2,1,0:T(8,128)(2,1)S(1)} %get-tuple-element.37.ch_ref.refs_3_.refs_5_, ...), custom_call_target="tpu_custom_call" | custom-call | tf_op jit(solution)/shard_map/down_1/pallas_call | solution.py:371
  44.0 2.7 %collective-permute-done.8.refs_0_ = f32[120,256]{1,0:T(8,128)S(1)} collective-permute-done((f32[120,256]{1,0:T(8,128)S(1)}, f32[120,256]{1,0:T(8,128)S(1)}, u32[]{:S(2)}, u32[]{:S(2)}) %collective-permute-start.8) | collective-permute-done | bytes 122912 | tf_op jit(solution)/shard_map/ppermute | solution.py:439
  46.8 0.0 collective-permute-done.9.refs_1_
  46.8 1.3 %collective-permute-done.10.refs_2_ = f32[120,256]{1,0:T(8,128)S(1)} collective-permute-done((f32[120,256]{1,0:T(8,128)S(1)}, f32[120,256]{1,0:T(8,128)S(1)}, u32[]{:S(2)}, u32[]{:S(2)}) %collective-permute-start.10) | collective-permute-done | bytes 122912 | tf_op jit(solution)/shard_map/ppermute | solution.py:439
  48.1 0.0 collective-permute-done.11.refs_3_
  48.1 0.0 collective-permute-done.12.refs_4_
  48.1 2.1 %down_theirs.1 = f32[4,120,256]{2,1,0:T(8,128)S(1)} custom-call(f32[120,256]{1,0:T(8,128)S(1)} %collective-permute-done.8.refs_0_, f32[120,256]{1,0:T(8,128)S(1)} %collective-permute-done.9.refs_1_, f32[120,256]{1,0:T(8,128)S(1)} %collective-permute-done.10.refs_2_, f32[120,256]{1,0:T(8,128)S(1)} %collective-permute-done.11.refs_3_, ...), custom_call_target="tpu_custom_call" | custom-call | tf_op jit(solution)/shard_map/down_theirs/pallas_call | solution.py:371
  50.3 1.3 %collective-permute-start.15 = (f32[4,120,256]{2,1,0:T(8,128)S(1)}, f32[4,120,256]{2,1,0:T(8,128)S(1)}, u32[]{:S(2)}, u32[]{:S(2)}) collective-permute-start(f32[4,120,256]{2,1,0:T(8,128)S(1)} %down_theirs.1), channel_id=1, source_target_pairs={{0,1},{1,0},{2,3},{3,2},{4,5},{5,4},{6,7},{7,6},{8,9},{9,8},{10,11... | collective-permute-start | bytes 1474568 | tf_op jit(solution)/shard_map/ppermute | solution.py:456
  51.6 2.1 %down_mine.1 = f32[4,120,256]{2,1,0:T(8,128)S(1)} custom-call(f32[120,256]{1,0:T(8,128)S(1)} %collective-permute-done.8.refs_0_, f32[120,256]{1,0:T(8,128)S(1)} %collective-permute-done.9.refs_1_, f32[120,256]{1,0:T(8,128)S(1)} %collective-permute-done.10.refs_2_, f32[120,256]{1,0:T(8,128)S(1)} %collective-permute-done.11.refs_3_, ...), custom_call_target="tpu_custom_call" | custom-call | tf_op jit(solution)/shard_map/down_mine/pallas_call | solution.py:371
  53.7 0.0 collective-permute-done.15
  53.7 0.1 add.3
  53.9 2.8 %collective-permute-start.18 = (f32[120,256]{1,0:T(8,128)S(1)}, f32[120,256]{1,0:T(8,128)S(1)}, u32[]{:S(2)}, u32[]{:S(2)}) collective-permute-start(f32[120,256]{1,0:T(8,128)S(1)} %get-tuple-element.61), channel_id=1, source_target_pairs={{0,6},{2,4},{4,2},{6,0},{1,7},{3,5},{5,3},{7,1},{8,14},{10,12},{12... | collective-permute-start | bytes 368648 | tf_op jit(solution)/shard_map/ppermute | solution.py:442
  56.7 0.4 collective-permute-start.17
  57.0 0.3 collective-permute-start.16
  57.3 4.5 %collective-permute-done.18.c_ref = f32[120,256]{1,0:T(8,128)S(1)} collective-permute-done((f32[120,256]{1,0:T(8,128)S(1)}, f32[120,256]{1,0:T(8,128)S(1)}, u32[]{:S(2)}, u32[]{:S(2)}) %collective-permute-start.18) | collective-permute-done | bytes 122912 | tf_op jit(solution)/shard_map/ppermute | solution.py:442
  61.9 0.9 %collective-permute-done.17.b_ref = f32[120,256]{1,0:T(8,128)S(1)} collective-permute-done((f32[120,256]{1,0:T(8,128)S(1)}, f32[120,256]{1,0:T(8,128)S(1)}, u32[]{:S(2)}, u32[]{:S(2)}) %collective-permute-start.17) | collective-permute-done | bytes 122912 | tf_op jit(solution)/shard_map/ppermute | solution.py:442
  62.8 0.5 collective-permute-done.16.a_ref
  63.3 0.1 sum_up.1.refs_0_
  63.4 2.7 %collective-permute-start.21 = (f32[120,256]{1,0:T(8,128)S(1)}, f32[120,256]{1,0:T(8,128)S(1)}, u32[]{:S(2)}, u32[]{:S(2)}) collective-permute-start(f32[120,256]{1,0:T(8,128)S(1)} %sum_up.1.refs_0_), channel_id=1, source_target_pairs={{0,6},{2,4},{4,2},{6,0},{1,7},{3,5},{5,3},{7,1},{8,14},{10,12},{12... | collective-permute-start | bytes 368648 | tf_op jit(solution)/shard_map/ppermute | solution.py:442
  66.1 0.4 collective-permute-start.20
  66.5 0.5 collective-permute-start.19
  67.0 2.2 %collective-permute-start.22 = (f32[120,256]{1,0:T(8,128)S(1)}, f32[120,256]{1,0:T(8,128)S(1)}, u32[]{:S(2)}, u32[]{:S(2)}) collective-permute-start(f32[120,256]{1,0:T(8,128)S(1)} %sum_up.1.refs_0_), channel_id=1, source_target_pairs={{0,1},{1,0},{2,3},{3,2},{4,5},{5,4},{6,7},{7,6},{8,9},{9,8},{10,11... | collective-permute-start | bytes 368648 | tf_op jit(solution)/shard_map/ppermute | solution.py:462
  69.1 0.6 collective-permute-done.21.refs_3_
  69.7 2.7 %collective-permute-start.25 = (f32[120,256]{1,0:T(8,128)S(1)}, f32[120,256]{1,0:T(8,128)S(1)}, u32[]{:S(2)}, u32[]{:S(2)}) collective-permute-start(f32[120,256]{1,0:T(8,128)S(1)} %collective-permute-done.21.refs_3_), channel_id=1, source_target_pairs={{0,1},{1,0},{2,3},{3,2},{4,5},{5,4},{6,7},{7,6},{8,9},{9,8},{10,11... | collective-permute-start | bytes 368648 | tf_op jit(solution)/shard_map/ppermute | solution.py:462
  72.5 0.0 collective-permute-done.20.refs_2_
  72.5 2.2 %collective-permute-start.24 = (f32[120,256]{1,0:T(8,128)S(1)}, f32[120,256]{1,0:T(8,128)S(1)}, u32[]{:S(2)}, u32[]{:S(2)}) collective-permute-start(f32[120,256]{1,0:T(8,128)S(1)} %collective-permute-done.20.refs_2_), channel_id=1, source_target_pairs={{0,1},{1,0},{2,3},{3,2},{4,5},{5,4},{6,7},{7,6},{8,9},{9,8},{10,11... | collective-permute-start | bytes 368648 | tf_op jit(solution)/shard_map/ppermute | solution.py:462
  74.7 0.0 collective-permute-done.19.refs_1_
  74.7 0.0 collective-permute-start.23
  74.7 0.0 collective-permute-done.22.refs_4_
  74.7 0.0 collective-permute-done.25.refs_7_
  74.7 1.0 %collective-permute-done.24.refs_6_ = f32[120,256]{1,0:T(8,128)S(1)} collective-permute-done((f32[120,256]{1,0:T(8,128)S(1)}, f32[120,256]{1,0:T(8,128)S(1)}, u32[]{:S(2)}, u32[]{:S(2)}) %collective-permute-start.24) | collective-permute-done | bytes 122912 | tf_op jit(solution)/shard_map/ppermute | solution.py:462
  75.7 0.4 collective-permute-done.23.refs_5_
  76.0 1.5 %store.1 = f32[8,28800]{1,0:T(8,128)} custom-call(f32[120,256]{1,0:T(8,128)S(1)} %sum_up.1.refs_0_, f32[120,256]{1,0:T(8,128)S(1)} %collective-permute-done.19.refs_1_, f32[120,256]{1,0:T(8,128)S(1)} %collective-permute-done.20.refs_2_, f32[120,256]{1,0:T(8,128)S(1)} %collective-permute-done.21.refs_3_, f32[120,256]{1,0:T(8,128)S(1)} %collective-permute-done.22.refs_4_, ...), custom_call_target="tpu_custom_call" | custom-call | tf_op jit(solution)/shard_map/store/pallas_call | solution.py:424
  (1 shorter events, 0.0 us)
Async XLA Ops:
  3.9 11.4 %collective-permute-start = (f32[120,256]{1,0:T(8,128)S(1)}, f32[120,256]{1,0:T(8,128)S(1)}, u32[]{:S(2)}, u32[]{:S(2)}) collective-permute-start(f32[120,256]{1,0:T(8,128)S(1)} %get-tuple-element.33), channel_id=1, source_target_pairs={{0,48},{8,56},{16,32},{24,40},{32,16},{40,24},{48,0},{56,8},{1,49}... | collective-permute-start | bytes 368648 | tf_op jit(solution)/shard_map/ppermute | solution.py:439
  8.9 6.8 %collective-permute-start.1 = (f32[120,256]{1,0:T(8,128)S(1)}, f32[120,256]{1,0:T(8,128)S(1)}, u32[]{:S(2)}, u32[]{:S(2)}) collective-permute-start(f32[120,256]{1,0:T(8,128)S(1)} %get-tuple-element.34), channel_id=1, source_target_pairs={{0,16},{8,24},{16,0},{24,8},{32,48},{40,56},{48,32},{56,40},{1,17}... | collective-permute-start | bytes 368648 | tf_op jit(solution)/shard_map/ppermute | solution.py:439
  9.1 9.2 %collective-permute-start.2 = (f32[120,256]{1,0:T(8,128)S(1)}, f32[120,256]{1,0:T(8,128)S(1)}, u32[]{:S(2)}, u32[]{:S(2)}) collective-permute-start(f32[120,256]{1,0:T(8,128)S(1)} %get-tuple-element.35), channel_id=1, source_target_pairs={{0,56},{8,48},{16,40},{24,32},{32,24},{40,16},{48,8},{56,0},{1,57}... | collective-permute-start | bytes 368648 | tf_op jit(solution)/shard_map/ppermute | solution.py:439
  13.5 5.7 %collective-permute-start.3 = (f32[120,256]{1,0:T(8,128)S(1)}, f32[120,256]{1,0:T(8,128)S(1)}, u32[]{:S(2)}, u32[]{:S(2)}) collective-permute-start(f32[120,256]{1,0:T(8,128)S(1)} %get-tuple-element.40), channel_id=1, source_target_pairs={{0,40},{8,32},{16,56},{24,48},{32,8},{40,0},{48,24},{56,16},{1,41}... | collective-permute-start | bytes 368648 | tf_op jit(solution)/shard_map/ppermute | solution.py:439
  14.9 8.4 %collective-permute-start.4 = (f32[120,256]{1,0:T(8,128)S(1)}, f32[120,256]{1,0:T(8,128)S(1)}, u32[]{:S(2)}, u32[]{:S(2)}) collective-permute-start(f32[120,256]{1,0:T(8,128)S(1)} %get-tuple-element.41), channel_id=1, source_target_pairs={{0,32},{8,40},{16,48},{24,56},{32,0},{40,8},{48,16},{56,24},{1,33}... | collective-permute-start | bytes 368648 | tf_op jit(solution)/shard_map/ppermute | solution.py:439
  15.3 7.9 %collective-permute-start.5 = (f32[120,256]{1,0:T(8,128)S(1)}, f32[120,256]{1,0:T(8,128)S(1)}, u32[]{:S(2)}, u32[]{:S(2)}) collective-permute-start(f32[120,256]{1,0:T(8,128)S(1)} %get-tuple-element.42), channel_id=1, source_target_pairs={{0,24},{8,16},{16,8},{24,0},{32,56},{40,48},{48,40},{56,32},{1,25}... | collective-permute-start | bytes 368648 | tf_op jit(solution)/shard_map/ppermute | solution.py:439
  15.8 7.5 %collective-permute-start.6 = (f32[120,256]{1,0:T(8,128)S(1)}, f32[120,256]{1,0:T(8,128)S(1)}, u32[]{:S(2)}, u32[]{:S(2)}) collective-permute-start(f32[120,256]{1,0:T(8,128)S(1)} %get-tuple-element.43), channel_id=1, source_target_pairs={{0,8},{8,0},{16,24},{24,16},{32,40},{40,32},{48,56},{56,48},{1,9},... | collective-permute-start | bytes 368648 | tf_op jit(solution)/shard_map/ppermute | solution.py:439
  24.2 6.9 %collective-permute-start.7 = (f32[120,256]{1,0:T(8,128)S(1)}, f32[120,256]{1,0:T(8,128)S(1)}, u32[]{:S(2)}, u32[]{:S(2)}) collective-permute-start(f32[120,256]{1,0:T(8,128)S(1)} %get-tuple-element.48.h_ref), channel_id=1, source_target_pairs={{0,96},{32,64},{64,32},{96,0},{1,97},{33,65},{65,33},{97,1},{2,98}... | collective-permute-start | bytes 368648 | tf_op jit(solution)/shard_map/ppermute | solution.py:448
  32.6 6.7 %collective-permute-start.13 = (f32[120,256]{1,0:T(8,128)S(1)}, f32[120,256]{1,0:T(8,128)S(1)}, u32[]{:S(2)}, u32[]{:S(2)}) collective-permute-start(f32[120,256]{1,0:T(8,128)S(1)} %get-tuple-element.59), channel_id=1, source_target_pairs={{0,48},{8,56},{16,32},{24,40},{32,16},{40,24},{48,0},{56,8},{1,49}... | collective-permute-start | bytes 368648 | tf_op jit(solution)/shard_map/ppermute | solution.py:439
  34.3 6.7 %collective-permute-start.14 = (f32[120,256]{1,0:T(8,128)S(1)}, f32[120,256]{1,0:T(8,128)S(1)}, u32[]{:S(2)}, u32[]{:S(2)}) collective-permute-start(f32[120,256]{1,0:T(8,128)S(1)} %get-tuple-element.60), channel_id=1, source_target_pairs={{0,16},{8,24},{16,0},{24,8},{32,48},{40,56},{48,32},{56,40},{1,17}... | collective-permute-start | bytes 368648 | tf_op jit(solution)/shard_map/ppermute | solution.py:439
  35.0 11.8 %collective-permute-start.8 = (f32[120,256]{1,0:T(8,128)S(1)}, f32[120,256]{1,0:T(8,128)S(1)}, u32[]{:S(2)}, u32[]{:S(2)}) collective-permute-start(f32[120,256]{1,0:T(8,128)S(1)} %get-tuple-element.49), channel_id=1, source_target_pairs={{0,56},{8,48},{16,40},{24,32},{32,24},{40,16},{48,8},{56,0},{1,57}... | collective-permute-start | bytes 368648 | tf_op jit(solution)/shard_map/ppermute | solution.py:439
  37.5 9.2 %collective-permute-start.9 = (f32[120,256]{1,0:T(8,128)S(1)}, f32[120,256]{1,0:T(8,128)S(1)}, u32[]{:S(2)}, u32[]{:S(2)}) collective-permute-start(f32[120,256]{1,0:T(8,128)S(1)} %get-tuple-element.50), channel_id=1, source_target_pairs={{0,40},{8,32},{16,56},{24,48},{32,8},{40,0},{48,24},{56,16},{1,41}... | collective-permute-start | bytes 368648 | tf_op jit(solution)/shard_map/ppermute | solution.py:439
  37.9 10.2 %collective-permute-start.10 = (f32[120,256]{1,0:T(8,128)S(1)}, f32[120,256]{1,0:T(8,128)S(1)}, u32[]{:S(2)}, u32[]{:S(2)}) collective-permute-start(f32[120,256]{1,0:T(8,128)S(1)} %get-tuple-element.51), channel_id=1, source_target_pairs={{0,32},{8,40},{16,48},{24,56},{32,0},{40,8},{48,16},{56,24},{1,33}... | collective-permute-start | bytes 368648 | tf_op jit(solution)/shard_map/ppermute | solution.py:439
  39.3 8.9 %collective-permute-start.11 = (f32[120,256]{1,0:T(8,128)S(1)}, f32[120,256]{1,0:T(8,128)S(1)}, u32[]{:S(2)}, u32[]{:S(2)}) collective-permute-start(f32[120,256]{1,0:T(8,128)S(1)} %get-tuple-element.52), channel_id=1, source_target_pairs={{0,24},{8,16},{16,8},{24,0},{32,56},{40,48},{48,40},{56,32},{1,25}... | collective-permute-start | bytes 368648 | tf_op jit(solution)/shard_map/ppermute | solution.py:439
  41.0 7.1 %collective-permute-start.12 = (f32[120,256]{1,0:T(8,128)S(1)}, f32[120,256]{1,0:T(8,128)S(1)}, u32[]{:S(2)}, u32[]{:S(2)}) collective-permute-start(f32[120,256]{1,0:T(8,128)S(1)} %get-tuple-element.53), channel_id=1, source_target_pairs={{0,8},{8,0},{16,24},{24,16},{32,40},{40,32},{48,56},{56,48},{1,9},... | collective-permute-start | bytes 368648 | tf_op jit(solution)/shard_map/ppermute | solution.py:439
  50.3 3.5 %collective-permute-start.15 = (f32[4,120,256]{2,1,0:T(8,128)S(1)}, f32[4,120,256]{2,1,0:T(8,128)S(1)}, u32[]{:S(2)}, u32[]{:S(2)}) collective-permute-start(f32[4,120,256]{2,1,0:T(8,128)S(1)} %down_theirs.1), channel_id=1, source_target_pairs={{0,1},{1,0},{2,3},{3,2},{4,5},{5,4},{6,7},{7,6},{8,9},{9,8},{10,11... | collective-permute-start | bytes 1474568 | tf_op jit(solution)/shard_map/ppermute | solution.py:456
  53.9 8.0 %collective-permute-start.18 = (f32[120,256]{1,0:T(8,128)S(1)}, f32[120,256]{1,0:T(8,128)S(1)}, u32[]{:S(2)}, u32[]{:S(2)}) collective-permute-start(f32[120,256]{1,0:T(8,128)S(1)} %get-tuple-element.61), channel_id=1, source_target_pairs={{0,6},{2,4},{4,2},{6,0},{1,7},{3,5},{5,3},{7,1},{8,14},{10,12},{12... | collective-permute-start | bytes 368648 | tf_op jit(solution)/shard_map/ppermute | solution.py:442
  56.7 6.1 %collective-permute-start.17 = (f32[120,256]{1,0:T(8,128)S(1)}, f32[120,256]{1,0:T(8,128)S(1)}, u32[]{:S(2)}, u32[]{:S(2)}) collective-permute-start(f32[120,256]{1,0:T(8,128)S(1)} %get-tuple-element.62), channel_id=1, source_target_pairs={{0,4},{2,6},{4,0},{6,2},{1,5},{3,7},{5,1},{7,3},{8,12},{10,14},{12... | collective-permute-start | bytes 368648 | tf_op jit(solution)/shard_map/ppermute | solution.py:442
  57.0 6.3 %collective-permute-start.16 = (f32[120,256]{1,0:T(8,128)S(1)}, f32[120,256]{1,0:T(8,128)S(1)}, u32[]{:S(2)}, u32[]{:S(2)}) collective-permute-start(f32[120,256]{1,0:T(8,128)S(1)} %get-tuple-element.63), channel_id=1, source_target_pairs={{0,2},{2,0},{4,6},{6,4},{1,3},{3,1},{5,7},{7,5},{8,10},{10,8},{12,... | collective-permute-start | bytes 368648 | tf_op jit(solution)/shard_map/ppermute | solution.py:442
  63.4 6.3 %collective-permute-start.21 = (f32[120,256]{1,0:T(8,128)S(1)}, f32[120,256]{1,0:T(8,128)S(1)}, u32[]{:S(2)}, u32[]{:S(2)}) collective-permute-start(f32[120,256]{1,0:T(8,128)S(1)} %sum_up.1.refs_0_), channel_id=1, source_target_pairs={{0,6},{2,4},{4,2},{6,0},{1,7},{3,5},{5,3},{7,1},{8,14},{10,12},{12... | collective-permute-start | bytes 368648 | tf_op jit(solution)/shard_map/ppermute | solution.py:442
  66.1 6.4 %collective-permute-start.20 = (f32[120,256]{1,0:T(8,128)S(1)}, f32[120,256]{1,0:T(8,128)S(1)}, u32[]{:S(2)}, u32[]{:S(2)}) collective-permute-start(f32[120,256]{1,0:T(8,128)S(1)} %sum_up.1.refs_0_), channel_id=1, source_target_pairs={{0,4},{2,6},{4,0},{6,2},{1,5},{3,7},{5,1},{7,3},{8,12},{10,14},{12... | collective-permute-start | bytes 368648 | tf_op jit(solution)/shard_map/ppermute | solution.py:442
  66.5 8.2 %collective-permute-start.19 = (f32[120,256]{1,0:T(8,128)S(1)}, f32[120,256]{1,0:T(8,128)S(1)}, u32[]{:S(2)}, u32[]{:S(2)}) collective-permute-start(f32[120,256]{1,0:T(8,128)S(1)} %sum_up.1.refs_0_), channel_id=1, source_target_pairs={{0,2},{2,0},{4,6},{6,4},{1,3},{3,1},{5,7},{7,5},{8,10},{10,8},{12,... | collective-permute-start | bytes 368648 | tf_op jit(solution)/shard_map/ppermute | solution.py:442
  67.0 7.7 %collective-permute-start.22 = (f32[120,256]{1,0:T(8,128)S(1)}, f32[120,256]{1,0:T(8,128)S(1)}, u32[]{:S(2)}, u32[]{:S(2)}) collective-permute-start(f32[120,256]{1,0:T(8,128)S(1)} %sum_up.1.refs_0_), channel_id=1, source_target_pairs={{0,1},{1,0},{2,3},{3,2},{4,5},{5,4},{6,7},{7,6},{8,9},{9,8},{10,11... | collective-permute-start | bytes 368648 | tf_op jit(solution)/shard_map/ppermute | solution.py:462
  69.7 5.0 %collective-permute-start.25 = (f32[120,256]{1,0:T(8,128)S(1)}, f32[120,256]{1,0:T(8,128)S(1)}, u32[]{:S(2)}, u32[]{:S(2)}) collective-permute-start(f32[120,256]{1,0:T(8,128)S(1)} %collective-permute-done.21.refs_3_), channel_id=1, source_target_pairs={{0,1},{1,0},{2,3},{3,2},{4,5},{5,4},{6,7},{7,6},{8,9},{9,8},{10,11... | collective-permute-start | bytes 368648 | tf_op jit(solution)/shard_map/ppermute | solution.py:462
  72.5 3.2 %collective-permute-start.24 = (f32[120,256]{1,0:T(8,128)S(1)}, f32[120,256]{1,0:T(8,128)S(1)}, u32[]{:S(2)}, u32[]{:S(2)}) collective-permute-start(f32[120,256]{1,0:T(8,128)S(1)} %collective-permute-done.20.refs_2_), channel_id=1, source_target_pairs={{0,1},{1,0},{2,3},{3,2},{4,5},{5,4},{6,7},{7,6},{8,9},{9,8},{10,11... | collective-permute-start | bytes 368648 | tf_op jit(solution)/shard_map/ppermute | solution.py:462
  74.7 1.3 %collective-permute-start.23 = (f32[120,256]{1,0:T(8,128)S(1)}, f32[120,256]{1,0:T(8,128)S(1)}, u32[]{:S(2)}, u32[]{:S(2)}) collective-permute-start(f32[120,256]{1,0:T(8,128)S(1)} %collective-permute-done.19.refs_1_), channel_id=1, source_target_pairs={{0,1},{1,0},{2,3},{3,2},{4,5},{5,4},{6,7},{7,6},{8,9},{9,8},{10,11... | collective-permute-start | bytes 368648 | tf_op jit(solution)/shard_map/ppermute | solution.py:462

commit v4 on v3

--- a/solution.py
+++ b/solution.py
@@ -17,7 +17,7 @@
 SMEM = pl.BlockSpec(memory_space=pltpu.SMEM)
 HBM = pl.BlockSpec(memory_space=pltpu.HBM)
 
-OFFSETS = (6, 2, 7, 5, 4, 3, 1, 0)
+OFFSETS = (2, 6, 4, 7, 3, 5, 1, 0)
 UP_GROUPS = ((0, 1, 2), (3, 4, 5, 6, 7))
 DOWN_GROUPS = ((7, 0, 1), (2, 3, 4, 5, 6))
 NODES = 2 * len(UP_GROUPS)
@@ -86,12 +86,13 @@
     zeros = jnp.zeros((ND, L - M), F32)
     for (a, b), copy in zip(ROWS, copies):
         copy.wait()
-        for m in range(a, b):
-            rows = pl.ds(m, ND, stride=L)
-            real = buffer_ref[:, m * W : m * W + M]
-            imag = buffer_ref[:, m * W + M : (m + 1) * W]
-            out_ref[0, rows, :] = jnp.concatenate([real, zeros], axis=1)
-            out_ref[1, rows, :] = jnp.concatenate([imag, zeros], axis=1)
+        for part in range(2):
+            for start in range(a, b, ND):
+                firsts = [m * W + part * M for m in range(start, start + ND)]
+                rows = [jnp.concatenate([buffer_ref[:, i : i + M], zeros], axis=1) for i in firsts]
+                block = jnp.swapaxes(jnp.stack(rows), 0, 1)
+                for k in range(ND):
+                    out_ref[part, k * L + start : k * L + start + ND, :] = block[k]
     for k in range(ND):
         out_ref[:, k * L + M : (k + 1) * L, :] = jnp.zeros((2, L - M, L), F32)
 
@@ -457,8 +458,10 @@
     mine = down(functools.partial(down_last_kernel, True, two), "down_mine", 4, two, last, tables, nodes, part)
 
     g = mine + received
-    total = sum_up(g[0], *[turned(i, g[i]) for i in range(1, 4)])
-    parts = [total] + [turned(i, total) for i in range(1, 4)]
+    order = (3, 1, 2)
+    total = sum_up(g[0], *[turned(i, g[i]) for i in order])
+    turns = {i: turned(i, total) for i in order}
+    parts = [total] + [turns[i] for i in (1, 2, 3)]
     parts += [lax.ppermute(x, "c", swap) for x in parts]
     return store(parts)
 

time: 77.8 us -> 77.4 us (level)
  starting transfers between devices: 38.1 us -> 40 us
  waiting for transfers between devices: 20 us -> 18.2 us
    ppermute x1, starting transfers between devices: 1.34 us -> 5.54 us  [shards(): received = lax.ppermute(theirs, 'c', swap)]
    ppermute x14, waiting for transfers between devices: 10.9 us -> 7.74 us  [exchange(): lax.ppermute(x, ('zl', 'x'), [(s, s ^ OFFSETS[i]) for s in range(ND)])]
    ppermute x4, starting transfers between devices: 7.12 us -> 4.89 us  [shards(): parts += [lax.ppermute(x, 'c', swap) for x in parts]]
    ppermute x6, waiting for transfers between devices: 6.58 us -> 8.62 us  [turned(): return lax.ppermute(x, 'y', [(s, s ^ i) for s in range(4)])]
  transfers between devices with their start and end apart: 26 -> 26, of which waited for: 12 -> 11; matrix products, arithmetic and copies ran while one was open for 0% -> 0% of each run, Pallas kernels for 12% -> 11%
where the time goes in v4:
time: 77.4 us; the launch traced here: 77.3 us
  starting transfers between devices  40 us (52%)
  Pallas kernels  18.6 us (24%)
  waiting for transfers between devices  18.2 us (24%)
    ppermute x14, starting transfers between devices, exchange(): lax.ppermute(x, ('zl', 'x'), [(s, s ^ OFFSETS[i]) for s in range(ND)])  18.7 us
    ppermute x6, waiting for transfers between devices, turned(): return lax.ppermute(x, 'y', [(s, s ^ i) for s in range(4)])  8.62 us
    ppermute x14, waiting for transfers between devices, exchange(): lax.ppermute(x, ('zl', 'x'), [(s, s ^ OFFSETS[i]) for s in range(ND)])  7.74 us
    ppermute x6, starting transfers between devices, turned(): return lax.ppermute(x, 'y', [(s, s ^ i) for s in range(4)])  7.47 us
    pallas_call x3, Pallas kernels, down(): pl.pallas_call(kernel, out_shape=single(sections, M, 2 * L), in_specs=[VM...  6.85 us
    ppermute x1, starting transfers between devices, shards(): received = lax.ppermute(theirs, 'c', swap)  5.54 us
    ppermute x4, starting transfers between devices, shards(): parts += [lax.ppermute(x, 'c', swap) for x in parts]  4.89 us
    pallas_call x1, Pallas kernels, up(): pl.pallas_call(functools.partial(up_kernel, group), out_shape=outs, in_sp...  3.66 us
  transfers between devices with their start and end apart: 26, of which 11 were waited for; matrix products, arithmetic and copies ran while one was open for 0% of the time, Pallas kernels for 11%

profile of v4, /device:TPU:1, one launch (start us, length us, event | category | flops | bytes accessed | tf_op | source)
XLA Modules:
  0.0 77.3 jit_solution(7612807993620563136)
XLA Ops:
  0.0 3.7 %up.1 = (f32[2,1024,128]{2,1,0:T(8,128)S(1)}, bf16[8,2,128,256]{3,2,1,0:T(8,128)(2,1)S(1)}, f32[2,64,128]{2,1,0:T(8,128)S(1)}, f32[2,128,64]{2,1,0:T(8,128)S(1)}...) custom-call(f32[8]{0:T(128)} %freq_hbm.1, ...), custom_call_target="tpu_custom_call" | custom-call | tf_op jit(solution)/shard_map/up/pallas_call | solution.py:192
  3.7 3.7 %collective-permute-start = (f32[120,256]{1,0:T(8,128)S(1)}, f32[120,256]{1,0:T(8,128)S(1)}, u32[]{:S(2)}, u32[]{:S(2)}) collective-permute-start(f32[120,256]{1,0:T(8,128)S(1)} %get-tuple-element.33), channel_id=1, source_target_pairs={{0,16},{8,24},{16,0},{24,8},{32,48},{40,56},{48,32},{56,40},{1,17}... | collective-permute-start | bytes 368648 | tf_op jit(solution)/shard_map/ppermute | solution.py:440
  7.3 1.6 %collective-permute-start.1 = (f32[120,256]{1,0:T(8,128)S(1)}, f32[120,256]{1,0:T(8,128)S(1)}, u32[]{:S(2)}, u32[]{:S(2)}) collective-permute-start(f32[120,256]{1,0:T(8,128)S(1)} %get-tuple-element.34), channel_id=1, source_target_pairs={{0,48},{8,56},{16,32},{24,40},{32,16},{40,24},{48,0},{56,8},{1,49}... | collective-permute-start | bytes 368648 | tf_op jit(solution)/shard_map/ppermute | solution.py:440
  8.9 0.1 collective-permute-start.2
  9.0 2.3 %up_second.1 = (bf16[4,5,2,128,256]{4,3,2,1,0:T(8,128)(2,1)S(1)}, bf16[2,5,2,128,256]{4,3,2,1,0:T(8,128)(2,1)S(1)}, f32[120,256]{1,0:T(8,128)S(1)}, f32[120,256]...) custom-call(f32[2,1024,128]{2,1,0:T(8,128)S(1)} %get-tuple-element.36.c_ref, ...), custom_call_target="tpu_custom_call" | custom-call | tf_op jit(solution)/shard_map/up_second/pallas_call | solution.py:212
  11.3 3.7 %collective-permute-start.3 = (f32[120,256]{1,0:T(8,128)S(1)}, f32[120,256]{1,0:T(8,128)S(1)}, u32[]{:S(2)}, u32[]{:S(2)}) collective-permute-start(f32[120,256]{1,0:T(8,128)S(1)} %get-tuple-element.40), channel_id=1, source_target_pairs={{0,56},{8,48},{16,40},{24,32},{32,24},{40,16},{48,8},{56,0},{1,57}... | collective-permute-start | bytes 368648 | tf_op jit(solution)/shard_map/ppermute | solution.py:440
  15.0 0.2 collective-permute-start.4
  15.2 0.0 collective-permute-done.refs_0_
  15.2 0.0 collective-permute-start.5
  15.2 0.0 collective-permute-done.1.refs_1_
  15.2 1.4 %collective-permute-start.6 = (f32[120,256]{1,0:T(8,128)S(1)}, f32[120,256]{1,0:T(8,128)S(1)}, u32[]{:S(2)}, u32[]{:S(2)}) collective-permute-start(f32[120,256]{1,0:T(8,128)S(1)} %get-tuple-element.43), channel_id=1, source_target_pairs={{0,8},{8,0},{16,24},{24,16},{32,40},{40,32},{48,56},{56,48},{1,9},... | collective-permute-start | bytes 368648 | tf_op jit(solution)/shard_map/ppermute | solution.py:440
  16.5 0.0 collective-permute-done.2.refs_2_
  16.5 0.8 %collective-permute-done.3.refs_3_ = f32[120,256]{1,0:T(8,128)S(1)} collective-permute-done((f32[120,256]{1,0:T(8,128)S(1)}, f32[120,256]{1,0:T(8,128)S(1)}, u32[]{:S(2)}, u32[]{:S(2)}) %collective-permute-start.3) | collective-permute-done | bytes 122912 | tf_op jit(solution)/shard_map/ppermute | solution.py:440
  17.3 3.4 %collective-permute-done.4.refs_4_ = f32[120,256]{1,0:T(8,128)S(1)} collective-permute-done((f32[120,256]{1,0:T(8,128)S(1)}, f32[120,256]{1,0:T(8,128)S(1)}, u32[]{:S(2)}, u32[]{:S(2)}) %collective-permute-start.4) | collective-permute-done | bytes 122912 | tf_op jit(solution)/shard_map/ppermute | solution.py:440
  20.7 0.0 collective-permute-done.5.refs_5_
  20.7 0.0 collective-permute-done.6.refs_6_
  20.7 0.9 %half.1 = (f32[120,256]{1,0:T(8,128)S(1)}, bf16[8,2,128,256]{3,2,1,0:T(8,128)(2,1)S(1)}, bf16[4,2,128,256]{3,2,1,0:T(8,128)(2,1)S(1)}, bf16[2,2,128,256]{3,2,1,0:T(8,128)(2,1)S(1)}) custom-call(f32[120,256]{1,0:T(8,128)S(1)} %collective-permute-done.refs_0_, f32[120,256]{1,0:T(8,128)S(1)} %collective-permute-done.1.refs_1_, ...), custom_call_target="tpu_custom_call" | custom-call | tf_op jit(solution)/shard_map/half/pallas_call | solution.py:237
  21.6 3.4 %collective-permute-start.7 = (f32[120,256]{1,0:T(8,128)S(1)}, f32[120,256]{1,0:T(8,128)S(1)}, u32[]{:S(2)}, u32[]{:S(2)}) collective-permute-start(f32[120,256]{1,0:T(8,128)S(1)} %get-tuple-element.48.h_ref), channel_id=1, source_target_pairs={{0,96},{32,64},{64,32},{96,0},{1,97},{33,65},{65,33},{97,1},{2,98}... | collective-permute-start | bytes 368648 | tf_op jit(solution)/shard_map/ppermute | solution.py:449
  25.0 1.8 %pick.1.m_ref = f32[128,256]{1,0:T(8,128)S(1)} custom-call(f32[8,28800]{1,0:T(8,128)} %flat_ref.1), custom_call_target="tpu_custom_call" | custom-call | tf_op jit(solution)/shard_map/pick/pallas_call | solution.py:253
  26.8 0.5 collective-permute-done.7.other_ref
  27.3 1.6 %top.1 = (f32[120,256]{1,0:T(8,128)S(1)}, f32[120,256]{1,0:T(8,128)S(1)}, f32[120,256]{1,0:T(8,128)S(1)}, f32[120,256]{1,0:T(8,128)S(1)}, f32[120,256]{1,0:T(8,1...) custom-call(bf16[8,2,128,256]{3,2,1,0:T(8,128)(2,1)S(1)} %get-tuple-element.45.r_ref, ...), custom_call_target="tpu_custom_call" | custom-call | tf_op jit(solution)/shard_map/top/pallas_call | solution.py:291
  28.9 3.2 %collective-permute-start.13 = (f32[120,256]{1,0:T(8,128)S(1)}, f32[120,256]{1,0:T(8,128)S(1)}, u32[]{:S(2)}, u32[]{:S(2)}) collective-permute-start(f32[120,256]{1,0:T(8,128)S(1)} %get-tuple-element.59), channel_id=1, source_target_pairs={{0,16},{8,24},{16,0},{24,8},{32,48},{40,56},{48,32},{56,40},{1,17}... | collective-permute-start | bytes 368648 | tf_op jit(solution)/shard_map/ppermute | solution.py:440
  32.1 0.0 collective-permute-start.14
  32.1 1.3 %collective-permute-start.8 = (f32[120,256]{1,0:T(8,128)S(1)}, f32[120,256]{1,0:T(8,128)S(1)}, u32[]{:S(2)}, u32[]{:S(2)}) collective-permute-start(f32[120,256]{1,0:T(8,128)S(1)} %get-tuple-element.49), channel_id=1, source_target_pairs={{0,32},{8,40},{16,48},{24,56},{32,0},{40,8},{48,16},{56,24},{1,33}... | collective-permute-start | bytes 368648 | tf_op jit(solution)/shard_map/ppermute | solution.py:440
  33.4 2.0 %collective-permute-start.9 = (f32[120,256]{1,0:T(8,128)S(1)}, f32[120,256]{1,0:T(8,128)S(1)}, u32[]{:S(2)}, u32[]{:S(2)}) collective-permute-start(f32[120,256]{1,0:T(8,128)S(1)} %get-tuple-element.50), channel_id=1, source_target_pairs={{0,56},{8,48},{16,40},{24,32},{32,24},{40,16},{48,8},{56,0},{1,57}... | collective-permute-start | bytes 368648 | tf_op jit(solution)/shard_map/ppermute | solution.py:440
  35.4 0.6 collective-permute-start.10
  35.9 0.0 collective-permute-done.13.refs_1_
  36.0 0.9 %collective-permute-start.11 = (f32[120,256]{1,0:T(8,128)S(1)}, f32[120,256]{1,0:T(8,128)S(1)}, u32[]{:S(2)}, u32[]{:S(2)}) collective-permute-start(f32[120,256]{1,0:T(8,128)S(1)} %get-tuple-element.52), channel_id=1, source_target_pairs={{0,40},{8,32},{16,56},{24,48},{32,8},{40,0},{48,24},{56,16},{1,41}... | collective-permute-start | bytes 368648 | tf_op jit(solution)/shard_map/ppermute | solution.py:440
  36.8 2.4 %collective-permute-done.14.refs_2_ = f32[120,256]{1,0:T(8,128)S(1)} collective-permute-done((f32[120,256]{1,0:T(8,128)S(1)}, f32[120,256]{1,0:T(8,128)S(1)}, u32[]{:S(2)}, u32[]{:S(2)}) %collective-permute-start.14) | collective-permute-done | bytes 122912 | tf_op jit(solution)/shard_map/ppermute | solution.py:440
  39.3 0.3 collective-permute-start.12
  39.6 2.6 %down_1.1.refs_12_ = f32[8,120,256]{2,1,0:T(8,128)S(1)} custom-call(f32[120,256]{1,0:T(8,128)S(1)} %get-tuple-element.58.refs_0_, f32[120,256]{1,0:T(8,128)S(1)} %collective-permute-done.13.refs_1_, f32[120,256]{1,0:T(8,128)S(1)} %collective-permute-done.14.refs_2_, bf16[8,2,128,256]{3,2,1,0:T(8,128)(2,1)S(1)} %get-tuple-element.37.ch_ref.refs_3_.refs_5_, ...), custom_call_target="tpu_custom_call" | custom-call | tf_op jit(solution)/shard_map/down_1/pallas_call | solution.py:372
  42.2 0.0 collective-permute-done.8.refs_0_
  42.2 0.0 collective-permute-done.9.refs_1_
  42.2 1.0 %collective-permute-done.10.refs_2_ = f32[120,256]{1,0:T(8,128)S(1)} collective-permute-done((f32[120,256]{1,0:T(8,128)S(1)}, f32[120,256]{1,0:T(8,128)S(1)}, u32[]{:S(2)}, u32[]{:S(2)}) %collective-permute-start.10) | collective-permute-done | bytes 122912 | tf_op jit(solution)/shard_map/ppermute | solution.py:440
  43.2 0.0 collective-permute-done.11.refs_3_
  43.2 0.1 collective-permute-done.12.refs_4_
  43.3 2.1 %down_theirs.1 = f32[4,120,256]{2,1,0:T(8,128)S(1)} custom-call(f32[120,256]{1,0:T(8,128)S(1)} %collective-permute-done.8.refs_0_, f32[120,256]{1,0:T(8,128)S(1)} %collective-permute-done.9.refs_1_, f32[120,256]{1,0:T(8,128)S(1)} %collective-permute-done.10.refs_2_, f32[120,256]{1,0:T(8,128)S(1)} %collective-permute-done.11.refs_3_, ...), custom_call_target="tpu_custom_call" | custom-call | tf_op jit(solution)/shard_map/down_theirs/pallas_call | solution.py:372
  45.4 5.5 %collective-permute-start.15 = (f32[4,120,256]{2,1,0:T(8,128)S(1)}, f32[4,120,256]{2,1,0:T(8,128)S(1)}, u32[]{:S(2)}, u32[]{:S(2)}) collective-permute-start(f32[4,120,256]{2,1,0:T(8,128)S(1)} %down_theirs.1), channel_id=1, source_target_pairs={{0,1},{1,0},{2,3},{3,2},{4,5},{5,4},{6,7},{7,6},{8,9},{9,8},{10,11... | collective-permute-start | bytes 1474568 | tf_op jit(solution)/shard_map/ppermute | solution.py:457
  51.0 2.1 %down_mine.1 = f32[4,120,256]{2,1,0:T(8,128)S(1)} custom-call(f32[120,256]{1,0:T(8,128)S(1)} %collective-permute-done.8.refs_0_, f32[120,256]{1,0:T(8,128)S(1)} %collective-permute-done.9.refs_1_, f32[120,256]{1,0:T(8,128)S(1)} %collective-permute-done.10.refs_2_, f32[120,256]{1,0:T(8,128)S(1)} %collective-permute-done.11.refs_3_, ...), custom_call_target="tpu_custom_call" | custom-call | tf_op jit(solution)/shard_map/down_mine/pallas_call | solution.py:372
  53.1 0.0 collective-permute-done.15
  53.1 0.1 add.3
  53.2 3.0 %collective-permute-start.18 = (f32[120,256]{1,0:T(8,128)S(1)}, f32[120,256]{1,0:T(8,128)S(1)}, u32[]{:S(2)}, u32[]{:S(2)}) collective-permute-start(f32[120,256]{1,0:T(8,128)S(1)} %get-tuple-element.61), channel_id=1, source_target_pairs={{0,4},{2,6},{4,0},{6,2},{1,5},{3,7},{5,1},{7,3},{8,12},{10,14},{12... | collective-permute-start | bytes 368648 | tf_op jit(solution)/shard_map/ppermute | solution.py:443
  56.2 0.4 collective-permute-start.17
  56.6 0.4 collective-permute-start.16
  57.0 2.7 %collective-permute-done.18.c_ref = f32[120,256]{1,0:T(8,128)S(1)} collective-permute-done((f32[120,256]{1,0:T(8,128)S(1)}, f32[120,256]{1,0:T(8,128)S(1)}, u32[]{:S(2)}, u32[]{:S(2)}) %collective-permute-start.18) | collective-permute-done | bytes 122912 | tf_op jit(solution)/shard_map/ppermute | solution.py:443
  59.7 3.0 %collective-permute-done.17.b_ref = f32[120,256]{1,0:T(8,128)S(1)} collective-permute-done((f32[120,256]{1,0:T(8,128)S(1)}, f32[120,256]{1,0:T(8,128)S(1)}, u32[]{:S(2)}, u32[]{:S(2)}) %collective-permute-start.17) | collective-permute-done | bytes 122912 | tf_op jit(solution)/shard_map/ppermute | solution.py:443
  62.7 0.0 collective-permute-done.16.a_ref
  62.7 0.1 sum_up.1.refs_0_
  62.8 3.0 %collective-permute-start.21 = (f32[120,256]{1,0:T(8,128)S(1)}, f32[120,256]{1,0:T(8,128)S(1)}, u32[]{:S(2)}, u32[]{:S(2)}) collective-permute-start(f32[120,256]{1,0:T(8,128)S(1)} %sum_up.1.refs_0_), channel_id=1, source_target_pairs={{0,6},{2,4},{4,2},{6,0},{1,7},{3,5},{5,3},{7,1},{8,14},{10,12},{12... | collective-permute-start | bytes 368648 | tf_op jit(solution)/shard_map/ppermute | solution.py:443
  65.8 0.3 collective-permute-start.20
  66.1 0.4 collective-permute-start.19
  66.5 1.6 %collective-permute-start.22 = (f32[120,256]{1,0:T(8,128)S(1)}, f32[120,256]{1,0:T(8,128)S(1)}, u32[]{:S(2)}, u32[]{:S(2)}) collective-permute-start(f32[120,256]{1,0:T(8,128)S(1)} %sum_up.1.refs_0_), channel_id=1, source_target_pairs={{0,1},{1,0},{2,3},{3,2},{4,5},{5,4},{6,7},{7,6},{8,9},{9,8},{10,11... | collective-permute-start | bytes 368648 | tf_op jit(solution)/shard_map/ppermute | solution.py:465
  68.1 2.9 %collective-permute-done.21.refs_3_ = f32[120,256]{1,0:T(8,128)S(1)} collective-permute-done((f32[120,256]{1,0:T(8,128)S(1)}, f32[120,256]{1,0:T(8,128)S(1)}, u32[]{:S(2)}, u32[]{:S(2)}) %collective-permute-start.21) | collective-permute-done | bytes 122912 | tf_op jit(solution)/shard_map/ppermute | solution.py:443
  71.0 1.0 %collective-permute-start.25 = (f32[120,256]{1,0:T(8,128)S(1)}, f32[120,256]{1,0:T(8,128)S(1)}, u32[]{:S(2)}, u32[]{:S(2)}) collective-permute-start(f32[120,256]{1,0:T(8,128)S(1)} %collective-permute-done.21.refs_3_), channel_id=1, source_target_pairs={{0,1},{1,0},{2,3},{3,2},{4,5},{5,4},{6,7},{7,6},{8,9},{9,8},{10,11... | collective-permute-start | bytes 368648 | tf_op jit(solution)/shard_map/ppermute | solution.py:465
  72.0 0.0 collective-permute-done.20.refs_2_
  72.0 2.3 %collective-permute-start.24 = (f32[120,256]{1,0:T(8,128)S(1)}, f32[120,256]{1,0:T(8,128)S(1)}, u32[]{:S(2)}, u32[]{:S(2)}) collective-permute-start(f32[120,256]{1,0:T(8,128)S(1)} %collective-permute-done.20.refs_2_), channel_id=1, source_target_pairs={{0,1},{1,0},{2,3},{3,2},{4,5},{5,4},{6,7},{7,6},{8,9},{9,8},{10,11... | collective-permute-start | bytes 368648 | tf_op jit(solution)/shard_map/ppermute | solution.py:465
  74.3 0.0 collective-permute-done.19.refs_1_
  74.3 0.0 collective-permute-start.23
  74.3 0.0 collective-permute-done.22.refs_4_
  74.3 0.0 collective-permute-done.25.refs_7_
  74.3 1.0 %collective-permute-done.24.refs_6_ = f32[120,256]{1,0:T(8,128)S(1)} collective-permute-done((f32[120,256]{1,0:T(8,128)S(1)}, f32[120,256]{1,0:T(8,128)S(1)}, u32[]{:S(2)}, u32[]{:S(2)}) %collective-permute-start.24) | collective-permute-done | bytes 122912 | tf_op jit(solution)/shard_map/ppermute | solution.py:465
  75.3 0.4 collective-permute-done.23.refs_5_
  75.7 1.5 %store.1 = f32[8,28800]{1,0:T(8,128)} custom-call(f32[120,256]{1,0:T(8,128)S(1)} %sum_up.1.refs_0_, f32[120,256]{1,0:T(8,128)S(1)} %collective-permute-done.19.refs_1_, f32[120,256]{1,0:T(8,128)S(1)} %collective-permute-done.20.refs_2_, f32[120,256]{1,0:T(8,128)S(1)} %collective-permute-done.21.refs_3_, f32[120,256]{1,0:T(8,128)S(1)} %collective-permute-done.22.refs_4_, ...), custom_call_target="tpu_custom_call" | custom-call | tf_op jit(solution)/shard_map/store/pallas_call | solution.py:425
  (1 shorter events, 0.0 us)
Async XLA Ops:
  3.7 11.5 %collective-permute-start = (f32[120,256]{1,0:T(8,128)S(1)}, f32[120,256]{1,0:T(8,128)S(1)}, u32[]{:S(2)}, u32[]{:S(2)}) collective-permute-start(f32[120,256]{1,0:T(8,128)S(1)} %get-tuple-element.33), channel_id=1, source_target_pairs={{0,16},{8,24},{16,0},{24,8},{32,48},{40,56},{48,32},{56,40},{1,17}... | collective-permute-start | bytes 368648 | tf_op jit(solution)/shard_map/ppermute | solution.py:440
  7.3 7.8 %collective-permute-start.1 = (f32[120,256]{1,0:T(8,128)S(1)}, f32[120,256]{1,0:T(8,128)S(1)}, u32[]{:S(2)}, u32[]{:S(2)}) collective-permute-start(f32[120,256]{1,0:T(8,128)S(1)} %get-tuple-element.34), channel_id=1, source_target_pairs={{0,48},{8,56},{16,32},{24,40},{32,16},{40,24},{48,0},{56,8},{1,49}... | collective-permute-start | bytes 368648 | tf_op jit(solution)/shard_map/ppermute | solution.py:440
  8.9 7.6 %collective-permute-start.2 = (f32[120,256]{1,0:T(8,128)S(1)}, f32[120,256]{1,0:T(8,128)S(1)}, u32[]{:S(2)}, u32[]{:S(2)}) collective-permute-start(f32[120,256]{1,0:T(8,128)S(1)} %get-tuple-element.35), channel_id=1, source_target_pairs={{0,32},{8,40},{16,48},{24,56},{32,0},{40,8},{48,16},{56,24},{1,33}... | collective-permute-start | bytes 368648 | tf_op jit(solution)/shard_map/ppermute | solution.py:440
  11.3 6.1 %collective-permute-start.3 = (f32[120,256]{1,0:T(8,128)S(1)}, f32[120,256]{1,0:T(8,128)S(1)}, u32[]{:S(2)}, u32[]{:S(2)}) collective-permute-start(f32[120,256]{1,0:T(8,128)S(1)} %get-tuple-element.40), channel_id=1, source_target_pairs={{0,56},{8,48},{16,40},{24,32},{32,24},{40,16},{48,8},{56,0},{1,57}... | collective-permute-start | bytes 368648 | tf_op jit(solution)/shard_map/ppermute | solution.py:440
  15.0 5.8 %collective-permute-start.4 = (f32[120,256]{1,0:T(8,128)S(1)}, f32[120,256]{1,0:T(8,128)S(1)}, u32[]{:S(2)}, u32[]{:S(2)}) collective-permute-start(f32[120,256]{1,0:T(8,128)S(1)} %get-tuple-element.41), channel_id=1, source_target_pairs={{0,24},{8,16},{16,8},{24,0},{32,56},{40,48},{48,40},{56,32},{1,25}... | collective-permute-start | bytes 368648 | tf_op jit(solution)/shard_map/ppermute | solution.py:440
  15.2 5.6 %collective-permute-start.5 = (f32[120,256]{1,0:T(8,128)S(1)}, f32[120,256]{1,0:T(8,128)S(1)}, u32[]{:S(2)}, u32[]{:S(2)}) collective-permute-start(f32[120,256]{1,0:T(8,128)S(1)} %get-tuple-element.42), channel_id=1, source_target_pairs={{0,40},{8,32},{16,56},{24,48},{32,8},{40,0},{48,24},{56,16},{1,41}... | collective-permute-start | bytes 368648 | tf_op jit(solution)/shard_map/ppermute | solution.py:440
  15.2 5.6 %collective-permute-start.6 = (f32[120,256]{1,0:T(8,128)S(1)}, f32[120,256]{1,0:T(8,128)S(1)}, u32[]{:S(2)}, u32[]{:S(2)}) collective-permute-start(f32[120,256]{1,0:T(8,128)S(1)} %get-tuple-element.43), channel_id=1, source_target_pairs={{0,8},{8,0},{16,24},{24,16},{32,40},{40,32},{48,56},{56,48},{1,9},... | collective-permute-start | bytes 368648 | tf_op jit(solution)/shard_map/ppermute | solution.py:440
  21.6 5.7 %collective-permute-start.7 = (f32[120,256]{1,0:T(8,128)S(1)}, f32[120,256]{1,0:T(8,128)S(1)}, u32[]{:S(2)}, u32[]{:S(2)}) collective-permute-start(f32[120,256]{1,0:T(8,128)S(1)} %get-tuple-element.48.h_ref), channel_id=1, source_target_pairs={{0,96},{32,64},{64,32},{96,0},{1,97},{33,65},{65,33},{97,1},{2,98}... | collective-permute-start | bytes 368648 | tf_op jit(solution)/shard_map/ppermute | solution.py:449
  28.9 7.0 %collective-permute-start.13 = (f32[120,256]{1,0:T(8,128)S(1)}, f32[120,256]{1,0:T(8,128)S(1)}, u32[]{:S(2)}, u32[]{:S(2)}) collective-permute-start(f32[120,256]{1,0:T(8,128)S(1)} %get-tuple-element.59), channel_id=1, source_target_pairs={{0,16},{8,24},{16,0},{24,8},{32,48},{40,56},{48,32},{56,40},{1,17}... | collective-permute-start | bytes 368648 | tf_op jit(solution)/shard_map/ppermute | solution.py:440
  32.1 7.2 %collective-permute-start.14 = (f32[120,256]{1,0:T(8,128)S(1)}, f32[120,256]{1,0:T(8,128)S(1)}, u32[]{:S(2)}, u32[]{:S(2)}) collective-permute-start(f32[120,256]{1,0:T(8,128)S(1)} %get-tuple-element.60), channel_id=1, source_target_pairs={{0,48},{8,56},{16,32},{24,40},{32,16},{40,24},{48,0},{56,8},{1,49}... | collective-permute-start | bytes 368648 | tf_op jit(solution)/shard_map/ppermute | solution.py:440
  32.1 10.1 %collective-permute-start.8 = (f32[120,256]{1,0:T(8,128)S(1)}, f32[120,256]{1,0:T(8,128)S(1)}, u32[]{:S(2)}, u32[]{:S(2)}) collective-permute-start(f32[120,256]{1,0:T(8,128)S(1)} %get-tuple-element.49), channel_id=1, source_target_pairs={{0,32},{8,40},{16,48},{24,56},{32,0},{40,8},{48,16},{56,24},{1,33}... | collective-permute-start | bytes 368648 | tf_op jit(solution)/shard_map/ppermute | solution.py:440
  33.4 8.8 %collective-permute-start.9 = (f32[120,256]{1,0:T(8,128)S(1)}, f32[120,256]{1,0:T(8,128)S(1)}, u32[]{:S(2)}, u32[]{:S(2)}) collective-permute-start(f32[120,256]{1,0:T(8,128)S(1)} %get-tuple-element.50), channel_id=1, source_target_pairs={{0,56},{8,48},{16,40},{24,32},{32,24},{40,16},{48,8},{56,0},{1,57}... | collective-permute-start | bytes 368648 | tf_op jit(solution)/shard_map/ppermute | solution.py:440
  35.4 7.8 %collective-permute-start.10 = (f32[120,256]{1,0:T(8,128)S(1)}, f32[120,256]{1,0:T(8,128)S(1)}, u32[]{:S(2)}, u32[]{:S(2)}) collective-permute-start(f32[120,256]{1,0:T(8,128)S(1)} %get-tuple-element.51), channel_id=1, source_target_pairs={{0,24},{8,16},{16,8},{24,0},{32,56},{40,48},{48,40},{56,32},{1,25}... | collective-permute-start | bytes 368648 | tf_op jit(solution)/shard_map/ppermute | solution.py:440
  36.0 7.2 %collective-permute-start.11 = (f32[120,256]{1,0:T(8,128)S(1)}, f32[120,256]{1,0:T(8,128)S(1)}, u32[]{:S(2)}, u32[]{:S(2)}) collective-permute-start(f32[120,256]{1,0:T(8,128)S(1)} %get-tuple-element.52), channel_id=1, source_target_pairs={{0,40},{8,32},{16,56},{24,48},{32,8},{40,0},{48,24},{56,16},{1,41}... | collective-permute-start | bytes 368648 | tf_op jit(solution)/shard_map/ppermute | solution.py:440
  39.3 4.0 %collective-permute-start.12 = (f32[120,256]{1,0:T(8,128)S(1)}, f32[120,256]{1,0:T(8,128)S(1)}, u32[]{:S(2)}, u32[]{:S(2)}) collective-permute-start(f32[120,256]{1,0:T(8,128)S(1)} %get-tuple-element.53), channel_id=1, source_target_pairs={{0,8},{8,0},{16,24},{24,16},{32,40},{40,32},{48,56},{56,48},{1,9},... | collective-permute-start | bytes 368648 | tf_op jit(solution)/shard_map/ppermute | solution.py:440
  45.4 7.7 %collective-permute-start.15 = (f32[4,120,256]{2,1,0:T(8,128)S(1)}, f32[4,120,256]{2,1,0:T(8,128)S(1)}, u32[]{:S(2)}, u32[]{:S(2)}) collective-permute-start(f32[4,120,256]{2,1,0:T(8,128)S(1)} %down_theirs.1), channel_id=1, source_target_pairs={{0,1},{1,0},{2,3},{3,2},{4,5},{5,4},{6,7},{7,6},{8,9},{9,8},{10,11... | collective-permute-start | bytes 1474568 | tf_op jit(solution)/shard_map/ppermute | solution.py:457
  53.2 6.5 %collective-permute-start.18 = (f32[120,256]{1,0:T(8,128)S(1)}, f32[120,256]{1,0:T(8,128)S(1)}, u32[]{:S(2)}, u32[]{:S(2)}) collective-permute-start(f32[120,256]{1,0:T(8,128)S(1)} %get-tuple-element.61), channel_id=1, source_target_pairs={{0,4},{2,6},{4,0},{6,2},{1,5},{3,7},{5,1},{7,3},{8,12},{10,14},{12... | collective-permute-start | bytes 368648 | tf_op jit(solution)/shard_map/ppermute | solution.py:443
  56.2 6.5 %collective-permute-start.17 = (f32[120,256]{1,0:T(8,128)S(1)}, f32[120,256]{1,0:T(8,128)S(1)}, u32[]{:S(2)}, u32[]{:S(2)}) collective-permute-start(f32[120,256]{1,0:T(8,128)S(1)} %get-tuple-element.62), channel_id=1, source_target_pairs={{0,2},{2,0},{4,6},{6,4},{1,3},{3,1},{5,7},{7,5},{8,10},{10,8},{12,... | collective-permute-start | bytes 368648 | tf_op jit(solution)/shard_map/ppermute | solution.py:443
  56.6 6.1 %collective-permute-start.16 = (f32[120,256]{1,0:T(8,128)S(1)}, f32[120,256]{1,0:T(8,128)S(1)}, u32[]{:S(2)}, u32[]{:S(2)}) collective-permute-start(f32[120,256]{1,0:T(8,128)S(1)} %get-tuple-element.63), channel_id=1, source_target_pairs={{0,6},{2,4},{4,2},{6,0},{1,7},{3,5},{5,3},{7,1},{8,14},{10,12},{12... | collective-permute-start | bytes 368648 | tf_op jit(solution)/shard_map/ppermute | solution.py:443
  62.8 8.2 %collective-permute-start.21 = (f32[120,256]{1,0:T(8,128)S(1)}, f32[120,256]{1,0:T(8,128)S(1)}, u32[]{:S(2)}, u32[]{:S(2)}) collective-permute-start(f32[120,256]{1,0:T(8,128)S(1)} %sum_up.1.refs_0_), channel_id=1, source_target_pairs={{0,6},{2,4},{4,2},{6,0},{1,7},{3,5},{5,3},{7,1},{8,14},{10,12},{12... | collective-permute-start | bytes 368648 | tf_op jit(solution)/shard_map/ppermute | solution.py:443
  65.8 6.2 %collective-permute-start.20 = (f32[120,256]{1,0:T(8,128)S(1)}, f32[120,256]{1,0:T(8,128)S(1)}, u32[]{:S(2)}, u32[]{:S(2)}) collective-permute-start(f32[120,256]{1,0:T(8,128)S(1)} %sum_up.1.refs_0_), channel_id=1, source_target_pairs={{0,4},{2,6},{4,0},{6,2},{1,5},{3,7},{5,1},{7,3},{8,12},{10,14},{12... | collective-permute-start | bytes 368648 | tf_op jit(solution)/shard_map/ppermute | solution.py:443
  66.1 8.2 %collective-permute-start.19 = (f32[120,256]{1,0:T(8,128)S(1)}, f32[120,256]{1,0:T(8,128)S(1)}, u32[]{:S(2)}, u32[]{:S(2)}) collective-permute-start(f32[120,256]{1,0:T(8,128)S(1)} %sum_up.1.refs_0_), channel_id=1, source_target_pairs={{0,2},{2,0},{4,6},{6,4},{1,3},{3,1},{5,7},{7,5},{8,10},{10,8},{12,... | collective-permute-start | bytes 368648 | tf_op jit(solution)/shard_map/ppermute | solution.py:443
  66.5 7.8 %collective-permute-start.22 = (f32[120,256]{1,0:T(8,128)S(1)}, f32[120,256]{1,0:T(8,128)S(1)}, u32[]{:S(2)}, u32[]{:S(2)}) collective-permute-start(f32[120,256]{1,0:T(8,128)S(1)} %sum_up.1.refs_0_), channel_id=1, source_target_pairs={{0,1},{1,0},{2,3},{3,2},{4,5},{5,4},{6,7},{7,6},{8,9},{9,8},{10,11... | collective-permute-start | bytes 368648 | tf_op jit(solution)/shard_map/ppermute | solution.py:465
  71.0 3.3 %collective-permute-start.25 = (f32[120,256]{1,0:T(8,128)S(1)}, f32[120,256]{1,0:T(8,128)S(1)}, u32[]{:S(2)}, u32[]{:S(2)}) collective-permute-start(f32[120,256]{1,0:T(8,128)S(1)} %collective-permute-done.21.refs_3_), channel_id=1, source_target_pairs={{0,1},{1,0},{2,3},{3,2},{4,5},{5,4},{6,7},{7,6},{8,9},{9,8},{10,11... | collective-permute-start | bytes 368648 | tf_op jit(solution)/shard_map/ppermute | solution.py:465
  72.0 3.2 %collective-permute-start.24 = (f32[120,256]{1,0:T(8,128)S(1)}, f32[120,256]{1,0:T(8,128)S(1)}, u32[]{:S(2)}, u32[]{:S(2)}) collective-permute-start(f32[120,256]{1,0:T(8,128)S(1)} %collective-permute-done.20.refs_2_), channel_id=1, source_target_pairs={{0,1},{1,0},{2,3},{3,2},{4,5},{5,4},{6,7},{7,6},{8,9},{9,8},{10,11... | collective-permute-start | bytes 368648 | tf_op jit(solution)/shard_map/ppermute | solution.py:465
  74.3 1.3 %collective-permute-start.23 = (f32[120,256]{1,0:T(8,128)S(1)}, f32[120,256]{1,0:T(8,128)S(1)}, u32[]{:S(2)}, u32[]{:S(2)}) collective-permute-start(f32[120,256]{1,0:T(8,128)S(1)} %collective-permute-done.19.refs_1_), channel_id=1, source_target_pairs={{0,1},{1,0},{2,3},{3,2},{4,5},{5,4},{6,7},{7,6},{8,9},{9,8},{10,11... | collective-permute-start | bytes 368648 | tf_op jit(solution)/shard_map/ppermute | solution.py:465

commit v5 on v4

--- a/solution.py
+++ b/solution.py
@@ -19,7 +19,7 @@
 
 OFFSETS = (2, 6, 4, 7, 3, 5, 1, 0)
 UP_GROUPS = ((0, 1, 2), (3, 4, 5, 6, 7))
-DOWN_GROUPS = ((7, 0, 1), (2, 3, 4, 5, 6))
+DOWN_GROUPS = ((7, 0), (1, 2, 3, 4, 5, 6))
 NODES = 2 * len(UP_GROUPS)
 ROWS = ((0, 32), (32, 64), (64, 96), (96, 120))
 

time: 77.4 us -> 77.3 us (level)
  starting transfers between devices: 40 us -> 41.7 us
  waiting for transfers between devices: 18.2 us -> 16.7 us
    ppermute x14, waiting for transfers between devices: 7.74 us -> 6.46 us  [exchange(): lax.ppermute(x, ('zl', 'x'), [(s, s ^ OFFSETS[i]) for s in range(ND)])]
    ppermute x14, starting transfers between devices: 18.7 us -> 19.9 us  [exchange(): lax.ppermute(x, ('zl', 'x'), [(s, s ^ OFFSETS[i]) for s in range(ND)])]
  transfers between devices with their start and end apart: 26 -> 26, of which waited for: 11 -> 11; matrix products, arithmetic and copies ran while one was open for 0% -> 0% of each run, Pallas kernels for 11% -> 10%
where the time goes in v5:
time: 77.3 us; the launch traced here: 77.2 us
  starting transfers between devices  41.7 us (54%)
  Pallas kernels  18.3 us (24%)
  waiting for transfers between devices  16.7 us (22%)
    ppermute x14, starting transfers between devices, exchange(): lax.ppermute(x, ('zl', 'x'), [(s, s ^ OFFSETS[i]) for s in range(ND)])  19.9 us
    ppermute x6, waiting for transfers between devices, turned(): return lax.ppermute(x, 'y', [(s, s ^ i) for s in range(4)])  8.41 us
    ppermute x6, starting transfers between devices, turned(): return lax.ppermute(x, 'y', [(s, s ^ i) for s in range(4)])  7.61 us
    pallas_call x3, Pallas kernels, down(): pl.pallas_call(kernel, out_shape=single(sections, M, 2 * L), in_specs=[VM...  6.71 us
    ppermute x14, waiting for transfers between devices, exchange(): lax.ppermute(x, ('zl', 'x'), [(s, s ^ OFFSETS[i]) for s in range(ND)])  6.46 us
    ppermute x1, starting transfers between devices, shards(): received = lax.ppermute(theirs, 'c', swap)  5.81 us
    ppermute x4, starting transfers between devices, shards(): parts += [lax.ppermute(x, 'c', swap) for x in parts]  4.97 us
    pallas_call x1, Pallas kernels, up(): pl.pallas_call(functools.partial(up_kernel, group), out_shape=outs, in_sp...  3.63 us
  transfers between devices with their start and end apart: 26, of which 11 were waited for; matrix products, arithmetic and copies ran while one was open for 0% of the time, Pallas kernels for 10%

profile of v5, /device:TPU:1, one launch (start us, length us, event | category | flops | bytes accessed | tf_op | source)
XLA Modules:
  0.0 77.2 jit_solution(13704827571296417546)
XLA Ops:
  0.0 3.6 %up.1 = (f32[2,1024,128]{2,1,0:T(8,128)S(1)}, bf16[8,2,128,256]{3,2,1,0:T(8,128)(2,1)S(1)}, f32[2,64,128]{2,1,0:T(8,128)S(1)}, f32[2,128,64]{2,1,0:T(8,128)S(1)}...) custom-call(f32[8]{0:T(128)} %freq_hbm.1, ...), custom_call_target="tpu_custom_call" | custom-call | tf_op jit(solution)/shard_map/up/pallas_call | solution.py:192
  3.6 3.7 %collective-permute-start = (f32[120,256]{1,0:T(8,128)S(1)}, f32[120,256]{1,0:T(8,128)S(1)}, u32[]{:S(2)}, u32[]{:S(2)}) collective-permute-start(f32[120,256]{1,0:T(8,128)S(1)} %get-tuple-element.33), channel_id=1, source_target_pairs={{0,16},{8,24},{16,0},{24,8},{32,48},{40,56},{48,32},{56,40},{1,17}... | collective-permute-start | bytes 368648 | tf_op jit(solution)/shard_map/ppermute | solution.py:440
  7.3 1.6 %collective-permute-start.1 = (f32[120,256]{1,0:T(8,128)S(1)}, f32[120,256]{1,0:T(8,128)S(1)}, u32[]{:S(2)}, u32[]{:S(2)}) collective-permute-start(f32[120,256]{1,0:T(8,128)S(1)} %get-tuple-element.34), channel_id=1, source_target_pairs={{0,48},{8,56},{16,32},{24,40},{32,16},{40,24},{48,0},{56,8},{1,49}... | collective-permute-start | bytes 368648 | tf_op jit(solution)/shard_map/ppermute | solution.py:440
  8.9 0.1 collective-permute-start.2
  8.9 2.2 %up_second.1 = (bf16[4,5,2,128,256]{4,3,2,1,0:T(8,128)(2,1)S(1)}, bf16[2,5,2,128,256]{4,3,2,1,0:T(8,128)(2,1)S(1)}, f32[120,256]{1,0:T(8,128)S(1)}, f32[120,256]...) custom-call(f32[2,1024,128]{2,1,0:T(8,128)S(1)} %get-tuple-element.36.c_ref, ...), custom_call_target="tpu_custom_call" | custom-call | tf_op jit(solution)/shard_map/up_second/pallas_call | solution.py:212
  11.1 3.7 %collective-permute-start.3 = (f32[120,256]{1,0:T(8,128)S(1)}, f32[120,256]{1,0:T(8,128)S(1)}, u32[]{:S(2)}, u32[]{:S(2)}) collective-permute-start(f32[120,256]{1,0:T(8,128)S(1)} %get-tuple-element.40), channel_id=1, source_target_pairs={{0,56},{8,48},{16,40},{24,32},{32,24},{40,16},{48,8},{56,0},{1,57}... | collective-permute-start | bytes 368648 | tf_op jit(solution)/shard_map/ppermute | solution.py:440
  14.8 0.2 collective-permute-start.4
  15.0 0.0 collective-permute-done.refs_0_
  15.0 0.0 collective-permute-start.5
  15.0 0.0 collective-permute-done.1.refs_1_
  15.0 1.3 %collective-permute-start.6 = (f32[120,256]{1,0:T(8,128)S(1)}, f32[120,256]{1,0:T(8,128)S(1)}, u32[]{:S(2)}, u32[]{:S(2)}) collective-permute-start(f32[120,256]{1,0:T(8,128)S(1)} %get-tuple-element.43), channel_id=1, source_target_pairs={{0,8},{8,0},{16,24},{24,16},{32,40},{40,32},{48,56},{56,48},{1,9},... | collective-permute-start | bytes 368648 | tf_op jit(solution)/shard_map/ppermute | solution.py:440
  16.4 0.0 collective-permute-done.2.refs_2_
  16.4 0.8 %collective-permute-done.3.refs_3_ = f32[120,256]{1,0:T(8,128)S(1)} collective-permute-done((f32[120,256]{1,0:T(8,128)S(1)}, f32[120,256]{1,0:T(8,128)S(1)}, u32[]{:S(2)}, u32[]{:S(2)}) %collective-permute-start.3) | collective-permute-done | bytes 122912 | tf_op jit(solution)/shard_map/ppermute | solution.py:440
  17.2 3.4 %collective-permute-done.4.refs_4_ = f32[120,256]{1,0:T(8,128)S(1)} collective-permute-done((f32[120,256]{1,0:T(8,128)S(1)}, f32[120,256]{1,0:T(8,128)S(1)}, u32[]{:S(2)}, u32[]{:S(2)}) %collective-permute-start.4) | collective-permute-done | bytes 122912 | tf_op jit(solution)/shard_map/ppermute | solution.py:440
  20.6 0.0 collective-permute-done.5.refs_5_
  20.6 0.0 collective-permute-done.6.refs_6_
  20.6 0.9 %half.1 = (f32[120,256]{1,0:T(8,128)S(1)}, bf16[8,2,128,256]{3,2,1,0:T(8,128)(2,1)S(1)}, bf16[4,2,128,256]{3,2,1,0:T(8,128)(2,1)S(1)}, bf16[2,2,128,256]{3,2,1,0:T(8,128)(2,1)S(1)}) custom-call(f32[120,256]{1,0:T(8,128)S(1)} %collective-permute-done.refs_0_, f32[120,256]{1,0:T(8,128)S(1)} %collective-permute-done.1.refs_1_, ...), custom_call_target="tpu_custom_call" | custom-call | tf_op jit(solution)/shard_map/half/pallas_call | solution.py:237
  21.5 3.5 %collective-permute-start.7 = (f32[120,256]{1,0:T(8,128)S(1)}, f32[120,256]{1,0:T(8,128)S(1)}, u32[]{:S(2)}, u32[]{:S(2)}) collective-permute-start(f32[120,256]{1,0:T(8,128)S(1)} %get-tuple-element.48.h_ref), channel_id=1, source_target_pairs={{0,96},{32,64},{64,32},{96,0},{1,97},{33,65},{65,33},{97,1},{2,98}... | collective-permute-start | bytes 368648 | tf_op jit(solution)/shard_map/ppermute | solution.py:449
  25.0 1.8 %pick.1.m_ref = f32[128,256]{1,0:T(8,128)S(1)} custom-call(f32[8,28800]{1,0:T(8,128)} %flat_ref.1), custom_call_target="tpu_custom_call" | custom-call | tf_op jit(solution)/shard_map/pick/pallas_call | solution.py:253
  26.8 0.5 collective-permute-done.7.other_ref
  27.3 1.6 %top.1 = (f32[120,256]{1,0:T(8,128)S(1)}, f32[120,256]{1,0:T(8,128)S(1)}, f32[120,256]{1,0:T(8,128)S(1)}, f32[120,256]{1,0:T(8,128)S(1)}, f32[120,256]{1,0:T(8,1...) custom-call(bf16[8,2,128,256]{3,2,1,0:T(8,128)(2,1)S(1)} %get-tuple-element.45.r_ref, ...), custom_call_target="tpu_custom_call" | custom-call | tf_op jit(solution)/shard_map/top/pallas_call | solution.py:291
  28.8 2.1 %collective-permute-start.8 = (f32[120,256]{1,0:T(8,128)S(1)}, f32[120,256]{1,0:T(8,128)S(1)}, u32[]{:S(2)}, u32[]{:S(2)}) collective-permute-start(f32[120,256]{1,0:T(8,128)S(1)} %get-tuple-element.49), channel_id=1, source_target_pairs={{0,48},{8,56},{16,32},{24,40},{32,16},{40,24},{48,0},{56,8},{1,49}... | collective-permute-start | bytes 368648 | tf_op jit(solution)/shard_map/ppermute | solution.py:440
  31.0 1.0 %collective-permute-start.14 = (f32[120,256]{1,0:T(8,128)S(1)}, f32[120,256]{1,0:T(8,128)S(1)}, u32[]{:S(2)}, u32[]{:S(2)}) collective-permute-start(f32[120,256]{1,0:T(8,128)S(1)} %get-tuple-element.60), channel_id=1, source_target_pairs={{0,16},{8,24},{16,0},{24,8},{32,48},{40,56},{48,32},{56,40},{1,17}... | collective-permute-start | bytes 368648 | tf_op jit(solution)/shard_map/ppermute | solution.py:440
  32.0 1.1 %collective-permute-start.9 = (f32[120,256]{1,0:T(8,128)S(1)}, f32[120,256]{1,0:T(8,128)S(1)}, u32[]{:S(2)}, u32[]{:S(2)}) collective-permute-start(f32[120,256]{1,0:T(8,128)S(1)} %get-tuple-element.50), channel_id=1, source_target_pairs={{0,32},{8,40},{16,48},{24,56},{32,0},{40,8},{48,16},{56,24},{1,33}... | collective-permute-start | bytes 368648 | tf_op jit(solution)/shard_map/ppermute | solution.py:440
  33.1 2.1 %collective-permute-start.10 = (f32[120,256]{1,0:T(8,128)S(1)}, f32[120,256]{1,0:T(8,128)S(1)}, u32[]{:S(2)}, u32[]{:S(2)}) collective-permute-start(f32[120,256]{1,0:T(8,128)S(1)} %get-tuple-element.51), channel_id=1, source_target_pairs={{0,56},{8,48},{16,40},{24,32},{32,24},{40,16},{48,8},{56,0},{1,57}... | collective-permute-start | bytes 368648 | tf_op jit(solution)/shard_map/ppermute | solution.py:440
  35.2 0.7 collective-permute-start.11
  35.9 0.0 collective-permute-done.8.refs_0_
  35.9 0.8 %collective-permute-start.12 = (f32[120,256]{1,0:T(8,128)S(1)}, f32[120,256]{1,0:T(8,128)S(1)}, u32[]{:S(2)}, u32[]{:S(2)}) collective-permute-start(f32[120,256]{1,0:T(8,128)S(1)} %get-tuple-element.53), channel_id=1, source_target_pairs={{0,40},{8,32},{16,56},{24,48},{32,8},{40,0},{48,24},{56,16},{1,41}... | collective-permute-start | bytes 368648 | tf_op jit(solution)/shard_map/ppermute | solution.py:440
  36.7 0.0 collective-permute-done.14.refs_1_
  36.7 1.5 %collective-permute-start.13 = (f32[120,256]{1,0:T(8,128)S(1)}, f32[120,256]{1,0:T(8,128)S(1)}, u32[]{:S(2)}, u32[]{:S(2)}) collective-permute-start(f32[120,256]{1,0:T(8,128)S(1)} %get-tuple-element.54), channel_id=1, source_target_pairs={{0,8},{8,0},{16,24},{24,16},{32,40},{40,32},{48,56},{56,48},{1,9},... | collective-permute-start | bytes 368648 | tf_op jit(solution)/shard_map/ppermute | solution.py:440
  38.2 1.7 %down_1.1.refs_13_ = f32[8,120,256]{2,1,0:T(8,128)S(1)} custom-call(f32[120,256]{1,0:T(8,128)S(1)} %get-tuple-element.59.refs_0_, f32[120,256]{1,0:T(8,128)S(1)} %collective-permute-done.14.refs_1_, bf16[8,2,128,256]{3,2,1,0:T(8,128)(2,1)S(1)} %get-tuple-element.37.ch_ref.refs_2_.refs_6_, f32[2,64,128]{2,1,0:T(8,128)S(1)} %get-tuple-element.38.tab_ref.refs_3_.refs_7_, ...), custom_call_target="tpu_custom_call" | custom-call | tf_op jit(solution)/shard_map/down_1/pallas_call | solution.py:372
  39.9 0.0 collective-permute-done.9.refs_1_
  39.9 1.9 %collective-permute-done.10.refs_2_ = f32[120,256]{1,0:T(8,128)S(1)} collective-permute-done((f32[120,256]{1,0:T(8,128)S(1)}, f32[120,256]{1,0:T(8,128)S(1)}, u32[]{:S(2)}, u32[]{:S(2)}) %collective-permute-start.10) | collective-permute-done | bytes 122912 | tf_op jit(solution)/shard_map/ppermute | solution.py:440
  41.7 0.2 collective-permute-done.11.refs_3_
  42.0 0.2 collective-permute-done.12.refs_4_
  42.1 0.0 collective-permute-done.13.refs_5_
  42.1 2.6 %down_theirs.1 = f32[4,120,256]{2,1,0:T(8,128)S(1)} custom-call(f32[120,256]{1,0:T(8,128)S(1)} %collective-permute-done.8.refs_0_, f32[120,256]{1,0:T(8,128)S(1)} %collective-permute-done.9.refs_1_, f32[120,256]{1,0:T(8,128)S(1)} %collective-permute-done.10.refs_2_, f32[120,256]{1,0:T(8,128)S(1)} %collective-permute-done.11.refs_3_, ...), custom_call_target="tpu_custom_call" | custom-call | tf_op jit(solution)/shard_map/down_theirs/pallas_call | solution.py:372
  44.7 5.8 %collective-permute-start.15 = (f32[4,120,256]{2,1,0:T(8,128)S(1)}, f32[4,120,256]{2,1,0:T(8,128)S(1)}, u32[]{:S(2)}, u32[]{:S(2)}) collective-permute-start(f32[4,120,256]{2,1,0:T(8,128)S(1)} %down_theirs.1), channel_id=1, source_target_pairs={{0,1},{1,0},{2,3},{3,2},{4,5},{5,4},{6,7},{7,6},{8,9},{9,8},{10,11... | collective-permute-start | bytes 1474568 | tf_op jit(solution)/shard_map/ppermute | solution.py:457
  50.5 2.5 %down_mine.1 = f32[4,120,256]{2,1,0:T(8,128)S(1)} custom-call(f32[120,256]{1,0:T(8,128)S(1)} %collective-permute-done.8.refs_0_, f32[120,256]{1,0:T(8,128)S(1)} %collective-permute-done.9.refs_1_, f32[120,256]{1,0:T(8,128)S(1)} %collective-permute-done.10.refs_2_, f32[120,256]{1,0:T(8,128)S(1)} %collective-permute-done.11.refs_3_, ...), custom_call_target="tpu_custom_call" | custom-call | tf_op jit(solution)/shard_map/down_mine/pallas_call | solution.py:372
  53.0 0.0 collective-permute-done.15
  53.0 0.1 add.3
  53.1 3.2 %collective-permute-start.18 = (f32[120,256]{1,0:T(8,128)S(1)}, f32[120,256]{1,0:T(8,128)S(1)}, u32[]{:S(2)}, u32[]{:S(2)}) collective-permute-start(f32[120,256]{1,0:T(8,128)S(1)} %get-tuple-element.61), channel_id=1, source_target_pairs={{0,4},{2,6},{4,0},{6,2},{1,5},{3,7},{5,1},{7,3},{8,12},{10,14},{12... | collective-permute-start | bytes 368648 | tf_op jit(solution)/shard_map/ppermute | solution.py:443
  56.3 0.4 collective-permute-start.17
  56.7 0.4 collective-permute-start.16
  57.1 2.6 %collective-permute-done.18.c_ref = f32[120,256]{1,0:T(8,128)S(1)} collective-permute-done((f32[120,256]{1,0:T(8,128)S(1)}, f32[120,256]{1,0:T(8,128)S(1)}, u32[]{:S(2)}, u32[]{:S(2)}) %collective-permute-start.18) | collective-permute-done | bytes 122912 | tf_op jit(solution)/shard_map/ppermute | solution.py:443
  59.7 3.0 %collective-permute-done.17.b_ref = f32[120,256]{1,0:T(8,128)S(1)} collective-permute-done((f32[120,256]{1,0:T(8,128)S(1)}, f32[120,256]{1,0:T(8,128)S(1)}, u32[]{:S(2)}, u32[]{:S(2)}) %collective-permute-start.17) | collective-permute-done | bytes 122912 | tf_op jit(solution)/shard_map/ppermute | solution.py:443
  62.7 0.0 collective-permute-done.16.a_ref
  62.7 0.1 sum_up.1.refs_0_
  62.8 2.9 %collective-permute-start.21 = (f32[120,256]{1,0:T(8,128)S(1)}, f32[120,256]{1,0:T(8,128)S(1)}, u32[]{:S(2)}, u32[]{:S(2)}) collective-permute-start(f32[120,256]{1,0:T(8,128)S(1)} %sum_up.1.refs_0_), channel_id=1, source_target_pairs={{0,6},{2,4},{4,2},{6,0},{1,7},{3,5},{5,3},{7,1},{8,14},{10,12},{12... | collective-permute-start | bytes 368648 | tf_op jit(solution)/shard_map/ppermute | solution.py:443
  65.7 0.3 collective-permute-start.20
  66.0 0.4 collective-permute-start.19
  66.4 1.6 %collective-permute-start.22 = (f32[120,256]{1,0:T(8,128)S(1)}, f32[120,256]{1,0:T(8,128)S(1)}, u32[]{:S(2)}, u32[]{:S(2)}) collective-permute-start(f32[120,256]{1,0:T(8,128)S(1)} %sum_up.1.refs_0_), channel_id=1, source_target_pairs={{0,1},{1,0},{2,3},{3,2},{4,5},{5,4},{6,7},{7,6},{8,9},{9,8},{10,11... | collective-permute-start | bytes 368648 | tf_op jit(solution)/shard_map/ppermute | solution.py:465
  68.0 2.8 %collective-permute-done.21.refs_3_ = f32[120,256]{1,0:T(8,128)S(1)} collective-permute-done((f32[120,256]{1,0:T(8,128)S(1)}, f32[120,256]{1,0:T(8,128)S(1)}, u32[]{:S(2)}, u32[]{:S(2)}) %collective-permute-start.21) | collective-permute-done | bytes 122912 | tf_op jit(solution)/shard_map/ppermute | solution.py:443
  70.9 1.0 %collective-permute-start.25 = (f32[120,256]{1,0:T(8,128)S(1)}, f32[120,256]{1,0:T(8,128)S(1)}, u32[]{:S(2)}, u32[]{:S(2)}) collective-permute-start(f32[120,256]{1,0:T(8,128)S(1)} %collective-permute-done.21.refs_3_), channel_id=1, source_target_pairs={{0,1},{1,0},{2,3},{3,2},{4,5},{5,4},{6,7},{7,6},{8,9},{9,8},{10,11... | collective-permute-start | bytes 368648 | tf_op jit(solution)/shard_map/ppermute | solution.py:465
  71.9 0.0 collective-permute-done.20.refs_2_
  71.9 2.3 %collective-permute-start.24 = (f32[120,256]{1,0:T(8,128)S(1)}, f32[120,256]{1,0:T(8,128)S(1)}, u32[]{:S(2)}, u32[]{:S(2)}) collective-permute-start(f32[120,256]{1,0:T(8,128)S(1)} %collective-permute-done.20.refs_2_), channel_id=1, source_target_pairs={{0,1},{1,0},{2,3},{3,2},{4,5},{5,4},{6,7},{7,6},{8,9},{9,8},{10,11... | collective-permute-start | bytes 368648 | tf_op jit(solution)/shard_map/ppermute | solution.py:465
  74.2 0.0 collective-permute-done.19.refs_1_
  74.2 0.0 collective-permute-start.23
  74.2 0.0 collective-permute-done.22.refs_4_
  74.2 0.0 collective-permute-done.25.refs_7_
  74.2 1.0 %collective-permute-done.24.refs_6_ = f32[120,256]{1,0:T(8,128)S(1)} collective-permute-done((f32[120,256]{1,0:T(8,128)S(1)}, f32[120,256]{1,0:T(8,128)S(1)}, u32[]{:S(2)}, u32[]{:S(2)}) %collective-permute-start.24) | collective-permute-done | bytes 122912 | tf_op jit(solution)/shard_map/ppermute | solution.py:465
  75.2 0.4 collective-permute-done.23.refs_5_
  75.6 1.5 %store.1 = f32[8,28800]{1,0:T(8,128)} custom-call(f32[120,256]{1,0:T(8,128)S(1)} %sum_up.1.refs_0_, f32[120,256]{1,0:T(8,128)S(1)} %collective-permute-done.19.refs_1_, f32[120,256]{1,0:T(8,128)S(1)} %collective-permute-done.20.refs_2_, f32[120,256]{1,0:T(8,128)S(1)} %collective-permute-done.21.refs_3_, f32[120,256]{1,0:T(8,128)S(1)} %collective-permute-done.22.refs_4_, ...), custom_call_target="tpu_custom_call" | custom-call | tf_op jit(solution)/shard_map/store/pallas_call | solution.py:425
  (1 shorter events, 0.0 us)
Async XLA Ops:
  3.6 11.4 %collective-permute-start = (f32[120,256]{1,0:T(8,128)S(1)}, f32[120,256]{1,0:T(8,128)S(1)}, u32[]{:S(2)}, u32[]{:S(2)}) collective-permute-start(f32[120,256]{1,0:T(8,128)S(1)} %get-tuple-element.33), channel_id=1, source_target_pairs={{0,16},{8,24},{16,0},{24,8},{32,48},{40,56},{48,32},{56,40},{1,17}... | collective-permute-start | bytes 368648 | tf_op jit(solution)/shard_map/ppermute | solution.py:440
  7.3 7.7 %collective-permute-start.1 = (f32[120,256]{1,0:T(8,128)S(1)}, f32[120,256]{1,0:T(8,128)S(1)}, u32[]{:S(2)}, u32[]{:S(2)}) collective-permute-start(f32[120,256]{1,0:T(8,128)S(1)} %get-tuple-element.34), channel_id=1, source_target_pairs={{0,48},{8,56},{16,32},{24,40},{32,16},{40,24},{48,0},{56,8},{1,49}... | collective-permute-start | bytes 368648 | tf_op jit(solution)/shard_map/ppermute | solution.py:440
  8.9 7.5 %collective-permute-start.2 = (f32[120,256]{1,0:T(8,128)S(1)}, f32[120,256]{1,0:T(8,128)S(1)}, u32[]{:S(2)}, u32[]{:S(2)}) collective-permute-start(f32[120,256]{1,0:T(8,128)S(1)} %get-tuple-element.35), channel_id=1, source_target_pairs={{0,32},{8,40},{16,48},{24,56},{32,0},{40,8},{48,16},{56,24},{1,33}... | collective-permute-start | bytes 368648 | tf_op jit(solution)/shard_map/ppermute | solution.py:440
  11.1 6.1 %collective-permute-start.3 = (f32[120,256]{1,0:T(8,128)S(1)}, f32[120,256]{1,0:T(8,128)S(1)}, u32[]{:S(2)}, u32[]{:S(2)}) collective-permute-start(f32[120,256]{1,0:T(8,128)S(1)} %get-tuple-element.40), channel_id=1, source_target_pairs={{0,56},{8,48},{16,40},{24,32},{32,24},{40,16},{48,8},{56,0},{1,57}... | collective-permute-start | bytes 368648 | tf_op jit(solution)/shard_map/ppermute | solution.py:440
  14.8 5.8 %collective-permute-start.4 = (f32[120,256]{1,0:T(8,128)S(1)}, f32[120,256]{1,0:T(8,128)S(1)}, u32[]{:S(2)}, u32[]{:S(2)}) collective-permute-start(f32[120,256]{1,0:T(8,128)S(1)} %get-tuple-element.41), channel_id=1, source_target_pairs={{0,24},{8,16},{16,8},{24,0},{32,56},{40,48},{48,40},{56,32},{1,25}... | collective-permute-start | bytes 368648 | tf_op jit(solution)/shard_map/ppermute | solution.py:440
  15.0 5.5 %collective-permute-start.5 = (f32[120,256]{1,0:T(8,128)S(1)}, f32[120,256]{1,0:T(8,128)S(1)}, u32[]{:S(2)}, u32[]{:S(2)}) collective-permute-start(f32[120,256]{1,0:T(8,128)S(1)} %get-tuple-element.42), channel_id=1, source_target_pairs={{0,40},{8,32},{16,56},{24,48},{32,8},{40,0},{48,24},{56,16},{1,41}... | collective-permute-start | bytes 368648 | tf_op jit(solution)/shard_map/ppermute | solution.py:440
  15.0 5.5 %collective-permute-start.6 = (f32[120,256]{1,0:T(8,128)S(1)}, f32[120,256]{1,0:T(8,128)S(1)}, u32[]{:S(2)}, u32[]{:S(2)}) collective-permute-start(f32[120,256]{1,0:T(8,128)S(1)} %get-tuple-element.43), channel_id=1, source_target_pairs={{0,8},{8,0},{16,24},{24,16},{32,40},{40,32},{48,56},{56,48},{1,9},... | collective-permute-start | bytes 368648 | tf_op jit(solution)/shard_map/ppermute | solution.py:440
  21.5 5.8 %collective-permute-start.7 = (f32[120,256]{1,0:T(8,128)S(1)}, f32[120,256]{1,0:T(8,128)S(1)}, u32[]{:S(2)}, u32[]{:S(2)}) collective-permute-start(f32[120,256]{1,0:T(8,128)S(1)} %get-tuple-element.48.h_ref), channel_id=1, source_target_pairs={{0,96},{32,64},{64,32},{96,0},{1,97},{33,65},{65,33},{97,1},{2,98}... | collective-permute-start | bytes 368648 | tf_op jit(solution)/shard_map/ppermute | solution.py:449
  28.8 7.1 %collective-permute-start.8 = (f32[120,256]{1,0:T(8,128)S(1)}, f32[120,256]{1,0:T(8,128)S(1)}, u32[]{:S(2)}, u32[]{:S(2)}) collective-permute-start(f32[120,256]{1,0:T(8,128)S(1)} %get-tuple-element.49), channel_id=1, source_target_pairs={{0,48},{8,56},{16,32},{24,40},{32,16},{40,24},{48,0},{56,8},{1,49}... | collective-permute-start | bytes 368648 | tf_op jit(solution)/shard_map/ppermute | solution.py:440
  31.0 5.7 %collective-permute-start.14 = (f32[120,256]{1,0:T(8,128)S(1)}, f32[120,256]{1,0:T(8,128)S(1)}, u32[]{:S(2)}, u32[]{:S(2)}) collective-permute-start(f32[120,256]{1,0:T(8,128)S(1)} %get-tuple-element.60), channel_id=1, source_target_pairs={{0,16},{8,24},{16,0},{24,8},{32,48},{40,56},{48,32},{56,40},{1,17}... | collective-permute-start | bytes 368648 | tf_op jit(solution)/shard_map/ppermute | solution.py:440
  32.0 7.8 %collective-permute-start.9 = (f32[120,256]{1,0:T(8,128)S(1)}, f32[120,256]{1,0:T(8,128)S(1)}, u32[]{:S(2)}, u32[]{:S(2)}) collective-permute-start(f32[120,256]{1,0:T(8,128)S(1)} %get-tuple-element.50), channel_id=1, source_target_pairs={{0,32},{8,40},{16,48},{24,56},{32,0},{40,8},{48,16},{56,24},{1,33}... | collective-permute-start | bytes 368648 | tf_op jit(solution)/shard_map/ppermute | solution.py:440
  33.1 8.6 %collective-permute-start.10 = (f32[120,256]{1,0:T(8,128)S(1)}, f32[120,256]{1,0:T(8,128)S(1)}, u32[]{:S(2)}, u32[]{:S(2)}) collective-permute-start(f32[120,256]{1,0:T(8,128)S(1)} %get-tuple-element.51), channel_id=1, source_target_pairs={{0,56},{8,48},{16,40},{24,32},{32,24},{40,16},{48,8},{56,0},{1,57}... | collective-permute-start | bytes 368648 | tf_op jit(solution)/shard_map/ppermute | solution.py:440
  35.2 6.7 %collective-permute-start.11 = (f32[120,256]{1,0:T(8,128)S(1)}, f32[120,256]{1,0:T(8,128)S(1)}, u32[]{:S(2)}, u32[]{:S(2)}) collective-permute-start(f32[120,256]{1,0:T(8,128)S(1)} %get-tuple-element.52), channel_id=1, source_target_pairs={{0,24},{8,16},{16,8},{24,0},{32,56},{40,48},{48,40},{56,32},{1,25}... | collective-permute-start | bytes 368648 | tf_op jit(solution)/shard_map/ppermute | solution.py:440
  35.9 6.2 %collective-permute-start.12 = (f32[120,256]{1,0:T(8,128)S(1)}, f32[120,256]{1,0:T(8,128)S(1)}, u32[]{:S(2)}, u32[]{:S(2)}) collective-permute-start(f32[120,256]{1,0:T(8,128)S(1)} %get-tuple-element.53), channel_id=1, source_target_pairs={{0,40},{8,32},{16,56},{24,48},{32,8},{40,0},{48,24},{56,16},{1,41}... | collective-permute-start | bytes 368648 | tf_op jit(solution)/shard_map/ppermute | solution.py:440
  36.7 5.4 %collective-permute-start.13 = (f32[120,256]{1,0:T(8,128)S(1)}, f32[120,256]{1,0:T(8,128)S(1)}, u32[]{:S(2)}, u32[]{:S(2)}) collective-permute-start(f32[120,256]{1,0:T(8,128)S(1)} %get-tuple-element.54), channel_id=1, source_target_pairs={{0,8},{8,0},{16,24},{24,16},{32,40},{40,32},{48,56},{56,48},{1,9},... | collective-permute-start | bytes 368648 | tf_op jit(solution)/shard_map/ppermute | solution.py:440
  44.7 8.3 %collective-permute-start.15 = (f32[4,120,256]{2,1,0:T(8,128)S(1)}, f32[4,120,256]{2,1,0:T(8,128)S(1)}, u32[]{:S(2)}, u32[]{:S(2)}) collective-permute-start(f32[4,120,256]{2,1,0:T(8,128)S(1)} %down_theirs.1), channel_id=1, source_target_pairs={{0,1},{1,0},{2,3},{3,2},{4,5},{5,4},{6,7},{7,6},{8,9},{9,8},{10,11... | collective-permute-start | bytes 1474568 | tf_op jit(solution)/shard_map/ppermute | solution.py:457
  53.1 6.6 %collective-permute-start.18 = (f32[120,256]{1,0:T(8,128)S(1)}, f32[120,256]{1,0:T(8,128)S(1)}, u32[]{:S(2)}, u32[]{:S(2)}) collective-permute-start(f32[120,256]{1,0:T(8,128)S(1)} %get-tuple-element.61), channel_id=1, source_target_pairs={{0,4},{2,6},{4,0},{6,2},{1,5},{3,7},{5,1},{7,3},{8,12},{10,14},{12... | collective-permute-start | bytes 368648 | tf_op jit(solution)/shard_map/ppermute | solution.py:443
  56.3 6.3 %collective-permute-start.17 = (f32[120,256]{1,0:T(8,128)S(1)}, f32[120,256]{1,0:T(8,128)S(1)}, u32[]{:S(2)}, u32[]{:S(2)}) collective-permute-start(f32[120,256]{1,0:T(8,128)S(1)} %get-tuple-element.62), channel_id=1, source_target_pairs={{0,2},{2,0},{4,6},{6,4},{1,3},{3,1},{5,7},{7,5},{8,10},{10,8},{12,... | collective-permute-start | bytes 368648 | tf_op jit(solution)/shard_map/ppermute | solution.py:443
  56.7 6.0 %collective-permute-start.16 = (f32[120,256]{1,0:T(8,128)S(1)}, f32[120,256]{1,0:T(8,128)S(1)}, u32[]{:S(2)}, u32[]{:S(2)}) collective-permute-start(f32[120,256]{1,0:T(8,128)S(1)} %get-tuple-element.63), channel_id=1, source_target_pairs={{0,6},{2,4},{4,2},{6,0},{1,7},{3,5},{5,3},{7,1},{8,14},{10,12},{12... | collective-permute-start | bytes 368648 | tf_op jit(solution)/shard_map/ppermute | solution.py:443
  62.8 8.1 %collective-permute-start.21 = (f32[120,256]{1,0:T(8,128)S(1)}, f32[120,256]{1,0:T(8,128)S(1)}, u32[]{:S(2)}, u32[]{:S(2)}) collective-permute-start(f32[120,256]{1,0:T(8,128)S(1)} %sum_up.1.refs_0_), channel_id=1, source_target_pairs={{0,6},{2,4},{4,2},{6,0},{1,7},{3,5},{5,3},{7,1},{8,14},{10,12},{12... | collective-permute-start | bytes 368648 | tf_op jit(solution)/shard_map/ppermute | solution.py:443
  65.7 6.2 %collective-permute-start.20 = (f32[120,256]{1,0:T(8,128)S(1)}, f32[120,256]{1,0:T(8,128)S(1)}, u32[]{:S(2)}, u32[]{:S(2)}) collective-permute-start(f32[120,256]{1,0:T(8,128)S(1)} %sum_up.1.refs_0_), channel_id=1, source_target_pairs={{0,4},{2,6},{4,0},{6,2},{1,5},{3,7},{5,1},{7,3},{8,12},{10,14},{12... | collective-permute-start | bytes 368648 | tf_op jit(solution)/shard_map/ppermute | solution.py:443
  66.0 8.2 %collective-permute-start.19 = (f32[120,256]{1,0:T(8,128)S(1)}, f32[120,256]{1,0:T(8,128)S(1)}, u32[]{:S(2)}, u32[]{:S(2)}) collective-permute-start(f32[120,256]{1,0:T(8,128)S(1)} %sum_up.1.refs_0_), channel_id=1, source_target_pairs={{0,2},{2,0},{4,6},{6,4},{1,3},{3,1},{5,7},{7,5},{8,10},{10,8},{12,... | collective-permute-start | bytes 368648 | tf_op jit(solution)/shard_map/ppermute | solution.py:443
  66.4 7.8 %collective-permute-start.22 = (f32[120,256]{1,0:T(8,128)S(1)}, f32[120,256]{1,0:T(8,128)S(1)}, u32[]{:S(2)}, u32[]{:S(2)}) collective-permute-start(f32[120,256]{1,0:T(8,128)S(1)} %sum_up.1.refs_0_), channel_id=1, source_target_pairs={{0,1},{1,0},{2,3},{3,2},{4,5},{5,4},{6,7},{7,6},{8,9},{9,8},{10,11... | collective-permute-start | bytes 368648 | tf_op jit(solution)/shard_map/ppermute | solution.py:465
  70.9 3.3 %collective-permute-start.25 = (f32[120,256]{1,0:T(8,128)S(1)}, f32[120,256]{1,0:T(8,128)S(1)}, u32[]{:S(2)}, u32[]{:S(2)}) collective-permute-start(f32[120,256]{1,0:T(8,128)S(1)} %collective-permute-done.21.refs_3_), channel_id=1, source_target_pairs={{0,1},{1,0},{2,3},{3,2},{4,5},{5,4},{6,7},{7,6},{8,9},{9,8},{10,11... | collective-permute-start | bytes 368648 | tf_op jit(solution)/shard_map/ppermute | solution.py:465
  71.9 3.3 %collective-permute-start.24 = (f32[120,256]{1,0:T(8,128)S(1)}, f32[120,256]{1,0:T(8,128)S(1)}, u32[]{:S(2)}, u32[]{:S(2)}) collective-permute-start(f32[120,256]{1,0:T(8,128)S(1)} %collective-permute-done.20.refs_2_), channel_id=1, source_target_pairs={{0,1},{1,0},{2,3},{3,2},{4,5},{5,4},{6,7},{7,6},{8,9},{9,8},{10,11... | collective-permute-start | bytes 368648 | tf_op jit(solution)/shard_map/ppermute | solution.py:465
  74.2 1.3 %collective-permute-start.23 = (f32[120,256]{1,0:T(8,128)S(1)}, f32[120,256]{1,0:T(8,128)S(1)}, u32[]{:S(2)}, u32[]{:S(2)}) collective-permute-start(f32[120,256]{1,0:T(8,128)S(1)} %collective-permute-done.19.refs_1_), channel_id=1, source_target_pairs={{0,1},{1,0},{2,3},{3,2},{4,5},{5,4},{6,7},{7,6},{8,9},{9,8},{10,11... | collective-permute-start | bytes 368648 | tf_op jit(solution)/shard_map/ppermute | solution.py:465

commit v6 on v5

--- a/solution.py
+++ b/solution.py
@@ -19,7 +19,7 @@
 
 OFFSETS = (2, 6, 4, 7, 3, 5, 1, 0)
 UP_GROUPS = ((0, 1, 2), (3, 4, 5, 6, 7))
-DOWN_GROUPS = ((7, 0), (1, 2, 3, 4, 5, 6))
+DOWN_GROUPS = ((7,), (0, 1, 2, 3, 4, 5, 6))
 NODES = 2 * len(UP_GROUPS)
 ROWS = ((0, 32), (32, 64), (64, 96), (96, 120))
 

time: 77.3 us -> 78.8 us (1.019)
  waiting for transfers between devices: 16.7 us -> 19.2 us
  starting transfers between devices: 41.7 us -> 40.3 us
    ppermute x14, waiting for transfers between devices: 6.46 us -> 9.26 us  [exchange(): lax.ppermute(x, ('zl', 'x'), [(s, s ^ OFFSETS[i]) for s in range(ND)])]
    ppermute x14, starting transfers between devices: 19.9 us -> 18.8 us  [exchange(): lax.ppermute(x, ('zl', 'x'), [(s, s ^ OFFSETS[i]) for s in range(ND)])]
  transfers between devices with their start and end apart: 26 -> 26, of which waited for: 11 -> 12; matrix products, arithmetic and copies ran while one was open for 0% -> 0% of each run, Pallas kernels for 10% -> 10%
where the time goes in v6:
time: 78.8 us; the launch traced here: 78.7 us
  starting transfers between devices  40.3 us (51%)
  waiting for transfers between devices  19.2 us (24%)
  Pallas kernels  18.8 us (24%)
    ppermute x14, starting transfers between devices, exchange(): lax.ppermute(x, ('zl', 'x'), [(s, s ^ OFFSETS[i]) for s in range(ND)])  18.8 us
    ppermute x14, waiting for transfers between devices, exchange(): lax.ppermute(x, ('zl', 'x'), [(s, s ^ OFFSETS[i]) for s in range(ND)])  9.26 us
    ppermute x6, waiting for transfers between devices, turned(): return lax.ppermute(x, 'y', [(s, s ^ i) for s in range(4)])  8.15 us
    ppermute x6, starting transfers between devices, turned(): return lax.ppermute(x, 'y', [(s, s ^ i) for s in range(4)])  7.55 us
    pallas_call x3, Pallas kernels, down(): pl.pallas_call(kernel, out_shape=single(sections, M, 2 * L), in_specs=[VM...  6.98 us
    ppermute x1, starting transfers between devices, shards(): received = lax.ppermute(theirs, 'c', swap)  5.48 us
    ppermute x4, starting transfers between devices, shards(): parts += [lax.ppermute(x, 'c', swap) for x in parts]  5.07 us
    pallas_call x1, Pallas kernels, up(): pl.pallas_call(functools.partial(up_kernel, group), out_shape=outs, in_sp...  3.67 us
  transfers between devices with their start and end apart: 26, of which 12 were waited for; matrix products, arithmetic and copies ran while one was open for 0% of the time, Pallas kernels for 10%

profile of v6, /device:TPU:1, one launch (start us, length us, event | category | flops | bytes accessed | tf_op | source)
XLA Modules:
  0.0 78.7 jit_solution(8455696174361834141)
XLA Ops:
  0.0 3.7 %up.1 = (f32[2,1024,128]{2,1,0:T(8,128)S(1)}, bf16[8,2,128,256]{3,2,1,0:T(8,128)(2,1)S(1)}, f32[2,64,128]{2,1,0:T(8,128)S(1)}, f32[2,128,64]{2,1,0:T(8,128)S(1)}...) custom-call(f32[8]{0:T(128)} %freq_hbm.1, ...), custom_call_target="tpu_custom_call" | custom-call | tf_op jit(solution)/shard_map/up/pallas_call | solution.py:192
  3.7 3.7 %collective-permute-start = (f32[120,256]{1,0:T(8,128)S(1)}, f32[120,256]{1,0:T(8,128)S(1)}, u32[]{:S(2)}, u32[]{:S(2)}) collective-permute-start(f32[120,256]{1,0:T(8,128)S(1)} %get-tuple-element.33), channel_id=1, source_target_pairs={{0,16},{8,24},{16,0},{24,8},{32,48},{40,56},{48,32},{56,40},{1,17}... | collective-permute-start | bytes 368648 | tf_op jit(solution)/shard_map/ppermute | solution.py:440
  7.3 1.6 %collective-permute-start.1 = (f32[120,256]{1,0:T(8,128)S(1)}, f32[120,256]{1,0:T(8,128)S(1)}, u32[]{:S(2)}, u32[]{:S(2)}) collective-permute-start(f32[120,256]{1,0:T(8,128)S(1)} %get-tuple-element.34), channel_id=1, source_target_pairs={{0,48},{8,56},{16,32},{24,40},{32,16},{40,24},{48,0},{56,8},{1,49}... | collective-permute-start | bytes 368648 | tf_op jit(solution)/shard_map/ppermute | solution.py:440
  8.9 0.1 collective-permute-start.2
  9.0 2.3 %up_second.1 = (bf16[4,5,2,128,256]{4,3,2,1,0:T(8,128)(2,1)S(1)}, bf16[2,5,2,128,256]{4,3,2,1,0:T(8,128)(2,1)S(1)}, f32[120,256]{1,0:T(8,128)S(1)}, f32[120,256]...) custom-call(f32[2,1024,128]{2,1,0:T(8,128)S(1)} %get-tuple-element.36.c_ref, ...), custom_call_target="tpu_custom_call" | custom-call | tf_op jit(solution)/shard_map/up_second/pallas_call | solution.py:212
  11.3 3.7 %collective-permute-start.3 = (f32[120,256]{1,0:T(8,128)S(1)}, f32[120,256]{1,0:T(8,128)S(1)}, u32[]{:S(2)}, u32[]{:S(2)}) collective-permute-start(f32[120,256]{1,0:T(8,128)S(1)} %get-tuple-element.40), channel_id=1, source_target_pairs={{0,56},{8,48},{16,40},{24,32},{32,24},{40,16},{48,8},{56,0},{1,57}... | collective-permute-start | bytes 368648 | tf_op jit(solution)/shard_map/ppermute | solution.py:440
  15.0 0.2 collective-permute-start.4
  15.2 0.0 collective-permute-done.refs_0_
  15.2 0.0 collective-permute-start.5
  15.2 0.0 collective-permute-done.1.refs_1_
  15.2 1.4 %collective-permute-start.6 = (f32[120,256]{1,0:T(8,128)S(1)}, f32[120,256]{1,0:T(8,128)S(1)}, u32[]{:S(2)}, u32[]{:S(2)}) collective-permute-start(f32[120,256]{1,0:T(8,128)S(1)} %get-tuple-element.43), channel_id=1, source_target_pairs={{0,8},{8,0},{16,24},{24,16},{32,40},{40,32},{48,56},{56,48},{1,9},... | collective-permute-start | bytes 368648 | tf_op jit(solution)/shard_map/ppermute | solution.py:440
  16.5 0.0 collective-permute-done.2.refs_2_
  16.5 0.8 %collective-permute-done.3.refs_3_ = f32[120,256]{1,0:T(8,128)S(1)} collective-permute-done((f32[120,256]{1,0:T(8,128)S(1)}, f32[120,256]{1,0:T(8,128)S(1)}, u32[]{:S(2)}, u32[]{:S(2)}) %collective-permute-start.3) | collective-permute-done | bytes 122912 | tf_op jit(solution)/shard_map/ppermute | solution.py:440
  17.3 3.4 %collective-permute-done.4.refs_4_ = f32[120,256]{1,0:T(8,128)S(1)} collective-permute-done((f32[120,256]{1,0:T(8,128)S(1)}, f32[120,256]{1,0:T(8,128)S(1)}, u32[]{:S(2)}, u32[]{:S(2)}) %collective-permute-start.4) | collective-permute-done | bytes 122912 | tf_op jit(solution)/shard_map/ppermute | solution.py:440
  20.7 0.0 collective-permute-done.5.refs_5_
  20.7 0.0 collective-permute-done.6.refs_6_
  20.7 0.9 %half.1 = (f32[120,256]{1,0:T(8,128)S(1)}, bf16[8,2,128,256]{3,2,1,0:T(8,128)(2,1)S(1)}, bf16[4,2,128,256]{3,2,1,0:T(8,128)(2,1)S(1)}, bf16[2,2,128,256]{3,2,1,0:T(8,128)(2,1)S(1)}) custom-call(f32[120,256]{1,0:T(8,128)S(1)} %collective-permute-done.refs_0_, f32[120,256]{1,0:T(8,128)S(1)} %collective-permute-done.1.refs_1_, ...), custom_call_target="tpu_custom_call" | custom-call | tf_op jit(solution)/shard_map/half/pallas_call | solution.py:237
  21.6 3.4 %collective-permute-start.7 = (f32[120,256]{1,0:T(8,128)S(1)}, f32[120,256]{1,0:T(8,128)S(1)}, u32[]{:S(2)}, u32[]{:S(2)}) collective-permute-start(f32[120,256]{1,0:T(8,128)S(1)} %get-tuple-element.48.h_ref), channel_id=1, source_target_pairs={{0,96},{32,64},{64,32},{96,0},{1,97},{33,65},{65,33},{97,1},{2,98}... | collective-permute-start | bytes 368648 | tf_op jit(solution)/shard_map/ppermute | solution.py:449
  25.0 1.8 %pick.1.m_ref = f32[128,256]{1,0:T(8,128)S(1)} custom-call(f32[8,28800]{1,0:T(8,128)} %flat_ref.1), custom_call_target="tpu_custom_call" | custom-call | tf_op jit(solution)/shard_map/pick/pallas_call | solution.py:253
  26.8 0.5 collective-permute-done.7.other_ref
  27.3 1.6 %top.1 = (f32[120,256]{1,0:T(8,128)S(1)}, f32[120,256]{1,0:T(8,128)S(1)}, f32[120,256]{1,0:T(8,128)S(1)}, f32[120,256]{1,0:T(8,128)S(1)}, f32[120,256]{1,0:T(8,1...) custom-call(bf16[8,2,128,256]{3,2,1,0:T(8,128)(2,1)S(1)} %get-tuple-element.45.r_ref, ...), custom_call_target="tpu_custom_call" | custom-call | tf_op jit(solution)/shard_map/top/pallas_call | solution.py:291
  28.9 3.2 %collective-permute-start.8 = (f32[120,256]{1,0:T(8,128)S(1)}, f32[120,256]{1,0:T(8,128)S(1)}, u32[]{:S(2)}, u32[]{:S(2)}) collective-permute-start(f32[120,256]{1,0:T(8,128)S(1)} %get-tuple-element.49), channel_id=1, source_target_pairs={{0,16},{8,24},{16,0},{24,8},{32,48},{40,56},{48,32},{56,40},{1,17}... | collective-permute-start | bytes 368648 | tf_op jit(solution)/shard_map/ppermute | solution.py:440
  32.1 0.0 collective-permute-start.9
  32.1 1.3 %collective-permute-start.10 = (f32[120,256]{1,0:T(8,128)S(1)}, f32[120,256]{1,0:T(8,128)S(1)}, u32[]{:S(2)}, u32[]{:S(2)}) collective-permute-start(f32[120,256]{1,0:T(8,128)S(1)} %get-tuple-element.51), channel_id=1, source_target_pairs={{0,32},{8,40},{16,48},{24,56},{32,0},{40,8},{48,16},{56,24},{1,33}... | collective-permute-start | bytes 368648 | tf_op jit(solution)/shard_map/ppermute | solution.py:440
  33.4 2.0 %collective-permute-start.11 = (f32[120,256]{1,0:T(8,128)S(1)}, f32[120,256]{1,0:T(8,128)S(1)}, u32[]{:S(2)}, u32[]{:S(2)}) collective-permute-start(f32[120,256]{1,0:T(8,128)S(1)} %get-tuple-element.52), channel_id=1, source_target_pairs={{0,56},{8,48},{16,40},{24,32},{32,24},{40,16},{48,8},{56,0},{1,57}... | collective-permute-start | bytes 368648 | tf_op jit(solution)/shard_map/ppermute | solution.py:440
  35.4 0.6 collective-permute-start.12
  36.0 0.0 collective-permute-done.8.refs_0_
  36.0 0.9 %collective-permute-start.13 = (f32[120,256]{1,0:T(8,128)S(1)}, f32[120,256]{1,0:T(8,128)S(1)}, u32[]{:S(2)}, u32[]{:S(2)}) collective-permute-start(f32[120,256]{1,0:T(8,128)S(1)} %get-tuple-element.54), channel_id=1, source_target_pairs={{0,40},{8,32},{16,56},{24,48},{32,8},{40,0},{48,24},{56,16},{1,41}... | collective-permute-start | bytes 368648 | tf_op jit(solution)/shard_map/ppermute | solution.py:440
  36.8 2.4 %collective-permute-done.9.refs_1_ = f32[120,256]{1,0:T(8,128)S(1)} collective-permute-done((f32[120,256]{1,0:T(8,128)S(1)}, f32[120,256]{1,0:T(8,128)S(1)}, u32[]{:S(2)}, u32[]{:S(2)}) %collective-permute-start.9) | collective-permute-done | bytes 122912 | tf_op jit(solution)/shard_map/ppermute | solution.py:440
  39.3 0.3 collective-permute-start.14
  39.6 1.1 %down_1.1.refs_14_ = f32[8,120,256]{2,1,0:T(8,128)S(1)} custom-call(f32[120,256]{1,0:T(8,128)S(1)} %get-tuple-element.60.refs_0_, bf16[8,2,128,256]{3,2,1,0:T(8,128)(2,1)S(1)} %get-tuple-element.37.ch_ref.refs_1_.refs_7_, f32[2,64,128]{2,1,0:T(8,128)S(1)} %get-tuple-element.38.tab_ref.refs_2_.refs_8_, ...), custom_call_target="tpu_custom_call" | custom-call | tf_op jit(solution)/shard_map/down_1/pallas_call | solution.py:372
  40.6 0.0 collective-permute-done.10.refs_2_
  40.6 0.4 collective-permute-done.11.refs_3_
  41.1 2.1 %collective-permute-done.12.refs_4_ = f32[120,256]{1,0:T(8,128)S(1)} collective-permute-done((f32[120,256]{1,0:T(8,128)S(1)}, f32[120,256]{1,0:T(8,128)S(1)}, u32[]{:S(2)}, u32[]{:S(2)}) %collective-permute-start.12) | collective-permute-done | bytes 122912 | tf_op jit(solution)/shard_map/ppermute | solution.py:440
  43.2 0.0 collective-permute-done.13.refs_5_
  43.2 0.1 collective-permute-done.14.refs_6_
  43.3 3.0 %down_theirs.1 = f32[4,120,256]{2,1,0:T(8,128)S(1)} custom-call(f32[120,256]{1,0:T(8,128)S(1)} %collective-permute-done.8.refs_0_, f32[120,256]{1,0:T(8,128)S(1)} %collective-permute-done.9.refs_1_, f32[120,256]{1,0:T(8,128)S(1)} %collective-permute-done.10.refs_2_, f32[120,256]{1,0:T(8,128)S(1)} %collective-permute-done.11.refs_3_, ...), custom_call_target="tpu_custom_call" | custom-call | tf_op jit(solution)/shard_map/down_theirs/pallas_call | solution.py:372
  46.3 5.5 %collective-permute-start.15 = (f32[4,120,256]{2,1,0:T(8,128)S(1)}, f32[4,120,256]{2,1,0:T(8,128)S(1)}, u32[]{:S(2)}, u32[]{:S(2)}) collective-permute-start(f32[4,120,256]{2,1,0:T(8,128)S(1)} %down_theirs.1), channel_id=1, source_target_pairs={{0,1},{1,0},{2,3},{3,2},{4,5},{5,4},{6,7},{7,6},{8,9},{9,8},{10,11... | collective-permute-start | bytes 1474568 | tf_op jit(solution)/shard_map/ppermute | solution.py:457
  51.8 2.9 %down_mine.1 = f32[4,120,256]{2,1,0:T(8,128)S(1)} custom-call(f32[120,256]{1,0:T(8,128)S(1)} %collective-permute-done.8.refs_0_, f32[120,256]{1,0:T(8,128)S(1)} %collective-permute-done.9.refs_1_, f32[120,256]{1,0:T(8,128)S(1)} %collective-permute-done.10.refs_2_, f32[120,256]{1,0:T(8,128)S(1)} %collective-permute-done.11.refs_3_, ...), custom_call_target="tpu_custom_call" | custom-call | tf_op jit(solution)/shard_map/down_mine/pallas_call | solution.py:372
  54.7 0.0 collective-permute-done.15
  54.7 0.1 add.3
  54.8 3.0 %collective-permute-start.18 = (f32[120,256]{1,0:T(8,128)S(1)}, f32[120,256]{1,0:T(8,128)S(1)}, u32[]{:S(2)}, u32[]{:S(2)}) collective-permute-start(f32[120,256]{1,0:T(8,128)S(1)} %get-tuple-element.61), channel_id=1, source_target_pairs={{0,4},{2,6},{4,0},{6,2},{1,5},{3,7},{5,1},{7,3},{8,12},{10,14},{12... | collective-permute-start | bytes 368648 | tf_op jit(solution)/shard_map/ppermute | solution.py:443
  57.8 0.4 collective-permute-start.17
  58.2 0.4 collective-permute-start.16
  58.6 2.4 %collective-permute-done.18.c_ref = f32[120,256]{1,0:T(8,128)S(1)} collective-permute-done((f32[120,256]{1,0:T(8,128)S(1)}, f32[120,256]{1,0:T(8,128)S(1)}, u32[]{:S(2)}, u32[]{:S(2)}) %collective-permute-start.18) | collective-permute-done | bytes 122912 | tf_op jit(solution)/shard_map/ppermute | solution.py:443
  61.0 3.0 %collective-permute-done.17.b_ref = f32[120,256]{1,0:T(8,128)S(1)} collective-permute-done((f32[120,256]{1,0:T(8,128)S(1)}, f32[120,256]{1,0:T(8,128)S(1)}, u32[]{:S(2)}, u32[]{:S(2)}) %collective-permute-start.17) | collective-permute-done | bytes 122912 | tf_op jit(solution)/shard_map/ppermute | solution.py:443
  64.0 0.0 collective-permute-done.16.a_ref
  64.0 0.1 sum_up.1.refs_0_
  64.1 3.1 %collective-permute-start.21 = (f32[120,256]{1,0:T(8,128)S(1)}, f32[120,256]{1,0:T(8,128)S(1)}, u32[]{:S(2)}, u32[]{:S(2)}) collective-permute-start(f32[120,256]{1,0:T(8,128)S(1)} %sum_up.1.refs_0_), channel_id=1, source_target_pairs={{0,6},{2,4},{4,2},{6,0},{1,7},{3,5},{5,3},{7,1},{8,14},{10,12},{12... | collective-permute-start | bytes 368648 | tf_op jit(solution)/shard_map/ppermute | solution.py:443
  67.2 0.3 collective-permute-start.20
  67.5 0.4 collective-permute-start.19
  67.9 1.7 %collective-permute-start.22 = (f32[120,256]{1,0:T(8,128)S(1)}, f32[120,256]{1,0:T(8,128)S(1)}, u32[]{:S(2)}, u32[]{:S(2)}) collective-permute-start(f32[120,256]{1,0:T(8,128)S(1)} %sum_up.1.refs_0_), channel_id=1, source_target_pairs={{0,1},{1,0},{2,3},{3,2},{4,5},{5,4},{6,7},{7,6},{8,9},{9,8},{10,11... | collective-permute-start | bytes 368648 | tf_op jit(solution)/shard_map/ppermute | solution.py:465
  69.6 2.8 %collective-permute-done.21.refs_3_ = f32[120,256]{1,0:T(8,128)S(1)} collective-permute-done((f32[120,256]{1,0:T(8,128)S(1)}, f32[120,256]{1,0:T(8,128)S(1)}, u32[]{:S(2)}, u32[]{:S(2)}) %collective-permute-start.21) | collective-permute-done | bytes 122912 | tf_op jit(solution)/shard_map/ppermute | solution.py:443
  72.3 1.0 %collective-permute-start.25 = (f32[120,256]{1,0:T(8,128)S(1)}, f32[120,256]{1,0:T(8,128)S(1)}, u32[]{:S(2)}, u32[]{:S(2)}) collective-permute-start(f32[120,256]{1,0:T(8,128)S(1)} %collective-permute-done.21.refs_3_), channel_id=1, source_target_pairs={{0,1},{1,0},{2,3},{3,2},{4,5},{5,4},{6,7},{7,6},{8,9},{9,8},{10,11... | collective-permute-start | bytes 368648 | tf_op jit(solution)/shard_map/ppermute | solution.py:465
  73.4 0.0 collective-permute-done.20.refs_2_
  73.4 2.3 %collective-permute-start.24 = (f32[120,256]{1,0:T(8,128)S(1)}, f32[120,256]{1,0:T(8,128)S(1)}, u32[]{:S(2)}, u32[]{:S(2)}) collective-permute-start(f32[120,256]{1,0:T(8,128)S(1)} %collective-permute-done.20.refs_2_), channel_id=1, source_target_pairs={{0,1},{1,0},{2,3},{3,2},{4,5},{5,4},{6,7},{7,6},{8,9},{9,8},{10,11... | collective-permute-start | bytes 368648 | tf_op jit(solution)/shard_map/ppermute | solution.py:465
  75.7 0.0 collective-permute-done.19.refs_1_
  75.7 0.0 collective-permute-start.23
  75.7 0.0 collective-permute-done.22.refs_4_
  75.7 0.0 collective-permute-done.25.refs_7_
  75.7 1.0 %collective-permute-done.24.refs_6_ = f32[120,256]{1,0:T(8,128)S(1)} collective-permute-done((f32[120,256]{1,0:T(8,128)S(1)}, f32[120,256]{1,0:T(8,128)S(1)}, u32[]{:S(2)}, u32[]{:S(2)}) %collective-permute-start.24) | collective-permute-done | bytes 122912 | tf_op jit(solution)/shard_map/ppermute | solution.py:465
  76.7 0.4 collective-permute-done.23.refs_5_
  77.0 1.5 %store.1 = f32[8,28800]{1,0:T(8,128)} custom-call(f32[120,256]{1,0:T(8,128)S(1)} %sum_up.1.refs_0_, f32[120,256]{1,0:T(8,128)S(1)} %collective-permute-done.19.refs_1_, f32[120,256]{1,0:T(8,128)S(1)} %collective-permute-done.20.refs_2_, f32[120,256]{1,0:T(8,128)S(1)} %collective-permute-done.21.refs_3_, f32[120,256]{1,0:T(8,128)S(1)} %collective-permute-done.22.refs_4_, ...), custom_call_target="tpu_custom_call" | custom-call | tf_op jit(solution)/shard_map/store/pallas_call | solution.py:425
  (1 shorter events, 0.0 us)
Async XLA Ops:
  3.7 11.5 %collective-permute-start = (f32[120,256]{1,0:T(8,128)S(1)}, f32[120,256]{1,0:T(8,128)S(1)}, u32[]{:S(2)}, u32[]{:S(2)}) collective-permute-start(f32[120,256]{1,0:T(8,128)S(1)} %get-tuple-element.33), channel_id=1, source_target_pairs={{0,16},{8,24},{16,0},{24,8},{32,48},{40,56},{48,32},{56,40},{1,17}... | collective-permute-start | bytes 368648 | tf_op jit(solution)/shard_map/ppermute | solution.py:440
  7.3 7.8 %collective-permute-start.1 = (f32[120,256]{1,0:T(8,128)S(1)}, f32[120,256]{1,0:T(8,128)S(1)}, u32[]{:S(2)}, u32[]{:S(2)}) collective-permute-start(f32[120,256]{1,0:T(8,128)S(1)} %get-tuple-element.34), channel_id=1, source_target_pairs={{0,48},{8,56},{16,32},{24,40},{32,16},{40,24},{48,0},{56,8},{1,49}... | collective-permute-start | bytes 368648 | tf_op jit(solution)/shard_map/ppermute | solution.py:440
  8.9 7.6 %collective-permute-start.2 = (f32[120,256]{1,0:T(8,128)S(1)}, f32[120,256]{1,0:T(8,128)S(1)}, u32[]{:S(2)}, u32[]{:S(2)}) collective-permute-start(f32[120,256]{1,0:T(8,128)S(1)} %get-tuple-element.35), channel_id=1, source_target_pairs={{0,32},{8,40},{16,48},{24,56},{32,0},{40,8},{48,16},{56,24},{1,33}... | collective-permute-start | bytes 368648 | tf_op jit(solution)/shard_map/ppermute | solution.py:440
  11.3 6.1 %collective-permute-start.3 = (f32[120,256]{1,0:T(8,128)S(1)}, f32[120,256]{1,0:T(8,128)S(1)}, u32[]{:S(2)}, u32[]{:S(2)}) collective-permute-start(f32[120,256]{1,0:T(8,128)S(1)} %get-tuple-element.40), channel_id=1, source_target_pairs={{0,56},{8,48},{16,40},{24,32},{32,24},{40,16},{48,8},{56,0},{1,57}... | collective-permute-start | bytes 368648 | tf_op jit(solution)/shard_map/ppermute | solution.py:440
  15.0 5.8 %collective-permute-start.4 = (f32[120,256]{1,0:T(8,128)S(1)}, f32[120,256]{1,0:T(8,128)S(1)}, u32[]{:S(2)}, u32[]{:S(2)}) collective-permute-start(f32[120,256]{1,0:T(8,128)S(1)} %get-tuple-element.41), channel_id=1, source_target_pairs={{0,24},{8,16},{16,8},{24,0},{32,56},{40,48},{48,40},{56,32},{1,25}... | collective-permute-start | bytes 368648 | tf_op jit(solution)/shard_map/ppermute | solution.py:440
  15.2 5.6 %collective-permute-start.5 = (f32[120,256]{1,0:T(8,128)S(1)}, f32[120,256]{1,0:T(8,128)S(1)}, u32[]{:S(2)}, u32[]{:S(2)}) collective-permute-start(f32[120,256]{1,0:T(8,128)S(1)} %get-tuple-element.42), channel_id=1, source_target_pairs={{0,40},{8,32},{16,56},{24,48},{32,8},{40,0},{48,24},{56,16},{1,41}... | collective-permute-start | bytes 368648 | tf_op jit(solution)/shard_map/ppermute | solution.py:440
  15.2 5.6 %collective-permute-start.6 = (f32[120,256]{1,0:T(8,128)S(1)}, f32[120,256]{1,0:T(8,128)S(1)}, u32[]{:S(2)}, u32[]{:S(2)}) collective-permute-start(f32[120,256]{1,0:T(8,128)S(1)} %get-tuple-element.43), channel_id=1, source_target_pairs={{0,8},{8,0},{16,24},{24,16},{32,40},{40,32},{48,56},{56,48},{1,9},... | collective-permute-start | bytes 368648 | tf_op jit(solution)/shard_map/ppermute | solution.py:440
  21.6 5.7 %collective-permute-start.7 = (f32[120,256]{1,0:T(8,128)S(1)}, f32[120,256]{1,0:T(8,128)S(1)}, u32[]{:S(2)}, u32[]{:S(2)}) collective-permute-start(f32[120,256]{1,0:T(8,128)S(1)} %get-tuple-element.48.h_ref), channel_id=1, source_target_pairs={{0,96},{32,64},{64,32},{96,0},{1,97},{33,65},{65,33},{97,1},{2,98}... | collective-permute-start | bytes 368648 | tf_op jit(solution)/shard_map/ppermute | solution.py:449
  28.9 7.1 %collective-permute-start.8 = (f32[120,256]{1,0:T(8,128)S(1)}, f32[120,256]{1,0:T(8,128)S(1)}, u32[]{:S(2)}, u32[]{:S(2)}) collective-permute-start(f32[120,256]{1,0:T(8,128)S(1)} %get-tuple-element.49), channel_id=1, source_target_pairs={{0,16},{8,24},{16,0},{24,8},{32,48},{40,56},{48,32},{56,40},{1,17}... | collective-permute-start | bytes 368648 | tf_op jit(solution)/shard_map/ppermute | solution.py:440
  32.1 7.2 %collective-permute-start.9 = (f32[120,256]{1,0:T(8,128)S(1)}, f32[120,256]{1,0:T(8,128)S(1)}, u32[]{:S(2)}, u32[]{:S(2)}) collective-permute-start(f32[120,256]{1,0:T(8,128)S(1)} %get-tuple-element.50), channel_id=1, source_target_pairs={{0,48},{8,56},{16,32},{24,40},{32,16},{40,24},{48,0},{56,8},{1,49}... | collective-permute-start | bytes 368648 | tf_op jit(solution)/shard_map/ppermute | solution.py:440
  32.1 8.5 %collective-permute-start.10 = (f32[120,256]{1,0:T(8,128)S(1)}, f32[120,256]{1,0:T(8,128)S(1)}, u32[]{:S(2)}, u32[]{:S(2)}) collective-permute-start(f32[120,256]{1,0:T(8,128)S(1)} %get-tuple-element.51), channel_id=1, source_target_pairs={{0,32},{8,40},{16,48},{24,56},{32,0},{40,8},{48,16},{56,24},{1,33}... | collective-permute-start | bytes 368648 | tf_op jit(solution)/shard_map/ppermute | solution.py:440
  33.4 7.7 %collective-permute-start.11 = (f32[120,256]{1,0:T(8,128)S(1)}, f32[120,256]{1,0:T(8,128)S(1)}, u32[]{:S(2)}, u32[]{:S(2)}) collective-permute-start(f32[120,256]{1,0:T(8,128)S(1)} %get-tuple-element.52), channel_id=1, source_target_pairs={{0,56},{8,48},{16,40},{24,32},{32,24},{40,16},{48,8},{56,0},{1,57}... | collective-permute-start | bytes 368648 | tf_op jit(solution)/shard_map/ppermute | solution.py:440
  35.4 7.8 %collective-permute-start.12 = (f32[120,256]{1,0:T(8,128)S(1)}, f32[120,256]{1,0:T(8,128)S(1)}, u32[]{:S(2)}, u32[]{:S(2)}) collective-permute-start(f32[120,256]{1,0:T(8,128)S(1)} %get-tuple-element.53), channel_id=1, source_target_pairs={{0,24},{8,16},{16,8},{24,0},{32,56},{40,48},{48,40},{56,32},{1,25}... | collective-permute-start | bytes 368648 | tf_op jit(solution)/shard_map/ppermute | solution.py:440
  36.0 7.2 %collective-permute-start.13 = (f32[120,256]{1,0:T(8,128)S(1)}, f32[120,256]{1,0:T(8,128)S(1)}, u32[]{:S(2)}, u32[]{:S(2)}) collective-permute-start(f32[120,256]{1,0:T(8,128)S(1)} %get-tuple-element.54), channel_id=1, source_target_pairs={{0,40},{8,32},{16,56},{24,48},{32,8},{40,0},{48,24},{56,16},{1,41}... | collective-permute-start | bytes 368648 | tf_op jit(solution)/shard_map/ppermute | solution.py:440
  39.3 4.0 %collective-permute-start.14 = (f32[120,256]{1,0:T(8,128)S(1)}, f32[120,256]{1,0:T(8,128)S(1)}, u32[]{:S(2)}, u32[]{:S(2)}) collective-permute-start(f32[120,256]{1,0:T(8,128)S(1)} %get-tuple-element.55), channel_id=1, source_target_pairs={{0,8},{8,0},{16,24},{24,16},{32,40},{40,32},{48,56},{56,48},{1,9},... | collective-permute-start | bytes 368648 | tf_op jit(solution)/shard_map/ppermute | solution.py:440
  46.3 8.4 %collective-permute-start.15 = (f32[4,120,256]{2,1,0:T(8,128)S(1)}, f32[4,120,256]{2,1,0:T(8,128)S(1)}, u32[]{:S(2)}, u32[]{:S(2)}) collective-permute-start(f32[4,120,256]{2,1,0:T(8,128)S(1)} %down_theirs.1), channel_id=1, source_target_pairs={{0,1},{1,0},{2,3},{3,2},{4,5},{5,4},{6,7},{7,6},{8,9},{9,8},{10,11... | collective-permute-start | bytes 1474568 | tf_op jit(solution)/shard_map/ppermute | solution.py:457
  54.8 6.2 %collective-permute-start.18 = (f32[120,256]{1,0:T(8,128)S(1)}, f32[120,256]{1,0:T(8,128)S(1)}, u32[]{:S(2)}, u32[]{:S(2)}) collective-permute-start(f32[120,256]{1,0:T(8,128)S(1)} %get-tuple-element.61), channel_id=1, source_target_pairs={{0,4},{2,6},{4,0},{6,2},{1,5},{3,7},{5,1},{7,3},{8,12},{10,14},{12... | collective-permute-start | bytes 368648 | tf_op jit(solution)/shard_map/ppermute | solution.py:443
  57.8 6.2 %collective-permute-start.17 = (f32[120,256]{1,0:T(8,128)S(1)}, f32[120,256]{1,0:T(8,128)S(1)}, u32[]{:S(2)}, u32[]{:S(2)}) collective-permute-start(f32[120,256]{1,0:T(8,128)S(1)} %get-tuple-element.62), channel_id=1, source_target_pairs={{0,2},{2,0},{4,6},{6,4},{1,3},{3,1},{5,7},{7,5},{8,10},{10,8},{12,... | collective-permute-start | bytes 368648 | tf_op jit(solution)/shard_map/ppermute | solution.py:443
  58.2 5.8 %collective-permute-start.16 = (f32[120,256]{1,0:T(8,128)S(1)}, f32[120,256]{1,0:T(8,128)S(1)}, u32[]{:S(2)}, u32[]{:S(2)}) collective-permute-start(f32[120,256]{1,0:T(8,128)S(1)} %get-tuple-element.63), channel_id=1, source_target_pairs={{0,6},{2,4},{4,2},{6,0},{1,7},{3,5},{5,3},{7,1},{8,14},{10,12},{12... | collective-permute-start | bytes 368648 | tf_op jit(solution)/shard_map/ppermute | solution.py:443
  64.1 8.2 %collective-permute-start.21 = (f32[120,256]{1,0:T(8,128)S(1)}, f32[120,256]{1,0:T(8,128)S(1)}, u32[]{:S(2)}, u32[]{:S(2)}) collective-permute-start(f32[120,256]{1,0:T(8,128)S(1)} %sum_up.1.refs_0_), channel_id=1, source_target_pairs={{0,6},{2,4},{4,2},{6,0},{1,7},{3,5},{5,3},{7,1},{8,14},{10,12},{12... | collective-permute-start | bytes 368648 | tf_op jit(solution)/shard_map/ppermute | solution.py:443
  67.2 6.2 %collective-permute-start.20 = (f32[120,256]{1,0:T(8,128)S(1)}, f32[120,256]{1,0:T(8,128)S(1)}, u32[]{:S(2)}, u32[]{:S(2)}) collective-permute-start(f32[120,256]{1,0:T(8,128)S(1)} %sum_up.1.refs_0_), channel_id=1, source_target_pairs={{0,4},{2,6},{4,0},{6,2},{1,5},{3,7},{5,1},{7,3},{8,12},{10,14},{12... | collective-permute-start | bytes 368648 | tf_op jit(solution)/shard_map/ppermute | solution.py:443
  67.5 8.2 %collective-permute-start.19 = (f32[120,256]{1,0:T(8,128)S(1)}, f32[120,256]{1,0:T(8,128)S(1)}, u32[]{:S(2)}, u32[]{:S(2)}) collective-permute-start(f32[120,256]{1,0:T(8,128)S(1)} %sum_up.1.refs_0_), channel_id=1, source_target_pairs={{0,2},{2,0},{4,6},{6,4},{1,3},{3,1},{5,7},{7,5},{8,10},{10,8},{12,... | collective-permute-start | bytes 368648 | tf_op jit(solution)/shard_map/ppermute | solution.py:443
  67.9 7.8 %collective-permute-start.22 = (f32[120,256]{1,0:T(8,128)S(1)}, f32[120,256]{1,0:T(8,128)S(1)}, u32[]{:S(2)}, u32[]{:S(2)}) collective-permute-start(f32[120,256]{1,0:T(8,128)S(1)} %sum_up.1.refs_0_), channel_id=1, source_target_pairs={{0,1},{1,0},{2,3},{3,2},{4,5},{5,4},{6,7},{7,6},{8,9},{9,8},{10,11... | collective-permute-start | bytes 368648 | tf_op jit(solution)/shard_map/ppermute | solution.py:465
  72.3 3.4 %collective-permute-start.25 = (f32[120,256]{1,0:T(8,128)S(1)}, f32[120,256]{1,0:T(8,128)S(1)}, u32[]{:S(2)}, u32[]{:S(2)}) collective-permute-start(f32[120,256]{1,0:T(8,128)S(1)} %collective-permute-done.21.refs_3_), channel_id=1, source_target_pairs={{0,1},{1,0},{2,3},{3,2},{4,5},{5,4},{6,7},{7,6},{8,9},{9,8},{10,11... | collective-permute-start | bytes 368648 | tf_op jit(solution)/shard_map/ppermute | solution.py:465
  73.4 3.3 %collective-permute-start.24 = (f32[120,256]{1,0:T(8,128)S(1)}, f32[120,256]{1,0:T(8,128)S(1)}, u32[]{:S(2)}, u32[]{:S(2)}) collective-permute-start(f32[120,256]{1,0:T(8,128)S(1)} %collective-permute-done.20.refs_2_), channel_id=1, source_target_pairs={{0,1},{1,0},{2,3},{3,2},{4,5},{5,4},{6,7},{7,6},{8,9},{9,8},{10,11... | collective-permute-start | bytes 368648 | tf_op jit(solution)/shard_map/ppermute | solution.py:465
  75.7 1.3 %collective-permute-start.23 = (f32[120,256]{1,0:T(8,128)S(1)}, f32[120,256]{1,0:T(8,128)S(1)}, u32[]{:S(2)}, u32[]{:S(2)}) collective-permute-start(f32[120,256]{1,0:T(8,128)S(1)} %collective-permute-done.19.refs_1_), channel_id=1, source_target_pairs={{0,1},{1,0},{2,3},{3,2},{4,5},{5,4},{6,7},{7,6},{8,9},{9,8},{10,11... | collective-permute-start | bytes 368648 | tf_op jit(solution)/shard_map/ppermute | solution.py:465
